TPU v7x, 32 devices: a whole 2x2x4 slice. The times are simulated.
32 devices in a mesh: groups: 2 (over x), expert: 16 (over z, y, core).
Axes of the slice: x: 2, y: 2, z: 4, core: 2. Of those that a mesh axis runs over, the one named last changes fastest.
Arguments:
- hidden_states: bfloat16 [2, 1024, 2560], P(None, ('groups', 'expert')), parts along dimension 1, may hold values from -6 to 6
- route_ids: int32 [2, 1024, 8], P(None, ('groups', 'expert')), parts along dimension 1, may hold values from 0 to 15, all different within a row; in each aligned block of 32 rows (0 to 31, 32 to 63, ..., all dimensions but the last counted through in order) at most 24 rows name the same one
- route_weights: float32 [2, 1024, 8], P(None, ('groups', 'expert')), parts along dimension 1, may hold values from 0.05 to 1
- gate_proj: bfloat16 [16, 2560, 768], P('expert'), may hold values from -0.125 to 0.125
- up_proj: bfloat16 [16, 2560, 768], P('expert'), may hold values from -0.125 to 0.125
- down_proj: bfloat16 [16, 768, 2560], P('expert'), may hold values from -0.21875 to 0.21875
Outputs:
- moe_output: bfloat16 [2, 1024, 2560], P(None, ('groups', 'expert')), parts along dimension 1
There are 2 independent parts, one for each index of `groups`. A program takes and returns all parts, laid end to end along the dimension named above; an argument that names none is the same for every part. Nothing has to cross between parts.
Inputs may be any that keep to these rules, and one draw needn't show every extreme that they name: `route_ids`: each row names 8 different experts. In each micro-batch, the 32 rows of one device name one expert at most 24 times, and some device names some expert exactly 24 times.
All inputs are finite; a program needn't handle non-finite values.
Results may differ from a plain program's by a relative error of at most 0.0057.
Values may be sent and summed in bfloat16 or wider, within the bound.
No kernel may reach another device: no remote copies, remote signals or barrier semaphores. Data moves between devices by JAX's collectives and lax.ppermute only.
A program may use at most 64 MiB of HBM per device.

v0:
```python
import jax
import jax.numpy as jnp
from jax import lax
from jax.sharding import PartitionSpec as P


def expert_rows(received, gate_proj, up_proj, down_proj):
    sources, slot_count, feature_width = received.shape
    stacked = received.reshape(sources * slot_count, feature_width)
    gate_values = jnp.dot(stacked, gate_proj[0], preferred_element_type=jnp.float32)
    up_values = jnp.dot(stacked, up_proj[0], preferred_element_type=jnp.float32)
    hidden = (jax.nn.silu(gate_values) * up_values).astype(jnp.bfloat16)
    result = jnp.dot(hidden, down_proj[0], preferred_element_type=jnp.float32)
    return result.astype(jnp.bfloat16).reshape(sources, slot_count, feature_width)


def slot_index(route_row, experts, capacity):
    row_count, top_count = route_row.shape
    labels = lax.broadcasted_iota(jnp.int32, (row_count, top_count, experts), 2)
    onehot = (route_row[:, :, None] == labels).astype(jnp.int32)
    per_row = jnp.sum(onehot, axis=1)
    before = jnp.cumsum(per_row, axis=0) - per_row
    position = jnp.sum(onehot * before[:, None, :], axis=2)
    return route_row * capacity + position


def on_device(hidden_states, route_ids, route_weights, gate_proj, up_proj, down_proj):
    step_count, row_count, feature_width = hidden_states.shape
    top_count = route_ids.shape[2]
    experts = lax.axis_size("expert") * gate_proj.shape[0]
    capacity = 3 * row_count * top_count // (2 * experts)
    route_slots = []
    outgoing = []
    for step_index in range(step_count):
        targets = slot_index(route_ids[step_index], experts, capacity)
        labels = lax.broadcasted_iota(jnp.int32, (experts * capacity, row_count, top_count), 0)
        selector = jnp.sum((targets[None, :, :] == labels).astype(jnp.int32), axis=2).astype(
            jnp.bfloat16
        )
        packed = jnp.dot(
            selector, hidden_states[step_index], preferred_element_type=jnp.float32
        ).astype(jnp.bfloat16)
        outgoing.append(packed.reshape(experts, capacity, feature_width))
        route_slots.append(targets)

    def serve_one(received):
        return lax.all_to_all(
            expert_rows(received, gate_proj, up_proj, down_proj),
            "expert",
            split_axis=0,
            concat_axis=0,
            tiled=True,
        )

    returned = [
        serve_one(lax.all_to_all(packed, "expert", split_axis=0, concat_axis=0, tiled=True))
        for packed in outgoing
    ]
    outputs = []
    for step_index in range(step_count):
        weights = route_weights[step_index]
        normalized = weights / jnp.sum(weights, axis=1, keepdims=True)
        returned_rows = returned[step_index].reshape(experts * capacity, feature_width)
        gathered = jnp.take(returned_rows, route_slots[step_index], axis=0)
        combined = jnp.sum(gathered.astype(jnp.float32) * normalized[:, :, None], axis=1)
        outputs.append(combined.astype(jnp.bfloat16))
    return jnp.stack(outputs)


def solution(mesh):
    placed = (
        P(None, ("groups", "expert"), None),
        P(None, ("groups", "expert"), None),
        P(None, ("groups", "expert"), None),
        P("expert", None, None),
        P("expert", None, None),
        P("expert", None, None),
    )
    return jax.shard_map(
        on_device,
        mesh=mesh,
        in_specs=placed,
        out_specs=P(None, ("groups", "expert"), None),
        check_vma=False,
    )
```

profile of v0, /device:TPU:13, one launch (start us, length us, event | category | flops | bytes accessed | tf_op | source)
XLA Modules:
  0.0 212.8 jit_solution(2939662833502115000)
XLA Ops:
  0.0 0.7 slice_bitcast_fusion.1
  1.0 0.7 fusion.35
  1.7 0.1 copy.29
  1.7 0.2 convert_reduce_fusion.1
  1.9 2.9 %convolution_convert_fusion.3 = bf16[384,2560]{1,0:T(8,128)(2,1)} fusion(bf16[2,32,2560]{2,1,0:T(8,128)(2,1)} %param.8, s32[384,32]{0,1:T(8,128)S(1)} %convert_reduce_fusion.1), kind=kOutput, calls=%fused_computation.5 | convolution fusion | flops 63909888 | bytes 2179072 | tf_op jit(solution)/shard_map/dot_general | solution.py:40
  4.8 6.7 %all-to-all-start = ((bf16[16,24,2560]{2,1,0:T(8,128)(2,1)}), bf16[16,24,2560]{2,1,0:T(8,128)(2,1)S(1)}, u32[]{:S(2)}, u32[]{:S(2)}) async-start(bf16[16,24,2560]{2,1,0:T(8,128)(2,1)} %bitcast.4), calls=%async_computation | async-start | bytes 3932160 | tf_op jit(solution)/shard_map/all_to_all | solution.py:56
  11.5 0.1 copy.32
  11.8 0.1 copy.36
  11.9 0.2 convert_reduce_fusion
  12.1 2.0 convolution_convert_fusion.1
  14.1 42.1 %all-to-all-done = bf16[16,24,2560]{2,1,0:T(8,128)(2,1)S(1)} async-done(((bf16[16,24,2560]{2,1,0:T(8,128)(2,1)}), bf16[16,24,2560]{2,1,0:T(8,128)(2,1)S(1)}, u32[]{:S(2)}, u32[]{:S(2)}) %all-to-all-start) | async-done | bytes 1966112 | tf_op jit(solution)/shard_map/all_to_all | solution.py:56
  56.1 4.9 %all-to-all-start.2 = ((bf16[16,24,2560]{2,1,0:T(8,128)(2,1)}), bf16[16,24,2560]{2,1,0:T(8,128)(2,1)}, u32[]{:S(2)}, u32[]{:S(2)}) async-start(bf16[16,24,2560]{2,1,0:T(8,128)(2,1)} %bitcast.18), calls=%async_computation.2 | async-start | bytes 3932160 | tf_op jit(solution)/shard_map/all_to_all | solution.py:56
  61.0 3.8 %fusion.8 = f32[384,768]{1,0:T(8,128)S(1)} fusion(bf16[384,2560]{1,0:T(8,128)(2,1)S(1)} %bitcast.87, bf16[1,2560,768]{2,1,0:T(8,128)(2,1)} %param.11), kind=kOutput, calls=%fused_computation.14 | convolution fusion | flops 1509949440 | bytes 7077888 | tf_op jit(solution)/shard_map/dot_general | solution.py:10
  64.8 8.9 %convolution_convert_fusion.2 = bf16[384,2560]{1,0:T(8,128)(2,1)} fusion(bf16[1,768,2560]{2,1,0:T(8,128)(2,1)} %param.13, bf16[384,2560]{1,0:T(8,128)(2,1)S(1)} %bitcast.88, bf16[1,2560,768]{2,1,0:T(8,128)(2,1)} %param.12, f32[384,768]{1,0:T(8,128)S(1)} %fusion.8), kind=kOutput, calls=%fused_computation.4 | convolution fusion | flops 3022651392 | bytes 12976128 | tf_op jit(solution)/shard_map/dot_general | solution.py:13
  73.7 32.1 %all-to-all-done.2 = bf16[16,24,2560]{2,1,0:T(8,128)(2,1)} async-done(((bf16[16,24,2560]{2,1,0:T(8,128)(2,1)}), bf16[16,24,2560]{2,1,0:T(8,128)(2,1)}, u32[]{:S(2)}, u32[]{:S(2)}) %all-to-all-start.2) | async-done | bytes 1966112 | tf_op jit(solution)/shard_map/all_to_all | solution.py:56
  105.8 4.9 %all-to-all-start.1 = ((bf16[16,24,2560]{2,1,0:T(8,128)(2,1)}), bf16[16,24,2560]{2,1,0:T(8,128)(2,1)S(1)}, u32[]{:S(2)}, u32[]{:S(2)}) async-start(bf16[16,24,2560]{2,1,0:T(8,128)(2,1)} %bitcast.89), calls=%async_computation.1 | async-start | bytes 3932160 | tf_op jit(solution)/shard_map/all_to_all | solution.py:47
  110.7 4.4 %fusion.6 = f32[384,768]{1,0:T(8,128)S(1)} fusion(bf16[384,2560]{1,0:T(8,128)(2,1)} %bitcast.19, bf16[1,2560,768]{2,1,0:T(8,128)(2,1)} %param.11), kind=kOutput, calls=%fused_computation.12 | convolution fusion | flops 1509949440 | bytes 7077888 | tf_op jit(solution)/shard_map/dot_general | solution.py:10
  115.1 9.4 %convolution_convert_fusion = bf16[384,2560]{1,0:T(8,128)(2,1)} fusion(bf16[1,768,2560]{2,1,0:T(8,128)(2,1)} %param.13, bf16[384,2560]{1,0:T(8,128)(2,1)} %bitcast.19, bf16[1,2560,768]{2,1,0:T(8,128)(2,1)} %param.12, f32[384,768]{1,0:T(8,128)S(1)} %fusion.6), kind=kOutput, calls=%fused_computation.2 | convolution fusion | flops 3022651392 | bytes 12976128 | tf_op jit(solution)/shard_map/dot_general | solution.py:13
  124.5 30.8 %all-to-all-done.1 = bf16[16,24,2560]{2,1,0:T(8,128)(2,1)S(1)} async-done(((bf16[16,24,2560]{2,1,0:T(8,128)(2,1)}), bf16[16,24,2560]{2,1,0:T(8,128)(2,1)S(1)}, u32[]{:S(2)}, u32[]{:S(2)}) %all-to-all-start.1) | async-done | bytes 1966112 | tf_op jit(solution)/shard_map/all_to_all | solution.py:47
  155.3 5.0 %all-to-all-start.3 = ((bf16[16,24,2560]{2,1,0:T(8,128)(2,1)}), bf16[16,24,2560]{2,1,0:T(8,128)(2,1)}, u32[]{:S(2)}, u32[]{:S(2)}) async-start(bf16[16,24,2560]{2,1,0:T(8,128)(2,1)} %bitcast.86), calls=%async_computation.3 | async-start | bytes 3932160 | tf_op jit(solution)/shard_map/all_to_all | solution.py:47
  160.3 0.1 copy.30
  160.4 0.1 reshape.135
  160.5 0.1 copy.28
  160.6 0.1 copy.31
  160.8 0.1 reshape.139
  160.9 0.1 copy.35
  161.1 1.4 gather_fusion
  162.5 42.5 %all-to-all-done.3 = bf16[16,24,2560]{2,1,0:T(8,128)(2,1)} async-done(((bf16[16,24,2560]{2,1,0:T(8,128)(2,1)}), bf16[16,24,2560]{2,1,0:T(8,128)(2,1)}, u32[]{:S(2)}, u32[]{:S(2)}) %all-to-all-start.3) | async-done | bytes 1966112 | tf_op jit(solution)/shard_map/all_to_all | solution.py:47
  205.0 4.5 %gather_fusion.1 = bf16[256,2560]{1,0:T(8,128)(2,1)S(1)} fusion(bf16[384,2560]{1,0:T(8,128)(2,1)} %bitcast.21, s32[1024]{0:T(1024)S(1)} %pad_clamp_fusion), kind=kCustom, calls=%fused_computation.1.clone | custom fusion | bytes 2622464 | tf_op jit(solution)/shard_map/jit(_take)/gather | solution.py:64
  209.6 1.3 multiply_reduce_fusion.1
  210.8 1.3 multiply_reduce_fusion
  212.1 0.8 pad_maximum_fusion
  (25 shorter events, 0.6 us)
Async XLA Ops:
  4.8 7.0 %copy-start.1 = (s32[2,32,8]{1,2,0:T(8,128)S(1)}, s32[2,32,8]{1,2,0:T(8,128)}, u32[]{:S(2)}) copy-start(s32[2,32,8]{1,2,0:T(8,128)} %param.9) | copy-start | bytes 6148
  4.8 7.2 %copy-start = (bf16[2,32,2560]{2,1,0:T(8,128)(2,1)S(1)}, bf16[2,32,2560]{2,1,0:T(8,128)(2,1)}, u32[]{:S(2)}) copy-start(bf16[2,32,2560]{2,1,0:T(8,128)(2,1)} %param.8) | copy-start | bytes 983044
  4.8 51.3 %all-to-all-start = ((bf16[16,24,2560]{2,1,0:T(8,128)(2,1)}), bf16[16,24,2560]{2,1,0:T(8,128)(2,1)S(1)}, u32[]{:S(2)}, u32[]{:S(2)}) async-start(bf16[16,24,2560]{2,1,0:T(8,128)(2,1)} %bitcast.4), calls=%async_computation | async-start | bytes 3932160 | tf_op jit(solution)/shard_map/all_to_all | solution.py:56
  56.1 49.6 %all-to-all-start.2 = ((bf16[16,24,2560]{2,1,0:T(8,128)(2,1)}), bf16[16,24,2560]{2,1,0:T(8,128)(2,1)}, u32[]{:S(2)}, u32[]{:S(2)}) async-start(bf16[16,24,2560]{2,1,0:T(8,128)(2,1)} %bitcast.18), calls=%async_computation.2 | async-start | bytes 3932160 | tf_op jit(solution)/shard_map/all_to_all | solution.py:56
  105.8 49.5 %all-to-all-start.1 = ((bf16[16,24,2560]{2,1,0:T(8,128)(2,1)}), bf16[16,24,2560]{2,1,0:T(8,128)(2,1)S(1)}, u32[]{:S(2)}, u32[]{:S(2)}) async-start(bf16[16,24,2560]{2,1,0:T(8,128)(2,1)} %bitcast.89), calls=%async_computation.1 | async-start | bytes 3932160 | tf_op jit(solution)/shard_map/all_to_all | solution.py:47
  155.3 5.3 %copy-start.2 = (f32[2,32,8]{1,2,0:T(8,128)S(1)}, f32[2,32,8]{1,2,0:T(8,128)}, u32[]{:S(2)}) copy-start(f32[2,32,8]{1,2,0:T(8,128)} %param.10) | copy-start | bytes 6148
  155.3 49.8 %all-to-all-start.3 = ((bf16[16,24,2560]{2,1,0:T(8,128)(2,1)}), bf16[16,24,2560]{2,1,0:T(8,128)(2,1)}, u32[]{:S(2)}, u32[]{:S(2)}) async-start(bf16[16,24,2560]{2,1,0:T(8,128)(2,1)} %bitcast.86), calls=%async_computation.3 | async-start | bytes 3932160 | tf_op jit(solution)/shard_map/all_to_all | solution.py:47
where the time goes:
time: 213 us
  waiting for transfers between devices  147 us (69%)
  matrix products  31.3 us (15%)
  starting transfers between devices  21.5 us (10%)
  local copies, waits for them, and re-layouts  7.79 us (4%)
  other arithmetic  4.6 us (2%)
    all_to_all x2, waiting for transfers between devices, on_device(): lax.all_to_all(packed, 'expert', split_axis=0, concat_axis=0, tiled=True)  74.1 us
    all_to_all x2, waiting for transfers between devices, serve_one(): lax.all_to_all(expert_rows(received, gate_proj, up_proj, down_proj), 'exp...  73.3 us
    dot_general x2, matrix products, expert_rows(): result = jnp.dot(hidden, down_proj[0], preferred_element_type=jnp.float32)  18.3 us
    all_to_all x2, starting transfers between devices, on_device(): lax.all_to_all(packed, 'expert', split_axis=0, concat_axis=0, tiled=True)  11.6 us
    all_to_all x2, starting transfers between devices, serve_one(): lax.all_to_all(expert_rows(received, gate_proj, up_proj, down_proj), 'exp...  9.95 us
    dot_general x2, matrix products, expert_rows(): jnp.dot(stacked, gate_proj[0], preferred_element_type=jnp.float32)  8.18 us
    gather x2, local copies, waits for them, and re-layouts, on_device(): gathered = jnp.take(returned_rows, route_slots[step_index], axis=0)  5.97 us
    dot_general x2, matrix products, on_device(): jnp.dot(selector, hidden_states[step_index], preferred_element_type=jnp.f...  4.87 us
  transfers between devices with their start and end apart: 4, of which 4 were waited for; matrix products, arithmetic and copies ran while one was open for 15% of the time, Pallas kernels for 0%

commit v1 on v0

v1 whole, which is shorter than its diff:
```python
import jax
import jax.numpy as jnp
from jax import lax
from jax.sharding import PartitionSpec as P

PIECES = 4


def swap(array, axis_size, bit):
    return lax.ppermute(array, "expert", [(i, i ^ bit) for i in range(axis_size)])


def dense_weights(route_ids, route_weights, experts):
    normalized = route_weights / jnp.sum(route_weights, axis=1, keepdims=True)
    labels = lax.broadcasted_iota(jnp.int32, (*route_ids.shape, experts), 2)
    chosen = jnp.where(route_ids[:, :, None] == labels, normalized[:, :, None], 0.0)
    return jnp.sum(chosen, axis=1)


def with_weights(rows, weights):
    high = weights.astype(jnp.bfloat16)
    low = (weights - high.astype(jnp.float32)).astype(jnp.bfloat16)
    experts = weights.shape[1]
    fill = -2 * experts % 128
    return jnp.concatenate(
        [rows, high, low, jnp.zeros((rows.shape[0], fill), jnp.bfloat16)], axis=1
    )


def expert_rows(rows, experts, gate_proj, up_proj, down_proj):
    width = gate_proj.shape[0]
    own = lax.axis_index("expert")
    tokens = rows[:, :width]
    spread = rows[:, width : width + 2 * experts].astype(jnp.float32)
    lane = lax.broadcasted_iota(jnp.int32, spread.shape, 1)
    weight = jnp.sum(jnp.where(lane % experts == own, spread, 0.0), axis=1, keepdims=True)
    gate_values = jnp.dot(tokens, gate_proj, preferred_element_type=jnp.float32)
    up_values = jnp.dot(tokens, up_proj, preferred_element_type=jnp.float32)
    hidden = (jax.nn.silu(gate_values) * up_values).astype(jnp.bfloat16)
    result = jnp.dot(hidden, down_proj, preferred_element_type=jnp.float32)
    return (result * weight).astype(jnp.bfloat16)


def on_device(hidden_states, route_ids, route_weights, gate_proj, up_proj, down_proj):
    step_count, row_count, feature_width = hidden_states.shape
    axis_size = lax.axis_size("expert")
    experts = axis_size * gate_proj.shape[0]
    total = step_count * row_count
    share = total // PIECES
    bits = [1 << i for i in reversed(range(axis_size.bit_length() - 1))]
    weights = dense_weights(
        route_ids.reshape(total, -1), route_weights.reshape(total, -1), experts
    )
    rows = with_weights(hidden_states.reshape(total, feature_width), weights)
    outputs = []
    for piece in range(PIECES):
        held = rows[piece * share : (piece + 1) * share]
        for bit in bits:
            held = jnp.concatenate([held, swap(held, axis_size, bit)], axis=0)
        sums = expert_rows(held, experts, gate_proj[0], up_proj[0], down_proj[0])
        for bit in reversed(bits):
            half = sums.shape[0] // 2
            arrived = swap(sums[half:], axis_size, bit)
            sums = (
                sums[:half].astype(jnp.float32) + arrived.astype(jnp.float32)
            ).astype(jnp.bfloat16)
        outputs.append(sums)
    return jnp.concatenate(outputs, axis=0).reshape(hidden_states.shape)


def solution(mesh):
    placed = (
        P(None, ("groups", "expert"), None),
        P(None, ("groups", "expert"), None),
        P(None, ("groups", "expert"), None),
        P("expert", None, None),
        P("expert", None, None),
        P("expert", None, None),
    )
    return jax.shard_map(
        on_device,
        mesh=mesh,
        in_specs=placed,
        out_specs=P(None, ("groups", "expert"), None),
        check_vma=False,
    )
```

time: 213 us -> 155 us (0.73)
  the two profiles are of different devices: /device:TPU:13 before, /device:TPU:0 now
where the time goes in v1:
time: 155 us
  waiting for transfers between devices  72.8 us (47%)
  matrix products  35.6 us (23%)
  starting transfers between devices  30.7 us (20%)
  local copies, waits for them, and re-layouts  8.65 us (6%)
  other arithmetic  6.49 us (4%)
    ppermute x32, waiting for transfers between devices, swap(): lax.ppermute(array, 'expert', [(i, i ^ bit) for i in range(axis_size)])  72.8 us
    ppermute x32, starting transfers between devices, swap(): lax.ppermute(array, 'expert', [(i, i ^ bit) for i in range(axis_size)])  30.7 us
    dot_general x4, matrix products, expert_rows(): result = jnp.dot(hidden, down_proj, preferred_element_type=jnp.float32)  27.3 us
    dot_general x4, matrix products, expert_rows(): up_values = jnp.dot(tokens, up_proj, preferred_element_type=jnp.float32)  8.25 us
    convert_element_type x16, other arithmetic, on_device(): sums = (sums[:half].astype(jnp.float32) + arrived.astype(jnp.float32)).as...  4.43 us
    unnamed x36, local copies, waits for them, and re-layouts  3.82 us
  transfers between devices with their start and end apart: 32, of which 20 were waited for; matrix products, arithmetic and copies ran while one was open for 21% of the time, Pallas kernels for 0%

profile of v1, /device:TPU:0, one launch (start us, length us, event | category | flops | bytes accessed | tf_op | source)
XLA Modules:
  0.0 154.8 jit_solution(6155610414881098237)
XLA Ops:
  4.4 4.0 %collective-permute-start.24 = (bf16[16,2688]{1,0:T(8,128)(2,1)S(1)}, bf16[16,2688]{1,0:T(8,128)(2,1)S(1)}, u32[]{:S(2)}, u32[]{:S(2)}) collective-permute-start(bf16[16,2688]{1,0:T(8,128)(2,1)S(1)} %get-tuple-element.16), channel_id=1, source_target_pairs={{0,8},{1,9},{2,10},{3,11},{4,12},{5,13},{6,14},{7,15},{8,0},{9,1},... | collective-permute-start | bytes 258056 | tf_op jit(solution)/shard_map/ppermute | solution.py:10
  8.5 2.9 %collective-permute-start.8 = (bf16[16,2688]{1,0:T(8,128)(2,1)S(1)}, bf16[16,2688]{1,0:T(8,128)(2,1)S(1)}, u32[]{:S(2)}, u32[]{:S(2)}) collective-permute-start(bf16[16,2688]{1,0:T(8,128)(2,1)S(1)} %get-tuple-element.11), channel_id=1, source_target_pairs={{0,8},{1,9},{2,10},{3,11},{4,12},{5,13},{6,14},{7,15},{8,0},{9,1},... | collective-permute-start | bytes 258056 | tf_op jit(solution)/shard_map/ppermute | solution.py:10
  11.4 7.4 %collective-permute-done.24 = bf16[16,2688]{1,0:T(8,128)(2,1)S(1)} collective-permute-done((bf16[16,2688]{1,0:T(8,128)(2,1)S(1)}, bf16[16,2688]{1,0:T(8,128)(2,1)S(1)}, u32[]{:S(2)}, u32[]{:S(2)}) %collective-permute-start.24) | collective-permute-done | bytes 86048 | tf_op jit(solution)/shard_map/ppermute | solution.py:10
  27.7 1.7 %collective-permute-start.26 = (bf16[64,2688]{1,0:T(8,128)(2,1)S(1)}, bf16[64,2688]{1,0:T(8,128)(2,1)S(1)}, u32[]{:S(2)}, u32[]{:S(2)}) collective-permute-start(bf16[64,2688]{1,0:T(8,128)(2,1)S(1)} %pad_maximum_fusion.7), channel_id=1, source_target_pairs={{0,2},{1,3},{2,0},{3,1},{4,6},{5,7},{6,4},{7,5},{8,10},{9,11},{10,... | collective-permute-start | bytes 1032200 | tf_op jit(solution)/shard_map/ppermute | solution.py:10
  29.4 1.9 %collective-permute-done.17 = bf16[32,2688]{1,0:T(8,128)(2,1)S(1)} collective-permute-done((bf16[32,2688]{1,0:T(8,128)(2,1)S(1)}, bf16[32,2688]{1,0:T(8,128)(2,1)S(1)}, u32[]{:S(2)}, u32[]{:S(2)}) %collective-permute-start.17) | collective-permute-done | bytes 172064 | tf_op jit(solution)/shard_map/ppermute | solution.py:10
  31.4 1.7 %collective-permute-start.18 = (bf16[64,2688]{1,0:T(8,128)(2,1)S(1)}, bf16[64,2688]{1,0:T(8,128)(2,1)S(1)}, u32[]{:S(2)}, u32[]{:S(2)}) collective-permute-start(bf16[64,2688]{1,0:T(8,128)(2,1)S(1)} %pad_maximum_fusion.6), channel_id=1, source_target_pairs={{0,2},{1,3},{2,0},{3,1},{4,6},{5,7},{6,4},{7,5},{8,10},{9,11},{10,... | collective-permute-start | bytes 1032200 | tf_op jit(solution)/shard_map/ppermute | solution.py:10
  33.1 1.9 %collective-permute-done.9 = bf16[32,2688]{1,0:T(8,128)(2,1)S(1)} collective-permute-done((bf16[32,2688]{1,0:T(8,128)(2,1)S(1)}, bf16[32,2688]{1,0:T(8,128)(2,1)S(1)}, u32[]{:S(2)}, u32[]{:S(2)}) %collective-permute-start.9) | collective-permute-done | bytes 172064 | tf_op jit(solution)/shard_map/ppermute | solution.py:10
  35.1 1.7 %collective-permute-start.10 = (bf16[64,2688]{1,0:T(8,128)(2,1)S(1)}, bf16[64,2688]{1,0:T(8,128)(2,1)S(1)}, u32[]{:S(2)}, u32[]{:S(2)}) collective-permute-start(bf16[64,2688]{1,0:T(8,128)(2,1)S(1)} %pad_maximum_fusion.5), channel_id=1, source_target_pairs={{0,2},{1,3},{2,0},{3,1},{4,6},{5,7},{6,4},{7,5},{8,10},{9,11},{10,... | collective-permute-start | bytes 1032200 | tf_op jit(solution)/shard_map/ppermute | solution.py:10
  36.8 1.8 %collective-permute-done.1 = bf16[32,2688]{1,0:T(8,128)(2,1)S(1)} collective-permute-done((bf16[32,2688]{1,0:T(8,128)(2,1)S(1)}, bf16[32,2688]{1,0:T(8,128)(2,1)S(1)}, u32[]{:S(2)}, u32[]{:S(2)}) %collective-permute-start.1) | collective-permute-done | bytes 172064 | tf_op jit(solution)/shard_map/ppermute | solution.py:10
  38.7 1.7 %collective-permute-start.2 = (bf16[64,2688]{1,0:T(8,128)(2,1)S(1)}, bf16[64,2688]{1,0:T(8,128)(2,1)S(1)}, u32[]{:S(2)}, u32[]{:S(2)}) collective-permute-start(bf16[64,2688]{1,0:T(8,128)(2,1)S(1)} %pad_maximum_fusion.4), channel_id=1, source_target_pairs={{0,2},{1,3},{2,0},{3,1},{4,6},{5,7},{6,4},{7,5},{8,10},{9,11},{10,... | collective-permute-start | bytes 1032200 | tf_op jit(solution)/shard_map/ppermute | solution.py:10
  40.7 5.4 %collective-permute-done.18 = bf16[64,2688]{1,0:T(8,128)(2,1)S(1)} collective-permute-done((bf16[64,2688]{1,0:T(8,128)(2,1)S(1)}, bf16[64,2688]{1,0:T(8,128)(2,1)S(1)}, u32[]{:S(2)}, u32[]{:S(2)}) %collective-permute-start.18) | collective-permute-done | bytes 344096 | tf_op jit(solution)/shard_map/ppermute | solution.py:10
  46.2 7.2 %collective-permute-done.10 = bf16[64,2688]{1,0:T(8,128)(2,1)S(1)} collective-permute-done((bf16[64,2688]{1,0:T(8,128)(2,1)S(1)}, bf16[64,2688]{1,0:T(8,128)(2,1)S(1)}, u32[]{:S(2)}, u32[]{:S(2)}) %collective-permute-start.10) | collective-permute-done | bytes 344096 | tf_op jit(solution)/shard_map/ppermute | solution.py:10
  53.6 6.2 %collective-permute-done.2 = bf16[64,2688]{1,0:T(8,128)(2,1)S(1)} collective-permute-done((bf16[64,2688]{1,0:T(8,128)(2,1)S(1)}, bf16[64,2688]{1,0:T(8,128)(2,1)S(1)}, u32[]{:S(2)}, u32[]{:S(2)}) %collective-permute-start.2) | collective-permute-done | bytes 344096 | tf_op jit(solution)/shard_map/ppermute | solution.py:10
  60.1 2.0 %collective-permute-done.3 = bf16[128,2688]{1,0:T(8,128)(2,1)S(1)} collective-permute-done((bf16[128,2688]{1,0:T(8,128)(2,1)S(1)}, bf16[128,2688]{1,0:T(8,128)(2,1)S(1)}, u32[]{:S(2)}, u32[]{:S(2)}) %collective-permute-start.3) | collective-permute-done | bytes 688160 | tf_op jit(solution)/shard_map/ppermute | solution.py:10
  62.3 2.1 %fusion.10 = f32[256,768]{1,0:T(8,128)} fusion(bf16[1,2560,768]{2,1,0:T(8,128)(2,1)S(1)} %copy-done.10, bf16[256,2688]{1,0:T(8,128)(2,1)S(1)} %get-tuple-element.19), kind=kOutput, calls=%fused_computation.14 | convolution fusion | flops 1006632960 | bytes 6029312 | tf_op jit(solution)/shard_map/dot_general | solution.py:38
  64.3 2.1 %fusion.8 = f32[256,768]{1,0:T(8,128)} fusion(bf16[1,2560,768]{2,1,0:T(8,128)(2,1)S(1)} %copy-done.10, bf16[256,2688]{1,0:T(8,128)(2,1)S(1)} %get-tuple-element.20), kind=kOutput, calls=%fused_computation.12 | convolution fusion | flops 1006632960 | bytes 6029312 | tf_op jit(solution)/shard_map/dot_general | solution.py:38
  66.6 2.1 %fusion.6 = f32[256,768]{1,0:T(8,128)} fusion(bf16[1,2560,768]{2,1,0:T(8,128)(2,1)S(1)} %copy-done.10, bf16[256,2688]{1,0:T(8,128)(2,1)S(1)} %get-tuple-element.21), kind=kOutput, calls=%fused_computation.10 | convolution fusion | flops 1006632960 | bytes 6029312 | tf_op jit(solution)/shard_map/dot_general | solution.py:38
  68.7 2.1 %fusion.4 = f32[256,768]{1,0:T(8,128)} fusion(bf16[1,2560,768]{2,1,0:T(8,128)(2,1)S(1)} %copy-done.10, bf16[256,2688]{1,0:T(8,128)(2,1)S(1)} %get-tuple-element.22), kind=kOutput, calls=%fused_computation.8 | convolution fusion | flops 1006632960 | bytes 6029312 | tf_op jit(solution)/shard_map/dot_general | solution.py:38
  70.9 6.5 %fusion.20 = bf16[256,2560]{1,0:T(8,128)(2,1)S(1)} fusion(bf16[1,768,2560]{2,1,0:T(8,128)(2,1)} %param.11, f32[256]{0:T(256)S(1)} %get-tuple-element.5, f32[256,768]{1,0:T(8,128)} %fusion.10, bf16[1,2560,768]{2,1,0:T(8,128)(2,1)} %param.9, bf16[256,2688]{1,0:T(8,128)(2,1)S(1)} %get-tuple-element.19), kind=kOutput, calls=%fused_computation.24 | convolution fusion | flops 2015756288 | bytes 11273216 | tf_op jit(solution)/shard_map/dot_general | solution.py:40
  78.8 6.9 %fusion.23 = bf16[256,2560]{1,0:T(8,128)(2,1)S(1)} fusion(bf16[1,768,2560]{2,1,0:T(8,128)(2,1)} %param.11, f32[256]{0:T(256)S(1)} %get-tuple-element.8, f32[256,768]{1,0:T(8,128)} %fusion.8, bf16[1,2560,768]{2,1,0:T(8,128)(2,1)} %param.9, bf16[256,2688]{1,0:T(8,128)(2,1)} %copy-done.5), kind=kOutput, calls=%fused_computation.25 | convolution fusion | flops 2015756288 | bytes 11273216 | tf_op jit(solution)/shard_map/dot_general | solution.py:40
  86.9 7.1 %fusion.26 = bf16[256,2560]{1,0:T(8,128)(2,1)S(1)} fusion(bf16[1,768,2560]{2,1,0:T(8,128)(2,1)} %param.11, f32[256]{0:T(256)S(1)} %get-tuple-element.7, f32[256,768]{1,0:T(8,128)} %fusion.6, bf16[1,2560,768]{2,1,0:T(8,128)(2,1)} %param.9, bf16[256,2688]{1,0:T(8,128)(2,1)} %copy-done.7), kind=kOutput, calls=%fused_computation.26 | convolution fusion | flops 2015756288 | bytes 11273216 | tf_op jit(solution)/shard_map/dot_general | solution.py:40
  94.3 6.9 %fusion.29 = bf16[256,2560]{1,0:T(8,128)(2,1)S(1)} fusion(bf16[1,768,2560]{2,1,0:T(8,128)(2,1)} %param.11, f32[256]{0:T(256)S(1)} %get-tuple-element.6, f32[256,768]{1,0:T(8,128)} %fusion.4, bf16[1,2560,768]{2,1,0:T(8,128)(2,1)} %param.9, bf16[256,2688]{1,0:T(8,128)(2,1)} %copy-done.9), kind=kOutput, calls=%fused_computation.27 | convolution fusion | flops 2015756288 | bytes 11273216 | tf_op jit(solution)/shard_map/dot_general | solution.py:40
  103.8 1.7 %collective-permute-start.5 = (bf16[64,2560]{1,0:T(8,128)(2,1)S(1)}, bf16[64,2560]{1,0:T(8,128)(2,1)S(1)}, u32[]{:S(2)}, u32[]{:S(2)}) collective-permute-start(bf16[64,2560]{1,0:T(8,128)(2,1)S(1)} %slice.182), channel_id=1, source_target_pairs={{0,2},{1,3},{2,0},{3,1},{4,6},{5,7},{6,4},{7,5},{8,10},{9,11},{10,... | collective-permute-start | bytes 983048 | tf_op jit(solution)/shard_map/ppermute | solution.py:10
  108.5 1.7 %collective-permute-start.21 = (bf16[64,2560]{1,0:T(8,128)(2,1)S(1)}, bf16[64,2560]{1,0:T(8,128)(2,1)S(1)}, u32[]{:S(2)}, u32[]{:S(2)}) collective-permute-start(bf16[64,2560]{1,0:T(8,128)(2,1)S(1)} %slice.204), channel_id=1, source_target_pairs={{0,2},{1,3},{2,0},{3,1},{4,6},{5,7},{6,4},{7,5},{8,10},{9,11},{10,... | collective-permute-start | bytes 983048 | tf_op jit(solution)/shard_map/ppermute | solution.py:10
  110.9 3.5 %collective-permute-done.5 = bf16[64,2560]{1,0:T(8,128)(2,1)S(1)} collective-permute-done((bf16[64,2560]{1,0:T(8,128)(2,1)S(1)}, bf16[64,2560]{1,0:T(8,128)(2,1)S(1)}, u32[]{:S(2)}, u32[]{:S(2)}) %collective-permute-start.5) | collective-permute-done | bytes 327712 | tf_op jit(solution)/shard_map/ppermute | solution.py:10
  114.6 6.8 %collective-permute-done.13 = bf16[64,2560]{1,0:T(8,128)(2,1)S(1)} collective-permute-done((bf16[64,2560]{1,0:T(8,128)(2,1)S(1)}, bf16[64,2560]{1,0:T(8,128)(2,1)S(1)}, u32[]{:S(2)}, u32[]{:S(2)}) %collective-permute-start.13) | collective-permute-done | bytes 327712 | tf_op jit(solution)/shard_map/ppermute | solution.py:10
  121.6 6.8 %collective-permute-done.21 = bf16[64,2560]{1,0:T(8,128)(2,1)S(1)} collective-permute-done((bf16[64,2560]{1,0:T(8,128)(2,1)S(1)}, bf16[64,2560]{1,0:T(8,128)(2,1)S(1)}, u32[]{:S(2)}, u32[]{:S(2)}) %collective-permute-start.21) | collective-permute-done | bytes 327712 | tf_op jit(solution)/shard_map/ppermute | solution.py:10
  128.6 6.3 %collective-permute-done.29 = bf16[64,2560]{1,0:T(8,128)(2,1)S(1)} collective-permute-done((bf16[64,2560]{1,0:T(8,128)(2,1)S(1)}, bf16[64,2560]{1,0:T(8,128)(2,1)S(1)}, u32[]{:S(2)}, u32[]{:S(2)}) %collective-permute-start.29) | collective-permute-done | bytes 327712 | tf_op jit(solution)/shard_map/ppermute | solution.py:10
  135.1 4.1 %collective-permute-start.7 = (bf16[16,2560]{1,0:T(8,128)(2,1)S(1)}, bf16[16,2560]{1,0:T(8,128)(2,1)S(1)}, u32[]{:S(2)}, u32[]{:S(2)}) collective-permute-start(bf16[16,2560]{1,0:T(8,128)(2,1)S(1)} %slice.186), channel_id=1, source_target_pairs={{0,8},{1,9},{2,10},{3,11},{4,12},{5,13},{6,14},{7,15},{8,0},{9,1},... | collective-permute-start | bytes 245768 | tf_op jit(solution)/shard_map/ppermute | solution.py:10
  139.5 3.0 %collective-permute-start.23 = (bf16[16,2560]{1,0:T(8,128)(2,1)S(1)}, bf16[16,2560]{1,0:T(8,128)(2,1)S(1)}, u32[]{:S(2)}, u32[]{:S(2)}) collective-permute-start(bf16[16,2560]{1,0:T(8,128)(2,1)S(1)} %slice.208), channel_id=1, source_target_pairs={{0,8},{1,9},{2,10},{3,11},{4,12},{5,13},{6,14},{7,15},{8,0},{9,1},... | collective-permute-start | bytes 245768 | tf_op jit(solution)/shard_map/ppermute | solution.py:10
  144.4 7.0 %collective-permute-done.15 = bf16[16,2560]{1,0:T(8,128)(2,1)S(1)} collective-permute-done((bf16[16,2560]{1,0:T(8,128)(2,1)S(1)}, bf16[16,2560]{1,0:T(8,128)(2,1)S(1)}, u32[]{:S(2)}, u32[]{:S(2)}) %collective-permute-start.15) | collective-permute-done | bytes 81952 | tf_op jit(solution)/shard_map/ppermute | solution.py:10
  151.4 1.7 %collective-permute-done.23 = bf16[16,2560]{1,0:T(8,128)(2,1)S(1)} collective-permute-done((bf16[16,2560]{1,0:T(8,128)(2,1)S(1)}, bf16[16,2560]{1,0:T(8,128)(2,1)S(1)}, u32[]{:S(2)}, u32[]{:S(2)}) %collective-permute-start.23) | collective-permute-done | bytes 81952 | tf_op jit(solution)/shard_map/ppermute | solution.py:10
  (138 shorter events, 28.2 us)
Async XLA Ops:
  4.4 14.4 %collective-permute-start.24 = (bf16[16,2688]{1,0:T(8,128)(2,1)S(1)}, bf16[16,2688]{1,0:T(8,128)(2,1)S(1)}, u32[]{:S(2)}, u32[]{:S(2)}) collective-permute-start(bf16[16,2688]{1,0:T(8,128)(2,1)S(1)} %get-tuple-element.16), channel_id=1, source_target_pairs={{0,8},{1,9},{2,10},{3,11},{4,12},{5,13},{6,14},{7,15},{8,0},{9,1},... | collective-permute-start | bytes 258056 | tf_op jit(solution)/shard_map/ppermute | solution.py:10
  8.5 12.3 %collective-permute-start.16 = (bf16[16,2688]{1,0:T(8,128)(2,1)S(1)}, bf16[16,2688]{1,0:T(8,128)(2,1)S(1)}, u32[]{:S(2)}, u32[]{:S(2)}) collective-permute-start(bf16[16,2688]{1,0:T(8,128)(2,1)S(1)} %get-tuple-element.17), channel_id=1, source_target_pairs={{0,8},{1,9},{2,10},{3,11},{4,12},{5,13},{6,14},{7,15},{8,0},{9,1},... | collective-permute-start | bytes 258056 | tf_op jit(solution)/shard_map/ppermute | solution.py:10
  8.5 14.1 %collective-permute-start.8 = (bf16[16,2688]{1,0:T(8,128)(2,1)S(1)}, bf16[16,2688]{1,0:T(8,128)(2,1)S(1)}, u32[]{:S(2)}, u32[]{:S(2)}) collective-permute-start(bf16[16,2688]{1,0:T(8,128)(2,1)S(1)} %get-tuple-element.11), channel_id=1, source_target_pairs={{0,8},{1,9},{2,10},{3,11},{4,12},{5,13},{6,14},{7,15},{8,0},{9,1},... | collective-permute-start | bytes 258056 | tf_op jit(solution)/shard_map/ppermute | solution.py:10
  11.4 12.6 %collective-permute-start = (bf16[16,2688]{1,0:T(8,128)(2,1)S(1)}, bf16[16,2688]{1,0:T(8,128)(2,1)S(1)}, u32[]{:S(2)}, u32[]{:S(2)}) collective-permute-start(bf16[16,2688]{1,0:T(8,128)(2,1)S(1)} %get-tuple-element.18), channel_id=1, source_target_pairs={{0,8},{1,9},{2,10},{3,11},{4,12},{5,13},{6,14},{7,15},{8,0},{9,1},... | collective-permute-start | bytes 258056 | tf_op jit(solution)/shard_map/ppermute | solution.py:10
  18.9 8.8 %collective-permute-start.25 = (bf16[32,2688]{1,0:T(8,128)(2,1)S(1)}, bf16[32,2688]{1,0:T(8,128)(2,1)S(1)}, u32[]{:S(2)}, u32[]{:S(2)}) collective-permute-start(bf16[32,2688]{1,0:T(8,128)(2,1)S(1)} %pad_maximum_fusion.12), channel_id=1, source_target_pairs={{0,4},{1,5},{2,6},{3,7},{4,0},{5,1},{6,2},{7,3},{8,12},{9,13},{10,... | collective-permute-start | bytes 516104 | tf_op jit(solution)/shard_map/ppermute | solution.py:10
  20.8 10.6 %collective-permute-start.17 = (bf16[32,2688]{1,0:T(8,128)(2,1)S(1)}, bf16[32,2688]{1,0:T(8,128)(2,1)S(1)}, u32[]{:S(2)}, u32[]{:S(2)}) collective-permute-start(bf16[32,2688]{1,0:T(8,128)(2,1)S(1)} %pad_maximum_fusion.11), channel_id=1, source_target_pairs={{0,4},{1,5},{2,6},{3,7},{4,0},{5,1},{6,2},{7,3},{8,12},{9,13},{10,... | collective-permute-start | bytes 516104 | tf_op jit(solution)/shard_map/ppermute | solution.py:10
  22.7 12.4 %collective-permute-start.9 = (bf16[32,2688]{1,0:T(8,128)(2,1)S(1)}, bf16[32,2688]{1,0:T(8,128)(2,1)S(1)}, u32[]{:S(2)}, u32[]{:S(2)}) collective-permute-start(bf16[32,2688]{1,0:T(8,128)(2,1)S(1)} %pad_maximum_fusion.10), channel_id=1, source_target_pairs={{0,4},{1,5},{2,6},{3,7},{4,0},{5,1},{6,2},{7,3},{8,12},{9,13},{10,... | collective-permute-start | bytes 516104 | tf_op jit(solution)/shard_map/ppermute | solution.py:10
  24.0 14.6 %collective-permute-start.1 = (bf16[32,2688]{1,0:T(8,128)(2,1)S(1)}, bf16[32,2688]{1,0:T(8,128)(2,1)S(1)}, u32[]{:S(2)}, u32[]{:S(2)}) collective-permute-start(bf16[32,2688]{1,0:T(8,128)(2,1)S(1)} %pad_maximum_fusion.9), channel_id=1, source_target_pairs={{0,4},{1,5},{2,6},{3,7},{4,0},{5,1},{6,2},{7,3},{8,12},{9,13},{10,... | collective-permute-start | bytes 516104 | tf_op jit(solution)/shard_map/ppermute | solution.py:10
  27.7 12.8 %collective-permute-start.26 = (bf16[64,2688]{1,0:T(8,128)(2,1)S(1)}, bf16[64,2688]{1,0:T(8,128)(2,1)S(1)}, u32[]{:S(2)}, u32[]{:S(2)}) collective-permute-start(bf16[64,2688]{1,0:T(8,128)(2,1)S(1)} %pad_maximum_fusion.7), channel_id=1, source_target_pairs={{0,2},{1,3},{2,0},{3,1},{4,6},{5,7},{6,4},{7,5},{8,10},{9,11},{10,... | collective-permute-start | bytes 1032200 | tf_op jit(solution)/shard_map/ppermute | solution.py:10
  31.4 14.7 %collective-permute-start.18 = (bf16[64,2688]{1,0:T(8,128)(2,1)S(1)}, bf16[64,2688]{1,0:T(8,128)(2,1)S(1)}, u32[]{:S(2)}, u32[]{:S(2)}) collective-permute-start(bf16[64,2688]{1,0:T(8,128)(2,1)S(1)} %pad_maximum_fusion.6), channel_id=1, source_target_pairs={{0,2},{1,3},{2,0},{3,1},{4,6},{5,7},{6,4},{7,5},{8,10},{9,11},{10,... | collective-permute-start | bytes 1032200 | tf_op jit(solution)/shard_map/ppermute | solution.py:10
  35.1 18.4 %collective-permute-start.10 = (bf16[64,2688]{1,0:T(8,128)(2,1)S(1)}, bf16[64,2688]{1,0:T(8,128)(2,1)S(1)}, u32[]{:S(2)}, u32[]{:S(2)}) collective-permute-start(bf16[64,2688]{1,0:T(8,128)(2,1)S(1)} %pad_maximum_fusion.5), channel_id=1, source_target_pairs={{0,2},{1,3},{2,0},{3,1},{4,6},{5,7},{6,4},{7,5},{8,10},{9,11},{10,... | collective-permute-start | bytes 1032200 | tf_op jit(solution)/shard_map/ppermute | solution.py:10
  38.7 21.1 %collective-permute-start.2 = (bf16[64,2688]{1,0:T(8,128)(2,1)S(1)}, bf16[64,2688]{1,0:T(8,128)(2,1)S(1)}, u32[]{:S(2)}, u32[]{:S(2)}) collective-permute-start(bf16[64,2688]{1,0:T(8,128)(2,1)S(1)} %pad_maximum_fusion.4), channel_id=1, source_target_pairs={{0,2},{1,3},{2,0},{3,1},{4,6},{5,7},{6,4},{7,5},{8,10},{9,11},{10,... | collective-permute-start | bytes 1032200 | tf_op jit(solution)/shard_map/ppermute | solution.py:10
  40.6 25.8 %collective-permute-start.27 = (bf16[128,2688]{1,0:T(8,128)(2,1)S(1)}, bf16[128,2688]{1,0:T(8,128)(2,1)S(1)}, u32[]{:S(2)}, u32[]{:S(2)}) collective-permute-start(bf16[128,2688]{1,0:T(8,128)(2,1)S(1)} %pad_maximum_fusion.3), channel_id=1, source_target_pairs={{0,1},{1,0},{2,3},{3,2},{4,5},{5,4},{6,7},{7,6},{8,9},{9,8},{10,11... | collective-permute-start | bytes 2064392 | tf_op jit(solution)/shard_map/ppermute | solution.py:10
  46.1 20.3 %collective-permute-start.19 = (bf16[128,2688]{1,0:T(8,128)(2,1)S(1)}, bf16[128,2688]{1,0:T(8,128)(2,1)S(1)}, u32[]{:S(2)}, u32[]{:S(2)}) collective-permute-start(bf16[128,2688]{1,0:T(8,128)(2,1)S(1)} %pad_maximum_fusion.2), channel_id=1, source_target_pairs={{0,1},{1,0},{2,3},{3,2},{4,5},{5,4},{6,7},{7,6},{8,9},{9,8},{10,11... | collective-permute-start | bytes 2064392 | tf_op jit(solution)/shard_map/ppermute | solution.py:10
  53.5 6.6 %collective-permute-start.11 = (bf16[128,2688]{1,0:T(8,128)(2,1)S(1)}, bf16[128,2688]{1,0:T(8,128)(2,1)S(1)}, u32[]{:S(2)}, u32[]{:S(2)}) collective-permute-start(bf16[128,2688]{1,0:T(8,128)(2,1)S(1)} %pad_maximum_fusion.1), channel_id=1, source_target_pairs={{0,1},{1,0},{2,3},{3,2},{4,5},{5,4},{6,7},{7,6},{8,9},{9,8},{10,11... | collective-permute-start | bytes 2064392 | tf_op jit(solution)/shard_map/ppermute | solution.py:10
  59.8 2.2 %collective-permute-start.3 = (bf16[128,2688]{1,0:T(8,128)(2,1)S(1)}, bf16[128,2688]{1,0:T(8,128)(2,1)S(1)}, u32[]{:S(2)}, u32[]{:S(2)}) collective-permute-start(bf16[128,2688]{1,0:T(8,128)(2,1)S(1)} %pad_maximum_fusion), channel_id=1, source_target_pairs={{0,1},{1,0},{2,3},{3,2},{4,5},{5,4},{6,7},{7,6},{8,9},{9,8},{10,11... | collective-permute-start | bytes 2064392 | tf_op jit(solution)/shard_map/ppermute | solution.py:10
  78.4 23.2 %collective-permute-start.4 = (bf16[128,2560]{1,0:T(8,128)(2,1)}, bf16[128,2560]{1,0:T(8,128)(2,1)}, u32[]{:S(2)}, u32[]{:S(2)}) collective-permute-start(bf16[128,2560]{1,0:T(8,128)(2,1)} %slice.180), channel_id=1, source_target_pairs={{0,1},{1,0},{2,3},{3,2},{4,5},{5,4},{6,7},{7,6},{8,9},{9,8},{10,11... | collective-permute-start | bytes 1966088 | tf_op jit(solution)/shard_map/ppermute | solution.py:10
  86.6 18.9 %collective-permute-start.12 = (bf16[128,2560]{1,0:T(8,128)(2,1)}, bf16[128,2560]{1,0:T(8,128)(2,1)}, u32[]{:S(2)}, u32[]{:S(2)}) collective-permute-start(bf16[128,2560]{1,0:T(8,128)(2,1)} %slice.191), channel_id=1, source_target_pairs={{0,1},{1,0},{2,3},{3,2},{4,5},{5,4},{6,7},{7,6},{8,9},{9,8},{10,11... | collective-permute-start | bytes 1966088 | tf_op jit(solution)/shard_map/ppermute | solution.py:10
  94.1 13.2 %collective-permute-start.20 = (bf16[128,2560]{1,0:T(8,128)(2,1)S(1)}, bf16[128,2560]{1,0:T(8,128)(2,1)}, u32[]{:S(2)}, u32[]{:S(2)}) collective-permute-start(bf16[128,2560]{1,0:T(8,128)(2,1)S(1)} %slice.202), channel_id=1, source_target_pairs={{0,1},{1,0},{2,3},{3,2},{4,5},{5,4},{6,7},{7,6},{8,9},{9,8},{10,11... | collective-permute-start | bytes 1966088 | tf_op jit(solution)/shard_map/ppermute | solution.py:10
  101.3 9.0 %collective-permute-start.28 = (bf16[128,2560]{1,0:T(8,128)(2,1)S(1)}, bf16[128,2560]{1,0:T(8,128)(2,1)S(1)}, u32[]{:S(2)}, u32[]{:S(2)}) collective-permute-start(bf16[128,2560]{1,0:T(8,128)(2,1)S(1)} %slice.213), channel_id=1, source_target_pairs={{0,1},{1,0},{2,3},{3,2},{4,5},{5,4},{6,7},{7,6},{8,9},{9,8},{10,11... | collective-permute-start | bytes 1966088 | tf_op jit(solution)/shard_map/ppermute | solution.py:10
  103.8 10.6 %collective-permute-start.5 = (bf16[64,2560]{1,0:T(8,128)(2,1)S(1)}, bf16[64,2560]{1,0:T(8,128)(2,1)S(1)}, u32[]{:S(2)}, u32[]{:S(2)}) collective-permute-start(bf16[64,2560]{1,0:T(8,128)(2,1)S(1)} %slice.182), channel_id=1, source_target_pairs={{0,2},{1,3},{2,0},{3,1},{4,6},{5,7},{6,4},{7,5},{8,10},{9,11},{10,... | collective-permute-start | bytes 983048 | tf_op jit(solution)/shard_map/ppermute | solution.py:10
  106.8 14.6 %collective-permute-start.13 = (bf16[64,2560]{1,0:T(8,128)(2,1)S(1)}, bf16[64,2560]{1,0:T(8,128)(2,1)S(1)}, u32[]{:S(2)}, u32[]{:S(2)}) collective-permute-start(bf16[64,2560]{1,0:T(8,128)(2,1)S(1)} %slice.193), channel_id=1, source_target_pairs={{0,2},{1,3},{2,0},{3,1},{4,6},{5,7},{6,4},{7,5},{8,10},{9,11},{10,... | collective-permute-start | bytes 983048 | tf_op jit(solution)/shard_map/ppermute | solution.py:10
  108.5 19.9 %collective-permute-start.21 = (bf16[64,2560]{1,0:T(8,128)(2,1)S(1)}, bf16[64,2560]{1,0:T(8,128)(2,1)S(1)}, u32[]{:S(2)}, u32[]{:S(2)}) collective-permute-start(bf16[64,2560]{1,0:T(8,128)(2,1)S(1)} %slice.204), channel_id=1, source_target_pairs={{0,2},{1,3},{2,0},{3,1},{4,6},{5,7},{6,4},{7,5},{8,10},{9,11},{10,... | collective-permute-start | bytes 983048 | tf_op jit(solution)/shard_map/ppermute | solution.py:10
  110.4 24.4 %collective-permute-start.29 = (bf16[64,2560]{1,0:T(8,128)(2,1)S(1)}, bf16[64,2560]{1,0:T(8,128)(2,1)S(1)}, u32[]{:S(2)}, u32[]{:S(2)}) collective-permute-start(bf16[64,2560]{1,0:T(8,128)(2,1)S(1)} %slice.215), channel_id=1, source_target_pairs={{0,2},{1,3},{2,0},{3,1},{4,6},{5,7},{6,4},{7,5},{8,10},{9,11},{10,... | collective-permute-start | bytes 983048 | tf_op jit(solution)/shard_map/ppermute | solution.py:10
  114.5 20.6 %collective-permute-start.6 = (bf16[32,2560]{1,0:T(8,128)(2,1)S(1)}, bf16[32,2560]{1,0:T(8,128)(2,1)S(1)}, u32[]{:S(2)}, u32[]{:S(2)}) collective-permute-start(bf16[32,2560]{1,0:T(8,128)(2,1)S(1)} %slice.184), channel_id=1, source_target_pairs={{0,4},{1,5},{2,6},{3,7},{4,0},{5,1},{6,2},{7,3},{8,12},{9,13},{10,... | collective-permute-start | bytes 491528 | tf_op jit(solution)/shard_map/ppermute | solution.py:10
  121.5 17.8 %collective-permute-start.14 = (bf16[32,2560]{1,0:T(8,128)(2,1)S(1)}, bf16[32,2560]{1,0:T(8,128)(2,1)S(1)}, u32[]{:S(2)}, u32[]{:S(2)}) collective-permute-start(bf16[32,2560]{1,0:T(8,128)(2,1)S(1)} %slice.195), channel_id=1, source_target_pairs={{0,4},{1,5},{2,6},{3,7},{4,0},{5,1},{6,2},{7,3},{8,12},{9,13},{10,... | collective-permute-start | bytes 491528 | tf_op jit(solution)/shard_map/ppermute | solution.py:10
  128.5 10.9 %collective-permute-start.22 = (bf16[32,2560]{1,0:T(8,128)(2,1)S(1)}, bf16[32,2560]{1,0:T(8,128)(2,1)S(1)}, u32[]{:S(2)}, u32[]{:S(2)}) collective-permute-start(bf16[32,2560]{1,0:T(8,128)(2,1)S(1)} %slice.206), channel_id=1, source_target_pairs={{0,4},{1,5},{2,6},{3,7},{4,0},{5,1},{6,2},{7,3},{8,12},{9,13},{10,... | collective-permute-start | bytes 491528 | tf_op jit(solution)/shard_map/ppermute | solution.py:10
  135.0 7.8 %collective-permute-start.30 = (bf16[32,2560]{1,0:T(8,128)(2,1)S(1)}, bf16[32,2560]{1,0:T(8,128)(2,1)S(1)}, u32[]{:S(2)}, u32[]{:S(2)}) collective-permute-start(bf16[32,2560]{1,0:T(8,128)(2,1)S(1)} %slice.217), channel_id=1, source_target_pairs={{0,4},{1,5},{2,6},{3,7},{4,0},{5,1},{6,2},{7,3},{8,12},{9,13},{10,... | collective-permute-start | bytes 491528 | tf_op jit(solution)/shard_map/ppermute | solution.py:10
  135.1 9.2 %collective-permute-start.7 = (bf16[16,2560]{1,0:T(8,128)(2,1)S(1)}, bf16[16,2560]{1,0:T(8,128)(2,1)S(1)}, u32[]{:S(2)}, u32[]{:S(2)}) collective-permute-start(bf16[16,2560]{1,0:T(8,128)(2,1)S(1)} %slice.186), channel_id=1, source_target_pairs={{0,8},{1,9},{2,10},{3,11},{4,12},{5,13},{6,14},{7,15},{8,0},{9,1},... | collective-permute-start | bytes 245768 | tf_op jit(solution)/shard_map/ppermute | solution.py:10
  139.3 12.1 %collective-permute-start.15 = (bf16[16,2560]{1,0:T(8,128)(2,1)S(1)}, bf16[16,2560]{1,0:T(8,128)(2,1)S(1)}, u32[]{:S(2)}, u32[]{:S(2)}) collective-permute-start(bf16[16,2560]{1,0:T(8,128)(2,1)S(1)} %slice.197), channel_id=1, source_target_pairs={{0,8},{1,9},{2,10},{3,11},{4,12},{5,13},{6,14},{7,15},{8,0},{9,1},... | collective-permute-start | bytes 245768 | tf_op jit(solution)/shard_map/ppermute | solution.py:10
  139.5 13.6 %collective-permute-start.23 = (bf16[16,2560]{1,0:T(8,128)(2,1)S(1)}, bf16[16,2560]{1,0:T(8,128)(2,1)S(1)}, u32[]{:S(2)}, u32[]{:S(2)}) collective-permute-start(bf16[16,2560]{1,0:T(8,128)(2,1)S(1)} %slice.208), channel_id=1, source_target_pairs={{0,8},{1,9},{2,10},{3,11},{4,12},{5,13},{6,14},{7,15},{8,0},{9,1},... | collective-permute-start | bytes 245768 | tf_op jit(solution)/shard_map/ppermute | solution.py:10
  142.8 11.2 %collective-permute-start.31 = (bf16[16,2560]{1,0:T(8,128)(2,1)S(1)}, bf16[16,2560]{1,0:T(8,128)(2,1)S(1)}, u32[]{:S(2)}, u32[]{:S(2)}) collective-permute-start(bf16[16,2560]{1,0:T(8,128)(2,1)S(1)} %slice.219), channel_id=1, source_target_pairs={{0,8},{1,9},{2,10},{3,11},{4,12},{5,13},{6,14},{7,15},{8,0},{9,1},... | collective-permute-start | bytes 245768 | tf_op jit(solution)/shard_map/ppermute | solution.py:10
  (11 other events, 83.0 us)

commit v2 on v1

v2 whole, which is shorter than its diff:
```python
import jax
import jax.numpy as jnp
from jax import lax
from jax.experimental import pallas as pl
from jax.experimental.pallas import tpu as pltpu
from jax.sharding import PartitionSpec as P

PIECES = 4
LANES = 128
BLOCK = 256


def swap(array, axis_size, bit):
    return lax.ppermute(array, "expert", [(i, i ^ bit) for i in range(axis_size)])


def dense_weights(route_ids, route_weights, experts):
    normalized = route_weights / jnp.sum(route_weights, axis=1, keepdims=True)
    labels = lax.broadcasted_iota(jnp.int32, (*route_ids.shape, experts), 2)
    chosen = jnp.where(route_ids[:, :, None] == labels, normalized[:, :, None], 0.0)
    return jnp.sum(chosen, axis=1)


def with_weights(rows, weights):
    high = weights.astype(jnp.bfloat16)
    low = (weights - high.astype(jnp.float32)).astype(jnp.bfloat16)
    fill = -2 * weights.shape[1] % LANES
    return jnp.concatenate(
        [rows, high, low, jnp.zeros((rows.shape[0], fill), jnp.bfloat16)], axis=1
    )


def expert_kernel(experts, own_ref, near_ref, far_ref, gate_ref, up_ref, down_ref, keep_ref, send_ref):
    width = gate_ref.shape[0]
    half = near_ref.shape[0]
    own = own_ref[0]
    block = min(BLOCK // 2, half)

    def step(index, carry):
        part = pl.ds(pl.multiple_of(index * block, block), block)
        rows = jnp.concatenate([near_ref[part, :], far_ref[part, :]], axis=0)
        tokens = rows[:, :width]
        spread = rows[:, width:].astype(jnp.float32)
        lane = lax.broadcasted_iota(jnp.int32, spread.shape, 1)
        mine = (lane == own) | (lane == own + experts)
        weight = jnp.sum(jnp.where(mine, spread, 0.0), axis=1, keepdims=True)
        gate = jnp.dot(tokens, gate_ref[...], preferred_element_type=jnp.float32)
        up = jnp.dot(tokens, up_ref[...], preferred_element_type=jnp.float32)
        hidden = (gate / (1.0 + jnp.exp(-gate)) * up).astype(jnp.bfloat16)
        result = jnp.dot(hidden, down_ref[...], preferred_element_type=jnp.float32)
        scaled = (result * weight).astype(jnp.bfloat16)
        keep_ref[part, :] = scaled[:block]
        send_ref[part, :] = scaled[block:]
        return carry

    if half == block:
        step(0, 0)
    else:
        lax.fori_loop(0, half // block, step, 0)


def expert_rows(near, far, experts, gate_proj, up_proj, down_proj):
    width, middle = gate_proj.shape
    half = near.shape[0]
    vmem = pl.BlockSpec(memory_space=pltpu.VMEM)
    shape = jax.ShapeDtypeStruct((half, width), jnp.bfloat16)
    size = 2 * half
    return pl.pallas_call(
        lambda *refs: expert_kernel(experts, *refs),
        out_shape=(shape, shape),
        in_specs=[pl.BlockSpec(memory_space=pltpu.SMEM)] + [vmem] * 5,
        out_specs=(vmem, vmem),
        compiler_params=pltpu.CompilerParams(vmem_limit_bytes=40 * 1024 * 1024),
        cost_estimate=pl.CostEstimate(
            flops=6 * size * width * middle,
            bytes_accessed=4 * size * width + 6 * width * middle,
            transcendentals=size * middle,
        ),
    )(lax.axis_index("expert").reshape(1), near, far, gate_proj, up_proj, down_proj)


def add_halves(kept, arrived):
    half = kept.shape[0] // 2
    if half == 0:
        return None

    def total(first, second):
        return (first.astype(jnp.float32) + second.astype(jnp.float32)).astype(jnp.bfloat16)

    return total(kept[:half], arrived[:half]), total(kept[half:], arrived[half:])


def on_device(hidden_states, route_ids, route_weights, gate_proj, up_proj, down_proj):
    step_count, row_count, feature_width = hidden_states.shape
    axis_size = lax.axis_size("expert")
    experts = axis_size * gate_proj.shape[0]
    total = step_count * row_count
    share = total // PIECES
    bits = [1 << i for i in reversed(range(axis_size.bit_length() - 1))]
    weights = dense_weights(
        route_ids.reshape(total, -1), route_weights.reshape(total, -1), experts
    )
    rows = with_weights(hidden_states.reshape(total, feature_width), weights)
    outputs = []
    for piece in range(PIECES):
        near = rows[piece * share : (piece + 1) * share]
        for bit in bits[:-1]:
            near = jnp.concatenate([near, swap(near, axis_size, bit)], axis=0)
        far = swap(near, axis_size, bits[-1])
        keep, send = expert_rows(near, far, experts, gate_proj[0], up_proj[0], down_proj[0])
        for bit in reversed(bits[1:]):
            keep, send = add_halves(keep, swap(send, axis_size, bit))
        arrived = swap(send, axis_size, bits[0])
        outputs.append((keep.astype(jnp.float32) + arrived.astype(jnp.float32)).astype(jnp.bfloat16))
    return jnp.concatenate(outputs, axis=0).reshape(hidden_states.shape)


def solution(mesh):
    placed = (
        P(None, ("groups", "expert"), None),
        P(None, ("groups", "expert"), None),
        P(None, ("groups", "expert"), None),
        P("expert", None, None),
        P("expert", None, None),
        P("expert", None, None),
    )
    return jax.shard_map(
        on_device,
        mesh=mesh,
        in_specs=placed,
        out_specs=P(None, ("groups", "expert"), None),
        check_vma=False,
    )
```

time: 155 us -> 128 us (0.83)
  matrix products: 35.6 us -> 0 us
  Pallas kernels: 0 us -> 13.1 us
  local copies, waits for them, and re-layouts: 8.65 us -> 5.05 us
  other arithmetic: 6.49 us -> 3.01 us
  waiting for transfers between devices: 72.8 us -> 75.5 us
    dot_general x8 -> x0, matrix products: 35.6 us -> none  [the longest x4 27.3 us: expert_rows(): result = jnp.dot(hidden, down_proj, preferred_element_type=jnp.float32)]
    pallas_call x0 -> x4, Pallas kernels: none -> 13.1 us  [expert_rows(): pl.pallas_call(lambda *refs: expert_kernel(experts, *refs), out_shape=(sh...]
    convert_element_type x16 -> x17, other arithmetic: 4.43 us -> 1.14 us  [the longest x12 1 us: total(): (first.astype(jnp.float32) + second.astype(jnp.float32)).astype(jnp.bfloa...]
    slice x17 -> x1, local copies, waits for them, and re-layouts: 2.95 us -> 0.03 us  [on_device(): near = rows[piece * share:(piece + 1) * share]]
    ppermute x32, waiting for transfers between devices: 72.8 us -> 75.5 us  [swap(): lax.ppermute(array, 'expert', [(i, i ^ bit) for i in range(axis_size)])]
    unnamed x36 -> x10, local copies, waits for them, and re-layouts: 3.82 us -> 3.52 us
  transfers between devices with their start and end apart: 32 -> 32, of which waited for: 20 -> 19; matrix products, arithmetic and copies ran while one was open for 21% -> 1% of each run, Pallas kernels for 0% -> 10%
where the time goes in v2:
time: 128 us; the launch traced here: 127 us
  waiting for transfers between devices  75.5 us (59%)
  starting transfers between devices  30.2 us (24%)
  Pallas kernels  13.1 us (10%)
  local copies, waits for them, and re-layouts  5.05 us (4%)
  other arithmetic  3.01 us (2%)
    ppermute x32, waiting for transfers between devices, swap(): lax.ppermute(array, 'expert', [(i, i ^ bit) for i in range(axis_size)])  75.5 us
    ppermute x32, starting transfers between devices, swap(): lax.ppermute(array, 'expert', [(i, i ^ bit) for i in range(axis_size)])  30.2 us
    pallas_call x4, Pallas kernels, expert_rows(): pl.pallas_call(lambda *refs: expert_kernel(experts, *refs), out_shape=(sh...  13.1 us
    unnamed x10, local copies, waits for them, and re-layouts  3.52 us
  transfers between devices with their start and end apart: 32, of which 19 were waited for; matrix products, arithmetic and copies ran while one was open for 1% of the time, Pallas kernels for 10%

profile of v2, /device:TPU:0, one launch (start us, length us, event | category | flops | bytes accessed | tf_op | source)
XLA Modules:
  0.0 127.2 jit_solution(1954628150037369172)
XLA Ops:
  2.6 1.1 concatenate.50
  3.7 4.1 %collective-permute-start = (bf16[16,2688]{1,0:T(8,128)(2,1)S(1)}, bf16[16,2688]{1,0:T(8,128)(2,1)S(1)}, u32[]{:S(2)}, u32[]{:S(2)}) collective-permute-start(bf16[16,2688]{1,0:T(8,128)(2,1)S(1)} %get-tuple-element.37), channel_id=1, source_target_pairs={{0,8},{1,9},{2,10},{3,11},{4,12},{5,13},{6,14},{7,15},{8,0},{9,1},... | collective-permute-start | bytes 258056 | tf_op jit(solution)/shard_map/ppermute | solution.py:14
  7.9 2.8 %collective-permute-start.16 = (bf16[16,2688]{1,0:T(8,128)(2,1)S(1)}, bf16[16,2688]{1,0:T(8,128)(2,1)S(1)}, u32[]{:S(2)}, u32[]{:S(2)}) collective-permute-start(bf16[16,2688]{1,0:T(8,128)(2,1)S(1)} %get-tuple-element.39), channel_id=1, source_target_pairs={{0,8},{1,9},{2,10},{3,11},{4,12},{5,13},{6,14},{7,15},{8,0},{9,1},... | collective-permute-start | bytes 258056 | tf_op jit(solution)/shard_map/ppermute | solution.py:14
  10.8 7.4 %collective-permute-done = bf16[16,2688]{1,0:T(8,128)(2,1)S(1)} collective-permute-done((bf16[16,2688]{1,0:T(8,128)(2,1)S(1)}, bf16[16,2688]{1,0:T(8,128)(2,1)S(1)}, u32[]{:S(2)}, u32[]{:S(2)}) %collective-permute-start) | collective-permute-done | bytes 86048 | tf_op jit(solution)/shard_map/ppermute | solution.py:14
  18.6 1.5 %collective-permute-done.8 = bf16[16,2688]{1,0:T(8,128)(2,1)S(1)} collective-permute-done((bf16[16,2688]{1,0:T(8,128)(2,1)S(1)}, bf16[16,2688]{1,0:T(8,128)(2,1)S(1)}, u32[]{:S(2)}, u32[]{:S(2)}) %collective-permute-start.8) | collective-permute-done | bytes 86048 | tf_op jit(solution)/shard_map/ppermute | solution.py:14
  20.5 1.5 %collective-permute-done.16 = bf16[16,2688]{1,0:T(8,128)(2,1)S(1)} collective-permute-done((bf16[16,2688]{1,0:T(8,128)(2,1)S(1)}, bf16[16,2688]{1,0:T(8,128)(2,1)S(1)}, u32[]{:S(2)}, u32[]{:S(2)}) %collective-permute-start.16) | collective-permute-done | bytes 86048 | tf_op jit(solution)/shard_map/ppermute | solution.py:14
  24.2 2.8 %collective-permute-done.1 = bf16[32,2688]{1,0:T(8,128)(2,1)S(1)} collective-permute-done((bf16[32,2688]{1,0:T(8,128)(2,1)S(1)}, bf16[32,2688]{1,0:T(8,128)(2,1)S(1)}, u32[]{:S(2)}, u32[]{:S(2)}) %collective-permute-start.1) | collective-permute-done | bytes 172064 | tf_op jit(solution)/shard_map/ppermute | solution.py:14
  27.1 1.7 %collective-permute-start.2 = (bf16[64,2688]{1,0:T(8,128)(2,1)S(1)}, bf16[64,2688]{1,0:T(8,128)(2,1)S(1)}, u32[]{:S(2)}, u32[]{:S(2)}) collective-permute-start(bf16[64,2688]{1,0:T(8,128)(2,1)S(1)} %pad_maximum_fusion.4), channel_id=1, source_target_pairs={{0,2},{1,3},{2,0},{3,1},{4,6},{5,7},{6,4},{7,5},{8,10},{9,11},{10,... | collective-permute-start | bytes 1032200 | tf_op jit(solution)/shard_map/ppermute | solution.py:14
  28.8 1.9 %collective-permute-done.9 = bf16[32,2688]{1,0:T(8,128)(2,1)S(1)} collective-permute-done((bf16[32,2688]{1,0:T(8,128)(2,1)S(1)}, bf16[32,2688]{1,0:T(8,128)(2,1)S(1)}, u32[]{:S(2)}, u32[]{:S(2)}) %collective-permute-start.9) | collective-permute-done | bytes 172064 | tf_op jit(solution)/shard_map/ppermute | solution.py:14
  30.8 1.7 %collective-permute-start.10 = (bf16[64,2688]{1,0:T(8,128)(2,1)S(1)}, bf16[64,2688]{1,0:T(8,128)(2,1)S(1)}, u32[]{:S(2)}, u32[]{:S(2)}) collective-permute-start(bf16[64,2688]{1,0:T(8,128)(2,1)S(1)} %pad_maximum_fusion.5), channel_id=1, source_target_pairs={{0,2},{1,3},{2,0},{3,1},{4,6},{5,7},{6,4},{7,5},{8,10},{9,11},{10,... | collective-permute-start | bytes 1032200 | tf_op jit(solution)/shard_map/ppermute | solution.py:14
  32.5 1.9 %collective-permute-done.17 = bf16[32,2688]{1,0:T(8,128)(2,1)S(1)} collective-permute-done((bf16[32,2688]{1,0:T(8,128)(2,1)S(1)}, bf16[32,2688]{1,0:T(8,128)(2,1)S(1)}, u32[]{:S(2)}, u32[]{:S(2)}) %collective-permute-start.17) | collective-permute-done | bytes 172064 | tf_op jit(solution)/shard_map/ppermute | solution.py:14
  34.4 1.7 %collective-permute-start.18 = (bf16[64,2688]{1,0:T(8,128)(2,1)S(1)}, bf16[64,2688]{1,0:T(8,128)(2,1)S(1)}, u32[]{:S(2)}, u32[]{:S(2)}) collective-permute-start(bf16[64,2688]{1,0:T(8,128)(2,1)S(1)} %pad_maximum_fusion.6), channel_id=1, source_target_pairs={{0,2},{1,3},{2,0},{3,1},{4,6},{5,7},{6,4},{7,5},{8,10},{9,11},{10,... | collective-permute-start | bytes 1032200 | tf_op jit(solution)/shard_map/ppermute | solution.py:14
  36.2 1.8 %collective-permute-done.25 = bf16[32,2688]{1,0:T(8,128)(2,1)S(1)} collective-permute-done((bf16[32,2688]{1,0:T(8,128)(2,1)S(1)}, bf16[32,2688]{1,0:T(8,128)(2,1)S(1)}, u32[]{:S(2)}, u32[]{:S(2)}) %collective-permute-start.25) | collective-permute-done | bytes 172064 | tf_op jit(solution)/shard_map/ppermute | solution.py:14
  38.0 1.7 %collective-permute-start.26 = (bf16[64,2688]{1,0:T(8,128)(2,1)S(1)}, bf16[64,2688]{1,0:T(8,128)(2,1)S(1)}, u32[]{:S(2)}, u32[]{:S(2)}) collective-permute-start(bf16[64,2688]{1,0:T(8,128)(2,1)S(1)} %pad_maximum_fusion.7), channel_id=1, source_target_pairs={{0,2},{1,3},{2,0},{3,1},{4,6},{5,7},{6,4},{7,5},{8,10},{9,11},{10,... | collective-permute-start | bytes 1032200 | tf_op jit(solution)/shard_map/ppermute | solution.py:14
  39.9 5.6 %collective-permute-done.10 = bf16[64,2688]{1,0:T(8,128)(2,1)S(1)} collective-permute-done((bf16[64,2688]{1,0:T(8,128)(2,1)S(1)}, bf16[64,2688]{1,0:T(8,128)(2,1)S(1)}, u32[]{:S(2)}, u32[]{:S(2)}) %collective-permute-start.10) | collective-permute-done | bytes 344096 | tf_op jit(solution)/shard_map/ppermute | solution.py:14
  45.6 7.2 %collective-permute-done.18 = bf16[64,2688]{1,0:T(8,128)(2,1)S(1)} collective-permute-done((bf16[64,2688]{1,0:T(8,128)(2,1)S(1)}, bf16[64,2688]{1,0:T(8,128)(2,1)S(1)}, u32[]{:S(2)}, u32[]{:S(2)}) %collective-permute-start.18) | collective-permute-done | bytes 344096 | tf_op jit(solution)/shard_map/ppermute | solution.py:14
  53.0 6.2 %collective-permute-done.26 = bf16[64,2688]{1,0:T(8,128)(2,1)S(1)} collective-permute-done((bf16[64,2688]{1,0:T(8,128)(2,1)S(1)}, bf16[64,2688]{1,0:T(8,128)(2,1)S(1)}, u32[]{:S(2)}, u32[]{:S(2)}) %collective-permute-start.26) | collective-permute-done | bytes 344096 | tf_op jit(solution)/shard_map/ppermute | solution.py:14
  59.3 2.1 %copy-done.2 = bf16[1,768,2560]{2,1,0:T(8,128)(2,1)S(1)} copy-done((bf16[1,768,2560]{2,1,0:T(8,128)(2,1)S(1)}, bf16[1,768,2560]{2,1,0:T(8,128)(2,1)}, u32[]{:S(2)}) %copy-start.2) | copy-done | bytes 3932184
  61.4 3.3 %shard_map.64 = (bf16[128,2560]{1,0:T(8,128)(2,1)S(1)}, bf16[128,2560]{1,0:T(8,128)(2,1)S(1)}) custom-call(s32[1]{0:T(128)} %bitcast.refs_0_, bf16[128,2688]{1,0:T(8,128)(2,1)S(1)} %pad_maximum_fusion.refs_1_, bf16[128,2688]{1,0:T(8,128)(2,1)S(1)} %collective-permute-done.3.refs_2_, bf16[2560,768]{1,0:T(8,128)(2,1)S(1)} %bitcast.10, ...), custom_call_target="tpu_custom_call" | custom-call | flops 3019898880 | bytes 14417920 | tf_op jit(solution)/shard_map/pallas_call | solution.py:68
  65.3 3.3 %shard_map.65 = (bf16[128,2560]{1,0:T(8,128)(2,1)S(1)}, bf16[128,2560]{1,0:T(8,128)(2,1)S(1)}) custom-call(s32[1]{0:T(128)} %bitcast.refs_0_, bf16[128,2688]{1,0:T(8,128)(2,1)S(1)} %pad_maximum_fusion.1.refs_1_, bf16[128,2688]{1,0:T(8,128)(2,1)S(1)} %collective-permute-done.11.refs_2_, bf16[2560,768]{1,0:T(8,128)(2,1)S(1)} %bitcast.11, ...), custom_call_target="tpu_custom_call" | custom-call | flops 3019898880 | bytes 14417920 | tf_op jit(solution)/shard_map/pallas_call | solution.py:68
  68.6 3.3 %shard_map.66 = (bf16[128,2560]{1,0:T(8,128)(2,1)S(1)}, bf16[128,2560]{1,0:T(8,128)(2,1)S(1)}) custom-call(s32[1]{0:T(128)} %bitcast.refs_0_, bf16[128,2688]{1,0:T(8,128)(2,1)S(1)} %pad_maximum_fusion.2.refs_1_, bf16[128,2688]{1,0:T(8,128)(2,1)S(1)} %collective-permute-done.19.refs_2_, bf16[2560,768]{1,0:T(8,128)(2,1)S(1)} %bitcast.12, ...), custom_call_target="tpu_custom_call" | custom-call | flops 3019898880 | bytes 14417920 | tf_op jit(solution)/shard_map/pallas_call | solution.py:68
  72.5 3.3 %shard_map.67 = (bf16[128,2560]{1,0:T(8,128)(2,1)S(1)}, bf16[128,2560]{1,0:T(8,128)(2,1)S(1)}) custom-call(s32[1]{0:T(128)} %bitcast.refs_0_, bf16[128,2688]{1,0:T(8,128)(2,1)S(1)} %pad_maximum_fusion.3.refs_1_, bf16[128,2688]{1,0:T(8,128)(2,1)S(1)} %collective-permute-done.27.refs_2_, bf16[2560,768]{1,0:T(8,128)(2,1)S(1)} %bitcast.13, ...), custom_call_target="tpu_custom_call" | custom-call | flops 3019898880 | bytes 14417920 | tf_op jit(solution)/shard_map/pallas_call | solution.py:68
  76.0 1.7 %collective-permute-start.5 = (bf16[64,2560]{1,0:T(8,128)(2,1)S(1)}, bf16[64,2560]{1,0:T(8,128)(2,1)S(1)}, u32[]{:S(2)}, u32[]{:S(2)}) collective-permute-start(bf16[64,2560]{1,0:T(8,128)(2,1)S(1)} %get-tuple-element.22), channel_id=1, source_target_pairs={{0,2},{1,3},{2,0},{3,1},{4,6},{5,7},{6,4},{7,5},{8,10},{9,11},{10,... | collective-permute-start | bytes 983048 | tf_op jit(solution)/shard_map/ppermute | solution.py:14
  78.5 1.7 %collective-permute-start.21 = (bf16[64,2560]{1,0:T(8,128)(2,1)S(1)}, bf16[64,2560]{1,0:T(8,128)(2,1)S(1)}, u32[]{:S(2)}, u32[]{:S(2)}) collective-permute-start(bf16[64,2560]{1,0:T(8,128)(2,1)S(1)} %get-tuple-element.26), channel_id=1, source_target_pairs={{0,2},{1,3},{2,0},{3,1},{4,6},{5,7},{6,4},{7,5},{8,10},{9,11},{10,... | collective-permute-start | bytes 983048 | tf_op jit(solution)/shard_map/ppermute | solution.py:14
  80.8 5.8 %collective-permute-done.5 = bf16[64,2560]{1,0:T(8,128)(2,1)S(1)} collective-permute-done((bf16[64,2560]{1,0:T(8,128)(2,1)S(1)}, bf16[64,2560]{1,0:T(8,128)(2,1)S(1)}, u32[]{:S(2)}, u32[]{:S(2)}) %collective-permute-start.5) | collective-permute-done | bytes 327712 | tf_op jit(solution)/shard_map/ppermute | solution.py:14
  86.7 6.9 %collective-permute-done.13 = bf16[64,2560]{1,0:T(8,128)(2,1)S(1)} collective-permute-done((bf16[64,2560]{1,0:T(8,128)(2,1)S(1)}, bf16[64,2560]{1,0:T(8,128)(2,1)S(1)}, u32[]{:S(2)}, u32[]{:S(2)}) %collective-permute-start.13) | collective-permute-done | bytes 327712 | tf_op jit(solution)/shard_map/ppermute | solution.py:14
  93.8 6.9 %collective-permute-done.21 = bf16[64,2560]{1,0:T(8,128)(2,1)S(1)} collective-permute-done((bf16[64,2560]{1,0:T(8,128)(2,1)S(1)}, bf16[64,2560]{1,0:T(8,128)(2,1)S(1)}, u32[]{:S(2)}, u32[]{:S(2)}) %collective-permute-start.21) | collective-permute-done | bytes 327712 | tf_op jit(solution)/shard_map/ppermute | solution.py:14
  100.8 6.4 %collective-permute-done.29 = bf16[64,2560]{1,0:T(8,128)(2,1)S(1)} collective-permute-done((bf16[64,2560]{1,0:T(8,128)(2,1)S(1)}, bf16[64,2560]{1,0:T(8,128)(2,1)S(1)}, u32[]{:S(2)}, u32[]{:S(2)}) %collective-permute-start.29) | collective-permute-done | bytes 327712 | tf_op jit(solution)/shard_map/ppermute | solution.py:14
  107.4 4.1 %collective-permute-start.7 = (bf16[16,2560]{1,0:T(8,128)(2,1)S(1)}, bf16[16,2560]{1,0:T(8,128)(2,1)S(1)}, u32[]{:S(2)}, u32[]{:S(2)}) collective-permute-start(bf16[16,2560]{1,0:T(8,128)(2,1)S(1)} %add_convert_fusion.26), channel_id=1, source_target_pairs={{0,8},{1,9},{2,10},{3,11},{4,12},{5,13},{6,14},{7,15},{8,0},{9,1},... | collective-permute-start | bytes 245768 | tf_op jit(solution)/shard_map/ppermute | solution.py:14
  111.7 3.0 %collective-permute-start.23 = (bf16[16,2560]{1,0:T(8,128)(2,1)S(1)}, bf16[16,2560]{1,0:T(8,128)(2,1)S(1)}, u32[]{:S(2)}, u32[]{:S(2)}) collective-permute-start(bf16[16,2560]{1,0:T(8,128)(2,1)S(1)} %add_convert_fusion.20), channel_id=1, source_target_pairs={{0,8},{1,9},{2,10},{3,11},{4,12},{5,13},{6,14},{7,15},{8,0},{9,1},... | collective-permute-start | bytes 245768 | tf_op jit(solution)/shard_map/ppermute | solution.py:14
  116.7 7.2 %collective-permute-done.15 = bf16[16,2560]{1,0:T(8,128)(2,1)S(1)} collective-permute-done((bf16[16,2560]{1,0:T(8,128)(2,1)S(1)}, bf16[16,2560]{1,0:T(8,128)(2,1)S(1)}, u32[]{:S(2)}, u32[]{:S(2)}) %collective-permute-start.15) | collective-permute-done | bytes 81952 | tf_op jit(solution)/shard_map/ppermute | solution.py:14
  124.0 1.6 %collective-permute-done.23 = bf16[16,2560]{1,0:T(8,128)(2,1)S(1)} collective-permute-done((bf16[16,2560]{1,0:T(8,128)(2,1)S(1)}, bf16[16,2560]{1,0:T(8,128)(2,1)S(1)}, u32[]{:S(2)}, u32[]{:S(2)}) %collective-permute-start.23) | collective-permute-done | bytes 81952 | tf_op jit(solution)/shard_map/ppermute | solution.py:14
  (88 shorter events, 13.5 us)
Async XLA Ops:
  3.7 14.5 %collective-permute-start = (bf16[16,2688]{1,0:T(8,128)(2,1)S(1)}, bf16[16,2688]{1,0:T(8,128)(2,1)S(1)}, u32[]{:S(2)}, u32[]{:S(2)}) collective-permute-start(bf16[16,2688]{1,0:T(8,128)(2,1)S(1)} %get-tuple-element.37), channel_id=1, source_target_pairs={{0,8},{1,9},{2,10},{3,11},{4,12},{5,13},{6,14},{7,15},{8,0},{9,1},... | collective-permute-start | bytes 258056 | tf_op jit(solution)/shard_map/ppermute | solution.py:14
  7.8 12.3 %collective-permute-start.8 = (bf16[16,2688]{1,0:T(8,128)(2,1)S(1)}, bf16[16,2688]{1,0:T(8,128)(2,1)S(1)}, u32[]{:S(2)}, u32[]{:S(2)}) collective-permute-start(bf16[16,2688]{1,0:T(8,128)(2,1)S(1)} %get-tuple-element.40), channel_id=1, source_target_pairs={{0,8},{1,9},{2,10},{3,11},{4,12},{5,13},{6,14},{7,15},{8,0},{9,1},... | collective-permute-start | bytes 258056 | tf_op jit(solution)/shard_map/ppermute | solution.py:14
  7.9 14.1 %collective-permute-start.16 = (bf16[16,2688]{1,0:T(8,128)(2,1)S(1)}, bf16[16,2688]{1,0:T(8,128)(2,1)S(1)}, u32[]{:S(2)}, u32[]{:S(2)}) collective-permute-start(bf16[16,2688]{1,0:T(8,128)(2,1)S(1)} %get-tuple-element.39), channel_id=1, source_target_pairs={{0,8},{1,9},{2,10},{3,11},{4,12},{5,13},{6,14},{7,15},{8,0},{9,1},... | collective-permute-start | bytes 258056 | tf_op jit(solution)/shard_map/ppermute | solution.py:14
  10.7 12.6 %collective-permute-start.24 = (bf16[16,2688]{1,0:T(8,128)(2,1)S(1)}, bf16[16,2688]{1,0:T(8,128)(2,1)S(1)}, u32[]{:S(2)}, u32[]{:S(2)}) collective-permute-start(bf16[16,2688]{1,0:T(8,128)(2,1)S(1)} %get-tuple-element.38), channel_id=1, source_target_pairs={{0,8},{1,9},{2,10},{3,11},{4,12},{5,13},{6,14},{7,15},{8,0},{9,1},... | collective-permute-start | bytes 258056 | tf_op jit(solution)/shard_map/ppermute | solution.py:14
  18.2 8.8 %collective-permute-start.1 = (bf16[32,2688]{1,0:T(8,128)(2,1)S(1)}, bf16[32,2688]{1,0:T(8,128)(2,1)S(1)}, u32[]{:S(2)}, u32[]{:S(2)}) collective-permute-start(bf16[32,2688]{1,0:T(8,128)(2,1)S(1)} %pad_maximum_fusion.9), channel_id=1, source_target_pairs={{0,4},{1,5},{2,6},{3,7},{4,0},{5,1},{6,2},{7,3},{8,12},{9,13},{10,... | collective-permute-start | bytes 516104 | tf_op jit(solution)/shard_map/ppermute | solution.py:14
  20.2 10.6 %collective-permute-start.9 = (bf16[32,2688]{1,0:T(8,128)(2,1)S(1)}, bf16[32,2688]{1,0:T(8,128)(2,1)S(1)}, u32[]{:S(2)}, u32[]{:S(2)}) collective-permute-start(bf16[32,2688]{1,0:T(8,128)(2,1)S(1)} %pad_maximum_fusion.10), channel_id=1, source_target_pairs={{0,4},{1,5},{2,6},{3,7},{4,0},{5,1},{6,2},{7,3},{8,12},{9,13},{10,... | collective-permute-start | bytes 516104 | tf_op jit(solution)/shard_map/ppermute | solution.py:14
  22.0 12.4 %collective-permute-start.17 = (bf16[32,2688]{1,0:T(8,128)(2,1)S(1)}, bf16[32,2688]{1,0:T(8,128)(2,1)S(1)}, u32[]{:S(2)}, u32[]{:S(2)}) collective-permute-start(bf16[32,2688]{1,0:T(8,128)(2,1)S(1)} %pad_maximum_fusion.11), channel_id=1, source_target_pairs={{0,4},{1,5},{2,6},{3,7},{4,0},{5,1},{6,2},{7,3},{8,12},{9,13},{10,... | collective-permute-start | bytes 516104 | tf_op jit(solution)/shard_map/ppermute | solution.py:14
  23.4 14.6 %collective-permute-start.25 = (bf16[32,2688]{1,0:T(8,128)(2,1)S(1)}, bf16[32,2688]{1,0:T(8,128)(2,1)S(1)}, u32[]{:S(2)}, u32[]{:S(2)}) collective-permute-start(bf16[32,2688]{1,0:T(8,128)(2,1)S(1)} %pad_maximum_fusion.12), channel_id=1, source_target_pairs={{0,4},{1,5},{2,6},{3,7},{4,0},{5,1},{6,2},{7,3},{8,12},{9,13},{10,... | collective-permute-start | bytes 516104 | tf_op jit(solution)/shard_map/ppermute | solution.py:14
  27.1 12.7 %collective-permute-start.2 = (bf16[64,2688]{1,0:T(8,128)(2,1)S(1)}, bf16[64,2688]{1,0:T(8,128)(2,1)S(1)}, u32[]{:S(2)}, u32[]{:S(2)}) collective-permute-start(bf16[64,2688]{1,0:T(8,128)(2,1)S(1)} %pad_maximum_fusion.4), channel_id=1, source_target_pairs={{0,2},{1,3},{2,0},{3,1},{4,6},{5,7},{6,4},{7,5},{8,10},{9,11},{10,... | collective-permute-start | bytes 1032200 | tf_op jit(solution)/shard_map/ppermute | solution.py:14
  30.8 14.7 %collective-permute-start.10 = (bf16[64,2688]{1,0:T(8,128)(2,1)S(1)}, bf16[64,2688]{1,0:T(8,128)(2,1)S(1)}, u32[]{:S(2)}, u32[]{:S(2)}) collective-permute-start(bf16[64,2688]{1,0:T(8,128)(2,1)S(1)} %pad_maximum_fusion.5), channel_id=1, source_target_pairs={{0,2},{1,3},{2,0},{3,1},{4,6},{5,7},{6,4},{7,5},{8,10},{9,11},{10,... | collective-permute-start | bytes 1032200 | tf_op jit(solution)/shard_map/ppermute | solution.py:14
  34.4 18.4 %collective-permute-start.18 = (bf16[64,2688]{1,0:T(8,128)(2,1)S(1)}, bf16[64,2688]{1,0:T(8,128)(2,1)S(1)}, u32[]{:S(2)}, u32[]{:S(2)}) collective-permute-start(bf16[64,2688]{1,0:T(8,128)(2,1)S(1)} %pad_maximum_fusion.6), channel_id=1, source_target_pairs={{0,2},{1,3},{2,0},{3,1},{4,6},{5,7},{6,4},{7,5},{8,10},{9,11},{10,... | collective-permute-start | bytes 1032200 | tf_op jit(solution)/shard_map/ppermute | solution.py:14
  38.0 21.1 %collective-permute-start.26 = (bf16[64,2688]{1,0:T(8,128)(2,1)S(1)}, bf16[64,2688]{1,0:T(8,128)(2,1)S(1)}, u32[]{:S(2)}, u32[]{:S(2)}) collective-permute-start(bf16[64,2688]{1,0:T(8,128)(2,1)S(1)} %pad_maximum_fusion.7), channel_id=1, source_target_pairs={{0,2},{1,3},{2,0},{3,1},{4,6},{5,7},{6,4},{7,5},{8,10},{9,11},{10,... | collective-permute-start | bytes 1032200 | tf_op jit(solution)/shard_map/ppermute | solution.py:14
  39.8 19.5 %collective-permute-start.3 = (bf16[128,2688]{1,0:T(8,128)(2,1)S(1)}, bf16[128,2688]{1,0:T(8,128)(2,1)S(1)}, u32[]{:S(2)}, u32[]{:S(2)}) collective-permute-start(bf16[128,2688]{1,0:T(8,128)(2,1)S(1)} %pad_maximum_fusion.refs_1_), channel_id=1, source_target_pairs={{0,1},{1,0},{2,3},{3,2},{4,5},{5,4},{6,7},{7,6},{8,9},{9,8},{10,11... | collective-permute-start | bytes 2064392 | tf_op jit(solution)/shard_map/ppermute | solution.py:14
  45.5 19.7 %collective-permute-start.11 = (bf16[128,2688]{1,0:T(8,128)(2,1)S(1)}, bf16[128,2688]{1,0:T(8,128)(2,1)S(1)}, u32[]{:S(2)}, u32[]{:S(2)}) collective-permute-start(bf16[128,2688]{1,0:T(8,128)(2,1)S(1)} %pad_maximum_fusion.1.refs_1_), channel_id=1, source_target_pairs={{0,1},{1,0},{2,3},{3,2},{4,5},{5,4},{6,7},{7,6},{8,9},{9,8},{10,11... | collective-permute-start | bytes 2064392 | tf_op jit(solution)/shard_map/ppermute | solution.py:14
  52.9 15.8 %collective-permute-start.19 = (bf16[128,2688]{1,0:T(8,128)(2,1)S(1)}, bf16[128,2688]{1,0:T(8,128)(2,1)S(1)}, u32[]{:S(2)}, u32[]{:S(2)}) collective-permute-start(bf16[128,2688]{1,0:T(8,128)(2,1)S(1)} %pad_maximum_fusion.2.refs_1_), channel_id=1, source_target_pairs={{0,1},{1,0},{2,3},{3,2},{4,5},{5,4},{6,7},{7,6},{8,9},{9,8},{10,11... | collective-permute-start | bytes 2064392 | tf_op jit(solution)/shard_map/ppermute | solution.py:14
  59.2 13.3 %collective-permute-start.27 = (bf16[128,2688]{1,0:T(8,128)(2,1)S(1)}, bf16[128,2688]{1,0:T(8,128)(2,1)S(1)}, u32[]{:S(2)}, u32[]{:S(2)}) collective-permute-start(bf16[128,2688]{1,0:T(8,128)(2,1)S(1)} %pad_maximum_fusion.3.refs_1_), channel_id=1, source_target_pairs={{0,1},{1,0},{2,3},{3,2},{4,5},{5,4},{6,7},{7,6},{8,9},{9,8},{10,11... | collective-permute-start | bytes 2064392 | tf_op jit(solution)/shard_map/ppermute | solution.py:14
  64.7 11.2 %collective-permute-start.4 = (bf16[128,2560]{1,0:T(8,128)(2,1)S(1)}, bf16[128,2560]{1,0:T(8,128)(2,1)S(1)}, u32[]{:S(2)}, u32[]{:S(2)}) collective-permute-start(bf16[128,2560]{1,0:T(8,128)(2,1)S(1)} %get-tuple-element.14), channel_id=1, source_target_pairs={{0,1},{1,0},{2,3},{3,2},{4,5},{5,4},{6,7},{7,6},{8,9},{9,8},{10,11... | collective-permute-start | bytes 1966088 | tf_op jit(solution)/shard_map/ppermute | solution.py:14
  68.5 9.2 %collective-permute-start.12 = (bf16[128,2560]{1,0:T(8,128)(2,1)S(1)}, bf16[128,2560]{1,0:T(8,128)(2,1)S(1)}, u32[]{:S(2)}, u32[]{:S(2)}) collective-permute-start(bf16[128,2560]{1,0:T(8,128)(2,1)S(1)} %get-tuple-element.16), channel_id=1, source_target_pairs={{0,1},{1,0},{2,3},{3,2},{4,5},{5,4},{6,7},{7,6},{8,9},{9,8},{10,11... | collective-permute-start | bytes 1966088 | tf_op jit(solution)/shard_map/ppermute | solution.py:14
  71.9 6.4 %collective-permute-start.20 = (bf16[128,2560]{1,0:T(8,128)(2,1)S(1)}, bf16[128,2560]{1,0:T(8,128)(2,1)S(1)}, u32[]{:S(2)}, u32[]{:S(2)}) collective-permute-start(bf16[128,2560]{1,0:T(8,128)(2,1)S(1)} %get-tuple-element.18), channel_id=1, source_target_pairs={{0,1},{1,0},{2,3},{3,2},{4,5},{5,4},{6,7},{7,6},{8,9},{9,8},{10,11... | collective-permute-start | bytes 1966088 | tf_op jit(solution)/shard_map/ppermute | solution.py:14
  75.8 4.5 %collective-permute-start.28 = (bf16[128,2560]{1,0:T(8,128)(2,1)S(1)}, bf16[128,2560]{1,0:T(8,128)(2,1)S(1)}, u32[]{:S(2)}, u32[]{:S(2)}) collective-permute-start(bf16[128,2560]{1,0:T(8,128)(2,1)S(1)} %get-tuple-element.20), channel_id=1, source_target_pairs={{0,1},{1,0},{2,3},{3,2},{4,5},{5,4},{6,7},{7,6},{8,9},{9,8},{10,11... | collective-permute-start | bytes 1966088 | tf_op jit(solution)/shard_map/ppermute | solution.py:14
  76.0 10.6 %collective-permute-start.5 = (bf16[64,2560]{1,0:T(8,128)(2,1)S(1)}, bf16[64,2560]{1,0:T(8,128)(2,1)S(1)}, u32[]{:S(2)}, u32[]{:S(2)}) collective-permute-start(bf16[64,2560]{1,0:T(8,128)(2,1)S(1)} %get-tuple-element.22), channel_id=1, source_target_pairs={{0,2},{1,3},{2,0},{3,1},{4,6},{5,7},{6,4},{7,5},{8,10},{9,11},{10,... | collective-permute-start | bytes 983048 | tf_op jit(solution)/shard_map/ppermute | solution.py:14
  77.9 15.7 %collective-permute-start.13 = (bf16[64,2560]{1,0:T(8,128)(2,1)S(1)}, bf16[64,2560]{1,0:T(8,128)(2,1)S(1)}, u32[]{:S(2)}, u32[]{:S(2)}) collective-permute-start(bf16[64,2560]{1,0:T(8,128)(2,1)S(1)} %get-tuple-element.24), channel_id=1, source_target_pairs={{0,2},{1,3},{2,0},{3,1},{4,6},{5,7},{6,4},{7,5},{8,10},{9,11},{10,... | collective-permute-start | bytes 983048 | tf_op jit(solution)/shard_map/ppermute | solution.py:14
  78.5 22.1 %collective-permute-start.21 = (bf16[64,2560]{1,0:T(8,128)(2,1)S(1)}, bf16[64,2560]{1,0:T(8,128)(2,1)S(1)}, u32[]{:S(2)}, u32[]{:S(2)}) collective-permute-start(bf16[64,2560]{1,0:T(8,128)(2,1)S(1)} %get-tuple-element.26), channel_id=1, source_target_pairs={{0,2},{1,3},{2,0},{3,1},{4,6},{5,7},{6,4},{7,5},{8,10},{9,11},{10,... | collective-permute-start | bytes 983048 | tf_op jit(solution)/shard_map/ppermute | solution.py:14
  80.4 26.9 %collective-permute-start.29 = (bf16[64,2560]{1,0:T(8,128)(2,1)S(1)}, bf16[64,2560]{1,0:T(8,128)(2,1)S(1)}, u32[]{:S(2)}, u32[]{:S(2)}) collective-permute-start(bf16[64,2560]{1,0:T(8,128)(2,1)S(1)} %get-tuple-element.28), channel_id=1, source_target_pairs={{0,2},{1,3},{2,0},{3,1},{4,6},{5,7},{6,4},{7,5},{8,10},{9,11},{10,... | collective-permute-start | bytes 983048 | tf_op jit(solution)/shard_map/ppermute | solution.py:14
  86.7 20.7 %collective-permute-start.6 = (bf16[32,2560]{1,0:T(8,128)(2,1)S(1)}, bf16[32,2560]{1,0:T(8,128)(2,1)S(1)}, u32[]{:S(2)}, u32[]{:S(2)}) collective-permute-start(bf16[32,2560]{1,0:T(8,128)(2,1)S(1)} %get-tuple-element.30), channel_id=1, source_target_pairs={{0,4},{1,5},{2,6},{3,7},{4,0},{5,1},{6,2},{7,3},{8,12},{9,13},{10,... | collective-permute-start | bytes 491528 | tf_op jit(solution)/shard_map/ppermute | solution.py:14
  93.7 17.9 %collective-permute-start.14 = (bf16[32,2560]{1,0:T(8,128)(2,1)S(1)}, bf16[32,2560]{1,0:T(8,128)(2,1)S(1)}, u32[]{:S(2)}, u32[]{:S(2)}) collective-permute-start(bf16[32,2560]{1,0:T(8,128)(2,1)S(1)} %get-tuple-element.32), channel_id=1, source_target_pairs={{0,4},{1,5},{2,6},{3,7},{4,0},{5,1},{6,2},{7,3},{8,12},{9,13},{10,... | collective-permute-start | bytes 491528 | tf_op jit(solution)/shard_map/ppermute | solution.py:14
  100.7 11.0 %collective-permute-start.22 = (bf16[32,2560]{1,0:T(8,128)(2,1)S(1)}, bf16[32,2560]{1,0:T(8,128)(2,1)S(1)}, u32[]{:S(2)}, u32[]{:S(2)}) collective-permute-start(bf16[32,2560]{1,0:T(8,128)(2,1)S(1)} %get-tuple-element.34), channel_id=1, source_target_pairs={{0,4},{1,5},{2,6},{3,7},{4,0},{5,1},{6,2},{7,3},{8,12},{9,13},{10,... | collective-permute-start | bytes 491528 | tf_op jit(solution)/shard_map/ppermute | solution.py:14
  107.3 8.2 %collective-permute-start.30 = (bf16[32,2560]{1,0:T(8,128)(2,1)S(1)}, bf16[32,2560]{1,0:T(8,128)(2,1)S(1)}, u32[]{:S(2)}, u32[]{:S(2)}) collective-permute-start(bf16[32,2560]{1,0:T(8,128)(2,1)S(1)} %get-tuple-element.36), channel_id=1, source_target_pairs={{0,4},{1,5},{2,6},{3,7},{4,0},{5,1},{6,2},{7,3},{8,12},{9,13},{10,... | collective-permute-start | bytes 491528 | tf_op jit(solution)/shard_map/ppermute | solution.py:14
  107.4 9.2 %collective-permute-start.7 = (bf16[16,2560]{1,0:T(8,128)(2,1)S(1)}, bf16[16,2560]{1,0:T(8,128)(2,1)S(1)}, u32[]{:S(2)}, u32[]{:S(2)}) collective-permute-start(bf16[16,2560]{1,0:T(8,128)(2,1)S(1)} %add_convert_fusion.26), channel_id=1, source_target_pairs={{0,8},{1,9},{2,10},{3,11},{4,12},{5,13},{6,14},{7,15},{8,0},{9,1},... | collective-permute-start | bytes 245768 | tf_op jit(solution)/shard_map/ppermute | solution.py:14
  111.6 12.3 %collective-permute-start.15 = (bf16[16,2560]{1,0:T(8,128)(2,1)S(1)}, bf16[16,2560]{1,0:T(8,128)(2,1)S(1)}, u32[]{:S(2)}, u32[]{:S(2)}) collective-permute-start(bf16[16,2560]{1,0:T(8,128)(2,1)S(1)} %add_convert_fusion.23), channel_id=1, source_target_pairs={{0,8},{1,9},{2,10},{3,11},{4,12},{5,13},{6,14},{7,15},{8,0},{9,1},... | collective-permute-start | bytes 245768 | tf_op jit(solution)/shard_map/ppermute | solution.py:14
  111.7 13.8 %collective-permute-start.23 = (bf16[16,2560]{1,0:T(8,128)(2,1)S(1)}, bf16[16,2560]{1,0:T(8,128)(2,1)S(1)}, u32[]{:S(2)}, u32[]{:S(2)}) collective-permute-start(bf16[16,2560]{1,0:T(8,128)(2,1)S(1)} %add_convert_fusion.20), channel_id=1, source_target_pairs={{0,8},{1,9},{2,10},{3,11},{4,12},{5,13},{6,14},{7,15},{8,0},{9,1},... | collective-permute-start | bytes 245768 | tf_op jit(solution)/shard_map/ppermute | solution.py:14
  115.6 10.8 %collective-permute-start.31 = (bf16[16,2560]{1,0:T(8,128)(2,1)S(1)}, bf16[16,2560]{1,0:T(8,128)(2,1)S(1)}, u32[]{:S(2)}, u32[]{:S(2)}) collective-permute-start(bf16[16,2560]{1,0:T(8,128)(2,1)S(1)} %add_convert_fusion.17), channel_id=1, source_target_pairs={{0,8},{1,9},{2,10},{3,11},{4,12},{5,13},{6,14},{7,15},{8,0},{9,1},... | collective-permute-start | bytes 245768 | tf_op jit(solution)/shard_map/ppermute | solution.py:14
  (4 other events, 52.1 us)

commit v3 on v2

v3 whole, which is shorter than its diff:
```python
import jax
import jax.numpy as jnp
from jax import lax
from jax.experimental import pallas as pl
from jax.experimental.pallas import tpu as pltpu
from jax.sharding import PartitionSpec as P

PIECES = 4
LANES = 128
BLOCK = 256
MIB = 1024 * 1024
WORK_COST = pl.CostEstimate(flops=1000, bytes_accessed=1000, transcendentals=0)
VMEM = pl.BlockSpec(memory_space=pltpu.VMEM)


def swap(array, axis_size, bit):
    return lax.ppermute(array, "expert", [(i, i ^ bit) for i in range(axis_size)])


def after(array, *others):
    return lax.optimization_barrier((array, *others))[0]


def prepare_kernel(experts, rows_ref, ids_ref, weights_ref, *refs):
    piece_refs, (ids_held, weights_held, sems) = refs[:-3], refs[-3:]
    steps, _, row_count = ids_ref.shape
    width = rows_ref.shape[1]
    share, full = piece_refs[0].shape
    small = [
        pltpu.make_async_copy(ids_ref, ids_held, sems.at[0]),
        pltpu.make_async_copy(weights_ref, weights_held, sems.at[1]),
    ]
    large = [
        pltpu.make_async_copy(
            rows_ref.at[pl.ds(piece * share, share)],
            ref.at[:, pl.ds(0, width)],
            sems.at[2 + piece],
        )
        for piece, ref in enumerate(piece_refs)
    ]
    for copy in small + large:
        copy.start()
    for copy in small:
        copy.wait()
    columns = []
    for step in range(steps):
        ids, weights = ids_held[step], weights_held[step]
        normalized = weights / jnp.sum(weights, axis=0, keepdims=True)
        labels = lax.broadcasted_iota(jnp.int32, (experts, row_count), 0)
        spread = jnp.zeros((experts, row_count), jnp.float32)
        for choice in range(ids.shape[0]):
            mine = ids[choice : choice + 1, :] == labels
            spread = spread + jnp.where(mine, normalized[choice : choice + 1, :], 0.0)
        high = spread.astype(jnp.bfloat16)
        low = (spread - high.astype(jnp.float32)).astype(jnp.bfloat16)
        parts = jnp.concatenate([high, low], axis=0)
        line = lax.broadcasted_iota(jnp.int32, (2 * experts, full - width), 0)
        lane = lax.broadcasted_iota(jnp.int32, (2 * experts, full - width), 1)
        unit = (line == lane).astype(jnp.bfloat16)
        turned = lax.dot_general(
            parts, unit, (((0,), (0,)), ((), ())), preferred_element_type=jnp.float32
        )
        columns.append(turned.astype(jnp.bfloat16))
    column = jnp.concatenate(columns, axis=0)
    for piece, ref in enumerate(piece_refs):
        ref[:, width:] = column[piece * share : (piece + 1) * share]
    for copy in large:
        copy.wait()


def prepare(rows, route_ids, route_weights, experts):
    total, width = rows.shape
    full = width + -(-2 * experts // LANES) * LANES
    shape = jax.ShapeDtypeStruct((total // PIECES, full), rows.dtype)
    ids, weights = jnp.swapaxes(route_ids, 1, 2), jnp.swapaxes(route_weights, 1, 2)
    return pl.pallas_call(
        lambda *refs: prepare_kernel(experts, *refs),
        out_shape=(shape,) * PIECES,
        in_specs=[pl.BlockSpec(memory_space=pltpu.HBM)] * 3,
        out_specs=(VMEM,) * PIECES,
        scratch_shapes=[
            pltpu.VMEM(ids.shape, ids.dtype),
            pltpu.VMEM(weights.shape, weights.dtype),
            pltpu.SemaphoreType.DMA((2 + PIECES,)),
        ],
        compiler_params=pltpu.CompilerParams(vmem_limit_bytes=40 * MIB),
    )(rows, ids, weights)


def expert_kernel(experts, places, own_ref, near_ref, far_ref, gate_ref, up_ref, down_ref, keep_ref, send_ref):
    width = gate_ref.shape[0]
    half = near_ref.shape[0]
    share = half // len(places)
    own = own_ref[0]
    block = min(BLOCK // 2, half)
    for start in range(0, half, block):
        part = slice(start, start + block)
        rows = jnp.concatenate([near_ref[part, :], far_ref[part, :]], axis=0)
        tokens = rows[:, :width]
        spread = rows[:, width:].astype(jnp.float32)
        lane = lax.broadcasted_iota(jnp.int32, spread.shape, 1)
        mine = (lane == own) | (lane == own + experts)
        weight = jnp.sum(jnp.where(mine, spread, 0.0), axis=1, keepdims=True)
        gate = jnp.dot(tokens, gate_ref[...], preferred_element_type=jnp.float32)
        up = jnp.dot(tokens, up_ref[...], preferred_element_type=jnp.float32)
        hidden = (gate / (1.0 + jnp.exp(-gate)) * up).astype(jnp.bfloat16)
        result = jnp.dot(hidden, down_ref[...], preferred_element_type=jnp.float32)
        scaled = (result * weight).astype(jnp.bfloat16)
        for row in range(0, block, share):
            place = places[(start + row) // share] * share
            keep_ref[place : place + share, :] = scaled[row : row + share]
            send_ref[place : place + share, :] = scaled[block + row : block + row + share]


def places_of(gather, scatter):
    blocks = []
    for index in range(1 << (len(gather) - 1)):
        taken = {bit for place, bit in enumerate(gather[:-1]) if index >> place & 1}
        blocks.append(sum(1 << place for place, bit in enumerate(reversed(scatter[1:])) if bit in taken))
    return tuple(blocks)


def expert_rows(near, far, experts, places, gate_proj, up_proj, down_proj):
    half = near.shape[0]
    shape = jax.ShapeDtypeStruct((half, gate_proj.shape[0]), jnp.bfloat16)
    return pl.pallas_call(
        lambda *refs: expert_kernel(experts, places, *refs),
        out_shape=(shape, shape),
        in_specs=[pl.BlockSpec(memory_space=pltpu.SMEM)] + [VMEM] * 5,
        out_specs=(VMEM, VMEM),
        compiler_params=pltpu.CompilerParams(vmem_limit_bytes=32 * MIB),
        cost_estimate=WORK_COST,
    )(lax.axis_index("expert").reshape(1), near, far, gate_proj, up_proj, down_proj)


def total_of(first, second):
    return (first.astype(jnp.float32) + second.astype(jnp.float32)).astype(jnp.bfloat16)


def add_halves(kept, arrived):
    half = kept.shape[0] // 2
    return total_of(kept[:half], arrived[:half]), total_of(kept[half:], arrived[half:])


def on_device(hidden_states, route_ids, route_weights, gate_proj, up_proj, down_proj):
    step_count, row_count, feature_width = hidden_states.shape
    axis_size = lax.axis_size("expert")
    experts = axis_size * gate_proj.shape[0]
    bits = [1 << i for i in reversed(range(axis_size.bit_length() - 1))]
    beside, last = bits[-2:]
    outward = bits
    gathers = [outward] * PIECES
    scatters = [outward[::-1]] * PIECES

    rows = hidden_states.reshape(step_count * row_count, feature_width)
    pieces = prepare(rows, route_ids, route_weights, experts)
    matrices = gate_proj[0], up_proj[0], down_proj[0]
    held = list(pieces)
    got = {}

    def grow(piece, stage, *ties, late=()):
        bit = gathers[piece][stage]
        far = swap(after(held[piece], *ties) if ties else held[piece], axis_size, bit)
        own = after(held[piece], *late) if late else held[piece]
        held[piece] = jnp.concatenate([own, far], axis=0)
        got[piece, stage] = held[piece]

    final = len(bits) - 1
    for piece in range(PIECES):
        ties = () if piece == 0 else (got[0, 0],) if piece == 1 else (got[piece - 2, final - 2],)
        grow(piece, 0, *ties)
        for stage in range(1, final):
            grow(piece, stage)
    sums = []
    for piece in range(PIECES):
        near = after(held[piece], sums[-1][0]) if sums else held[piece]
        far = swap(near, axis_size, last)
        places = places_of(gathers[piece], scatters[piece])
        sums.append(expert_rows(near, far, experts, places, *matrices))

    def shrink(piece, stage, *late):
        keep, send = sums[piece]
        if late:
            keep = after(keep, *late)
        arrived = swap(send, axis_size, scatters[piece][stage])
        if stage == final:
            sums[piece] = (total_of(keep, arrived), None)
        else:
            sums[piece] = add_halves(keep, arrived)

    firsts = [keep for keep, _ in sums]
    for piece in range(PIECES):
        shrink(piece, 0, *firsts[piece + 1 : piece + 2])
    closed = sums[-1][0]

    for stage in range(1, final + 1):
        for piece in range(PIECES):
            shrink(piece, stage, *((closed,) if stage == 1 and piece + 1 < PIECES else ()))
    outputs = [total for total, _ in sums]
    return jnp.concatenate(outputs, axis=0).reshape(hidden_states.shape)


def solution(mesh):
    placed = (
        P(None, ("groups", "expert"), None),
        P(None, ("groups", "expert"), None),
        P(None, ("groups", "expert"), None),
        P("expert", None, None),
        P("expert", None, None),
        P("expert", None, None),
    )
    return jax.shard_map(
        on_device,
        mesh=mesh,
        in_specs=placed,
        out_specs=P(None, ("groups", "expert"), None),
        check_vma=False,
    )
```

time: 128 us -> 105 us (0.82)
  waiting for transfers between devices: 75.5 us -> 54 us
  local copies, waits for them, and re-layouts: 5.05 us -> 6.75 us
  starting transfers between devices: 30.2 us -> 28.5 us
    ppermute x32, waiting for transfers between devices: 75.5 us -> 54 us  [swap(): lax.ppermute(array, 'expert', [(i, i ^ bit) for i in range(axis_size)])]
    unnamed x10 -> x21, local copies, waits for them, and re-layouts: 3.52 us -> 6.7 us
    ppermute x32, starting transfers between devices: 30.2 us -> 28.5 us  [swap(): lax.ppermute(array, 'expert', [(i, i ^ bit) for i in range(axis_size)])]
    pallas_call x4 -> x5, Pallas kernels: 13.1 us -> 13.6 us  [the longest x4 13.1 us: expert_rows(): pl.pallas_call(lambda *refs: expert_kernel(experts, places, *refs), out_s...]
  transfers between devices with their start and end apart: 32 -> 32, of which waited for: 19 -> 20; matrix products, arithmetic and copies ran while one was open for 1% -> 1% of each run, Pallas kernels for 10% -> 12%
where the time goes in v3:
time: 105 us
  waiting for transfers between devices  54 us (51%)
  starting transfers between devices  28.5 us (27%)
  Pallas kernels  13.6 us (13%)
  local copies, waits for them, and re-layouts  6.75 us (6%)
  other arithmetic  2.16 us (2%)
    ppermute x32, waiting for transfers between devices, swap(): lax.ppermute(array, 'expert', [(i, i ^ bit) for i in range(axis_size)])  54 us
    ppermute x32, starting transfers between devices, swap(): lax.ppermute(array, 'expert', [(i, i ^ bit) for i in range(axis_size)])  28.5 us
    pallas_call x4, Pallas kernels, expert_rows(): pl.pallas_call(lambda *refs: expert_kernel(experts, places, *refs), out_s...  13.1 us
    unnamed x21, local copies, waits for them, and re-layouts  6.7 us
  transfers between devices with their start and end apart: 32, of which 20 were waited for; matrix products, arithmetic and copies ran while one was open for 1% of the time, Pallas kernels for 12%

profile of v3, /device:TPU:0, one launch (start us, length us, event | category | flops | bytes accessed | tf_op | source)
XLA Modules:
  0.0 105.2 jit_solution(10181399441615044397)
XLA Ops:
  2.8 4.1 %collective-permute-start = (bf16[16,2688]{1,0:T(8,128)(2,1)S(1)}, bf16[16,2688]{1,0:T(8,128)(2,1)S(1)}, u32[]{:S(2)}, u32[]{:S(2)}) collective-permute-start(bf16[16,2688]{1,0:T(8,128)(2,1)S(1)} %get-tuple-element.29), channel_id=1, source_target_pairs={{0,8},{1,9},{2,10},{3,11},{4,12},{5,13},{6,14},{7,15},{8,0},{9,1},... | collective-permute-start | bytes 258056 | tf_op jit(solution)/shard_map/ppermute | solution.py:17
  7.0 4.4 %collective-permute-done = bf16[16,2688]{1,0:T(8,128)(2,1)S(1)} collective-permute-done((bf16[16,2688]{1,0:T(8,128)(2,1)S(1)}, bf16[16,2688]{1,0:T(8,128)(2,1)S(1)}, u32[]{:S(2)}, u32[]{:S(2)}) %collective-permute-start) | collective-permute-done | bytes 86048 | tf_op jit(solution)/shard_map/ppermute | solution.py:17
  12.4 3.1 %collective-permute-start.1 = (bf16[32,2688]{1,0:T(8,128)(2,1)S(1)}, bf16[32,2688]{1,0:T(8,128)(2,1)S(1)}, u32[]{:S(2)}, u32[]{:S(2)}) collective-permute-start(bf16[32,2688]{1,0:T(8,128)(2,1)S(1)} %get-tuple-element.73), channel_id=1, source_target_pairs={{0,4},{1,5},{2,6},{3,7},{4,0},{5,1},{6,2},{7,3},{8,12},{9,13},{10,... | collective-permute-start | bytes 516104 | tf_op jit(solution)/shard_map/ppermute | solution.py:17
  15.5 3.1 %collective-permute-done.4 = bf16[16,2688]{1,0:T(8,128)(2,1)S(1)} collective-permute-done((bf16[16,2688]{1,0:T(8,128)(2,1)S(1)}, bf16[16,2688]{1,0:T(8,128)(2,1)S(1)}, u32[]{:S(2)}, u32[]{:S(2)}) %collective-permute-start.4) | collective-permute-done | bytes 86048 | tf_op jit(solution)/shard_map/ppermute | solution.py:17
  19.0 2.6 %collective-permute-done.1 = bf16[32,2688]{1,0:T(8,128)(2,1)S(1)} collective-permute-done((bf16[32,2688]{1,0:T(8,128)(2,1)S(1)}, bf16[32,2688]{1,0:T(8,128)(2,1)S(1)}, u32[]{:S(2)}, u32[]{:S(2)}) %collective-permute-start.1) | collective-permute-done | bytes 172064 | tf_op jit(solution)/shard_map/ppermute | solution.py:17
  21.6 1.6 %collective-permute-start.2 = (bf16[64,2688]{1,0:T(8,128)(2,1)S(1)}, bf16[64,2688]{1,0:T(8,128)(2,1)S(1)}, u32[]{:S(2)}, u32[]{:S(2)}) collective-permute-start(bf16[64,2688]{1,0:T(8,128)(2,1)S(1)} %get-tuple-element.70), channel_id=1, source_target_pairs={{0,2},{1,3},{2,0},{3,1},{4,6},{5,7},{6,4},{7,5},{8,10},{9,11},{10,... | collective-permute-start | bytes 1032200 | tf_op jit(solution)/shard_map/ppermute | solution.py:17
  24.3 2.5 %collective-permute-start.6 = (bf16[64,2688]{1,0:T(8,128)(2,1)S(1)}, bf16[64,2688]{1,0:T(8,128)(2,1)S(1)}, u32[]{:S(2)}, u32[]{:S(2)}) collective-permute-start(bf16[64,2688]{1,0:T(8,128)(2,1)S(1)} %constant_dynamic-update-slice_fusion.9), channel_id=1, source_target_pairs={{0,2},{1,3},{2,0},{3,1},{4,6},{5,7},{6,4},{7,5},{8,10},{9,11},{10,... | collective-permute-start | bytes 1032200 | tf_op jit(solution)/shard_map/ppermute | solution.py:17
  26.8 1.2 %collective-permute-start.9 = (bf16[16,2688]{1,0:T(8,128)(2,1)S(1)}, bf16[16,2688]{1,0:T(8,128)(2,1)S(1)}, u32[]{:S(2)}, u32[]{:S(2)}) collective-permute-start(bf16[16,2688]{1,0:T(8,128)(2,1)S(1)} %get-tuple-element.38), channel_id=1, source_target_pairs={{0,8},{1,9},{2,10},{3,11},{4,12},{5,13},{6,14},{7,15},{8,0},{9,1},... | collective-permute-start | bytes 258056 | tf_op jit(solution)/shard_map/ppermute | solution.py:17
  28.0 3.3 %collective-permute-done.12 = bf16[16,2688]{1,0:T(8,128)(2,1)S(1)} collective-permute-done((bf16[16,2688]{1,0:T(8,128)(2,1)S(1)}, bf16[16,2688]{1,0:T(8,128)(2,1)S(1)}, u32[]{:S(2)}, u32[]{:S(2)}) %collective-permute-start.12) | collective-permute-done | bytes 86048 | tf_op jit(solution)/shard_map/ppermute | solution.py:17
  31.4 1.7 %collective-permute-done.9 = bf16[16,2688]{1,0:T(8,128)(2,1)S(1)} collective-permute-done((bf16[16,2688]{1,0:T(8,128)(2,1)S(1)}, bf16[16,2688]{1,0:T(8,128)(2,1)S(1)}, u32[]{:S(2)}, u32[]{:S(2)}) %collective-permute-start.9) | collective-permute-done | bytes 86048 | tf_op jit(solution)/shard_map/ppermute | solution.py:17
  33.6 4.0 %collective-permute-done.13 = bf16[32,2688]{1,0:T(8,128)(2,1)S(1)} collective-permute-done((bf16[32,2688]{1,0:T(8,128)(2,1)S(1)}, bf16[32,2688]{1,0:T(8,128)(2,1)S(1)}, u32[]{:S(2)}, u32[]{:S(2)}) %collective-permute-start.13) | collective-permute-done | bytes 172064 | tf_op jit(solution)/shard_map/ppermute | solution.py:17
  38.3 1.2 %collective-permute-done.10 = bf16[32,2688]{1,0:T(8,128)(2,1)S(1)} collective-permute-done((bf16[32,2688]{1,0:T(8,128)(2,1)S(1)}, bf16[32,2688]{1,0:T(8,128)(2,1)S(1)}, u32[]{:S(2)}, u32[]{:S(2)}) %collective-permute-start.10) | collective-permute-done | bytes 172064 | tf_op jit(solution)/shard_map/ppermute | solution.py:17
  40.4 2.1 %copy-done.1 = bf16[1,2560,768]{2,1,0:T(8,128)(2,1)S(1)} copy-done((bf16[1,2560,768]{2,1,0:T(8,128)(2,1)S(1)}, bf16[1,2560,768]{2,1,0:T(8,128)(2,1)}, u32[]{:S(2)}) %copy-start.1) | copy-done | bytes 3932184
  42.5 2.1 %copy-done.3 = bf16[1,768,2560]{2,1,0:T(8,128)(2,1)S(1)} copy-done((bf16[1,768,2560]{2,1,0:T(8,128)(2,1)S(1)}, bf16[1,768,2560]{2,1,0:T(8,128)(2,1)}, u32[]{:S(2)}) %copy-start.3) | copy-done | bytes 3932184
  44.6 3.3 %shard_map.65 = (bf16[128,2560]{1,0:T(8,128)(2,1)S(1)}, bf16[128,2560]{1,0:T(8,128)(2,1)S(1)}) custom-call(s32[1]{0:T(128)} %bitcast.refs_0_, bf16[128,2688]{1,0:T(8,128)(2,1)S(1)} %constant_dynamic-update-slice_fusion.5.refs_1_, bf16[128,2688]{1,0:T(8,128)(2,1)S(1)} %collective-permute-done.3.refs_2_, bf16[2560,768]{1,0:T(8,128)(2,1)S(1)} %bitcast.8, ...), custom_call_target="tpu_custom_call" | custom-call | flops 1000 | bytes 1000 | tf_op jit(solution)/shard_map/pallas_call | solution.py:126
  48.6 3.8 %collective-permute-done.11 = bf16[64,2688]{1,0:T(8,128)(2,1)S(1)} collective-permute-done((bf16[64,2688]{1,0:T(8,128)(2,1)S(1)}, bf16[64,2688]{1,0:T(8,128)(2,1)S(1)}, u32[]{:S(2)}, u32[]{:S(2)}) %collective-permute-start.11) | collective-permute-done | bytes 344096 | tf_op jit(solution)/shard_map/ppermute | solution.py:17
  52.5 3.3 %shard_map.66 = (bf16[128,2560]{1,0:T(8,128)(2,1)S(1)}, bf16[128,2560]{1,0:T(8,128)(2,1)S(1)}) custom-call(s32[1]{0:T(128)} %bitcast.refs_0_, bf16[128,2688]{1,0:T(8,128)(2,1)S(1)} %pad_maximum_fusion.refs_1_, bf16[128,2688]{1,0:T(8,128)(2,1)S(1)} %collective-permute-done.7.refs_2_, bf16[2560,768]{1,0:T(8,128)(2,1)S(1)} %bitcast.9, ...), custom_call_target="tpu_custom_call" | custom-call | flops 1000 | bytes 1000 | tf_op jit(solution)/shard_map/pallas_call | solution.py:126
  56.5 1.2 %collective-permute-start.18 = (bf16[64,2560]{1,0:T(8,128)(2,1)S(1)}, bf16[64,2560]{1,0:T(8,128)(2,1)S(1)}, u32[]{:S(2)}, u32[]{:S(2)}) collective-permute-start(bf16[64,2560]{1,0:T(8,128)(2,1)S(1)} %get-tuple-element.54), channel_id=1, source_target_pairs={{0,2},{1,3},{2,0},{3,1},{4,6},{5,7},{6,4},{7,5},{8,10},{9,11},{10,... | collective-permute-start | bytes 983048 | tf_op jit(solution)/shard_map/ppermute | solution.py:17
  57.6 1.2 %collective-permute-done.15.refs_2_ = bf16[128,2688]{1,0:T(8,128)(2,1)S(1)} collective-permute-done((bf16[128,2688]{1,0:T(8,128)(2,1)S(1)}, bf16[128,2688]{1,0:T(8,128)(2,1)S(1)}, u32[]{:S(2)}, u32[]{:S(2)}) %collective-permute-start.15) | collective-permute-done | bytes 688160 | tf_op jit(solution)/shard_map/ppermute | solution.py:17
  58.9 3.3 %shard_map.67 = (bf16[128,2560]{1,0:T(8,128)(2,1)S(1)}, bf16[128,2560]{1,0:T(8,128)(2,1)S(1)}) custom-call(s32[1]{0:T(128)} %bitcast.refs_0_, bf16[128,2688]{1,0:T(8,128)(2,1)S(1)} %pad_maximum_fusion.2.refs_1_, bf16[128,2688]{1,0:T(8,128)(2,1)S(1)} %collective-permute-done.15.refs_2_, bf16[2560,768]{1,0:T(8,128)(2,1)S(1)} %bitcast.10, ...), custom_call_target="tpu_custom_call" | custom-call | flops 1000 | bytes 1000 | tf_op jit(solution)/shard_map/pallas_call | solution.py:126
  64.1 1.2 %collective-permute-done.16.refs_2_ = bf16[128,2688]{1,0:T(8,128)(2,1)S(1)} collective-permute-done((bf16[128,2688]{1,0:T(8,128)(2,1)S(1)}, bf16[128,2688]{1,0:T(8,128)(2,1)S(1)}, u32[]{:S(2)}, u32[]{:S(2)}) %collective-permute-start.16) | collective-permute-done | bytes 688160 | tf_op jit(solution)/shard_map/ppermute | solution.py:17
  65.3 3.3 %shard_map.68 = (bf16[128,2560]{1,0:T(8,128)(2,1)S(1)}, bf16[128,2560]{1,0:T(8,128)(2,1)S(1)}) custom-call(s32[1]{0:T(128)} %bitcast.refs_0_, bf16[128,2688]{1,0:T(8,128)(2,1)S(1)} %pad_maximum_fusion.1.refs_1_, bf16[128,2688]{1,0:T(8,128)(2,1)S(1)} %collective-permute-done.16.refs_2_, bf16[2560,768]{1,0:T(8,128)(2,1)S(1)} %bitcast.11, ...), custom_call_target="tpu_custom_call" | custom-call | flops 1000 | bytes 1000 | tf_op jit(solution)/shard_map/pallas_call | solution.py:126
  69.0 1.2 %collective-permute-start.26 = (bf16[64,2560]{1,0:T(8,128)(2,1)S(1)}, bf16[64,2560]{1,0:T(8,128)(2,1)S(1)}, u32[]{:S(2)}, u32[]{:S(2)}) collective-permute-start(bf16[64,2560]{1,0:T(8,128)(2,1)S(1)} %get-tuple-element.58), channel_id=1, source_target_pairs={{0,2},{1,3},{2,0},{3,1},{4,6},{5,7},{6,4},{7,5},{8,10},{9,11},{10,... | collective-permute-start | bytes 983048 | tf_op jit(solution)/shard_map/ppermute | solution.py:17
  71.4 2.3 %collective-permute-done.22 = bf16[64,2560]{1,0:T(8,128)(2,1)S(1)} collective-permute-done((bf16[64,2560]{1,0:T(8,128)(2,1)S(1)}, bf16[64,2560]{1,0:T(8,128)(2,1)S(1)}, u32[]{:S(2)}, u32[]{:S(2)}) %collective-permute-start.22) | collective-permute-done | bytes 327712 | tf_op jit(solution)/shard_map/ppermute | solution.py:17
  74.1 6.1 %collective-permute-done.26 = bf16[64,2560]{1,0:T(8,128)(2,1)S(1)} collective-permute-done((bf16[64,2560]{1,0:T(8,128)(2,1)S(1)}, bf16[64,2560]{1,0:T(8,128)(2,1)S(1)}, u32[]{:S(2)}, u32[]{:S(2)}) %collective-permute-start.26) | collective-permute-done | bytes 327712 | tf_op jit(solution)/shard_map/ppermute | solution.py:17
  80.7 1.2 %collective-permute-start.29 = (bf16[64,2560]{1,0:T(8,128)(2,1)S(1)}, bf16[64,2560]{1,0:T(8,128)(2,1)S(1)}, u32[]{:S(2)}, u32[]{:S(2)}) collective-permute-start(bf16[64,2560]{1,0:T(8,128)(2,1)S(1)} %get-tuple-element.60), channel_id=1, source_target_pairs={{0,2},{1,3},{2,0},{3,1},{4,6},{5,7},{6,4},{7,5},{8,10},{9,11},{10,... | collective-permute-start | bytes 983048 | tf_op jit(solution)/shard_map/ppermute | solution.py:17
  81.9 2.6 %collective-permute-start.20 = (bf16[16,2560]{1,0:T(8,128)(2,1)S(1)}, bf16[16,2560]{1,0:T(8,128)(2,1)S(1)}, u32[]{:S(2)}, u32[]{:S(2)}) collective-permute-start(bf16[16,2560]{1,0:T(8,128)(2,1)S(1)} %add_convert_fusion.26), channel_id=1, source_target_pairs={{0,8},{1,9},{2,10},{3,11},{4,12},{5,13},{6,14},{7,15},{8,0},{9,1},... | collective-permute-start | bytes 245768 | tf_op jit(solution)/shard_map/ppermute | solution.py:17
  85.0 2.5 %collective-permute-done.27 = bf16[32,2560]{1,0:T(8,128)(2,1)S(1)} collective-permute-done((bf16[32,2560]{1,0:T(8,128)(2,1)S(1)}, bf16[32,2560]{1,0:T(8,128)(2,1)S(1)}, u32[]{:S(2)}, u32[]{:S(2)}) %collective-permute-start.27) | collective-permute-done | bytes 163872 | tf_op jit(solution)/shard_map/ppermute | solution.py:17
  88.1 4.8 %collective-permute-done.20 = bf16[16,2560]{1,0:T(8,128)(2,1)S(1)} collective-permute-done((bf16[16,2560]{1,0:T(8,128)(2,1)S(1)}, bf16[16,2560]{1,0:T(8,128)(2,1)S(1)}, u32[]{:S(2)}, u32[]{:S(2)}) %collective-permute-start.20) | collective-permute-done | bytes 81952 | tf_op jit(solution)/shard_map/ppermute | solution.py:17
  93.2 1.5 %collective-permute-done.24 = bf16[16,2560]{1,0:T(8,128)(2,1)S(1)} collective-permute-done((bf16[16,2560]{1,0:T(8,128)(2,1)S(1)}, bf16[16,2560]{1,0:T(8,128)(2,1)S(1)}, u32[]{:S(2)}, u32[]{:S(2)}) %collective-permute-start.24) | collective-permute-done | bytes 81952 | tf_op jit(solution)/shard_map/ppermute | solution.py:17
  94.8 3.7 %collective-permute-done.30 = bf16[32,2560]{1,0:T(8,128)(2,1)S(1)} collective-permute-done((bf16[32,2560]{1,0:T(8,128)(2,1)S(1)}, bf16[32,2560]{1,0:T(8,128)(2,1)S(1)}, u32[]{:S(2)}, u32[]{:S(2)}) %collective-permute-start.30) | collective-permute-done | bytes 163872 | tf_op jit(solution)/shard_map/ppermute | solution.py:17
  99.7 4.7 %collective-permute-done.31 = bf16[16,2560]{1,0:T(8,128)(2,1)S(1)} collective-permute-done((bf16[16,2560]{1,0:T(8,128)(2,1)S(1)}, bf16[16,2560]{1,0:T(8,128)(2,1)S(1)}, u32[]{:S(2)}, u32[]{:S(2)}) %collective-permute-start.31) | collective-permute-done | bytes 81952 | tf_op jit(solution)/shard_map/ppermute | solution.py:17
  (85 shorter events, 16.6 us)
Async XLA Ops:
  2.8 8.5 %collective-permute-start = (bf16[16,2688]{1,0:T(8,128)(2,1)S(1)}, bf16[16,2688]{1,0:T(8,128)(2,1)S(1)}, u32[]{:S(2)}, u32[]{:S(2)}) collective-permute-start(bf16[16,2688]{1,0:T(8,128)(2,1)S(1)} %get-tuple-element.29), channel_id=1, source_target_pairs={{0,8},{1,9},{2,10},{3,11},{4,12},{5,13},{6,14},{7,15},{8,0},{9,1},... | collective-permute-start | bytes 258056 | tf_op jit(solution)/shard_map/ppermute | solution.py:17
  11.3 7.2 %collective-permute-start.4 = (bf16[16,2688]{1,0:T(8,128)(2,1)S(1)}, bf16[16,2688]{1,0:T(8,128)(2,1)S(1)}, u32[]{:S(2)}, u32[]{:S(2)}) collective-permute-start(bf16[16,2688]{1,0:T(8,128)(2,1)S(1)} %get-tuple-element.32), channel_id=1, source_target_pairs={{0,8},{1,9},{2,10},{3,11},{4,12},{5,13},{6,14},{7,15},{8,0},{9,1},... | collective-permute-start | bytes 258056 | tf_op jit(solution)/shard_map/ppermute | solution.py:17
  12.4 9.1 %collective-permute-start.1 = (bf16[32,2688]{1,0:T(8,128)(2,1)S(1)}, bf16[32,2688]{1,0:T(8,128)(2,1)S(1)}, u32[]{:S(2)}, u32[]{:S(2)}) collective-permute-start(bf16[32,2688]{1,0:T(8,128)(2,1)S(1)} %get-tuple-element.73), channel_id=1, source_target_pairs={{0,4},{1,5},{2,6},{3,7},{4,0},{5,1},{6,2},{7,3},{8,12},{9,13},{10,... | collective-permute-start | bytes 516104 | tf_op jit(solution)/shard_map/ppermute | solution.py:17
  18.6 5.7 %collective-permute-start.5 = (bf16[32,2688]{1,0:T(8,128)(2,1)S(1)}, bf16[32,2688]{1,0:T(8,128)(2,1)S(1)}, u32[]{:S(2)}, u32[]{:S(2)}) collective-permute-start(bf16[32,2688]{1,0:T(8,128)(2,1)S(1)} %pad_maximum_fusion.6), channel_id=1, source_target_pairs={{0,4},{1,5},{2,6},{3,7},{4,0},{5,1},{6,2},{7,3},{8,12},{9,13},{10,... | collective-permute-start | bytes 516104 | tf_op jit(solution)/shard_map/ppermute | solution.py:17
  21.6 16.6 %collective-permute-start.2 = (bf16[64,2688]{1,0:T(8,128)(2,1)S(1)}, bf16[64,2688]{1,0:T(8,128)(2,1)S(1)}, u32[]{:S(2)}, u32[]{:S(2)}) collective-permute-start(bf16[64,2688]{1,0:T(8,128)(2,1)S(1)} %get-tuple-element.70), channel_id=1, source_target_pairs={{0,2},{1,3},{2,0},{3,1},{4,6},{5,7},{6,4},{7,5},{8,10},{9,11},{10,... | collective-permute-start | bytes 1032200 | tf_op jit(solution)/shard_map/ppermute | solution.py:17
  23.2 8.2 %collective-permute-start.12 = (bf16[16,2688]{1,0:T(8,128)(2,1)S(1)}, bf16[16,2688]{1,0:T(8,128)(2,1)S(1)}, u32[]{:S(2)}, u32[]{:S(2)}) collective-permute-start(bf16[16,2688]{1,0:T(8,128)(2,1)S(1)} %get-tuple-element.40), channel_id=1, source_target_pairs={{0,8},{1,9},{2,10},{3,11},{4,12},{5,13},{6,14},{7,15},{8,0},{9,1},... | collective-permute-start | bytes 258056 | tf_op jit(solution)/shard_map/ppermute | solution.py:17
  24.3 15.7 %collective-permute-start.6 = (bf16[64,2688]{1,0:T(8,128)(2,1)S(1)}, bf16[64,2688]{1,0:T(8,128)(2,1)S(1)}, u32[]{:S(2)}, u32[]{:S(2)}) collective-permute-start(bf16[64,2688]{1,0:T(8,128)(2,1)S(1)} %constant_dynamic-update-slice_fusion.9), channel_id=1, source_target_pairs={{0,2},{1,3},{2,0},{3,1},{4,6},{5,7},{6,4},{7,5},{8,10},{9,11},{10,... | collective-permute-start | bytes 1032200 | tf_op jit(solution)/shard_map/ppermute | solution.py:17
  26.8 6.3 %collective-permute-start.9 = (bf16[16,2688]{1,0:T(8,128)(2,1)S(1)}, bf16[16,2688]{1,0:T(8,128)(2,1)S(1)}, u32[]{:S(2)}, u32[]{:S(2)}) collective-permute-start(bf16[16,2688]{1,0:T(8,128)(2,1)S(1)} %get-tuple-element.38), channel_id=1, source_target_pairs={{0,8},{1,9},{2,10},{3,11},{4,12},{5,13},{6,14},{7,15},{8,0},{9,1},... | collective-permute-start | bytes 258056 | tf_op jit(solution)/shard_map/ppermute | solution.py:17
  31.3 6.3 %collective-permute-start.13 = (bf16[32,2688]{1,0:T(8,128)(2,1)S(1)}, bf16[32,2688]{1,0:T(8,128)(2,1)S(1)}, u32[]{:S(2)}, u32[]{:S(2)}) collective-permute-start(bf16[32,2688]{1,0:T(8,128)(2,1)S(1)} %pad_maximum_fusion.8), channel_id=1, source_target_pairs={{0,4},{1,5},{2,6},{3,7},{4,0},{5,1},{6,2},{7,3},{8,12},{9,13},{10,... | collective-permute-start | bytes 516104 | tf_op jit(solution)/shard_map/ppermute | solution.py:17
  33.1 6.4 %collective-permute-start.10 = (bf16[32,2688]{1,0:T(8,128)(2,1)S(1)}, bf16[32,2688]{1,0:T(8,128)(2,1)S(1)}, u32[]{:S(2)}, u32[]{:S(2)}) collective-permute-start(bf16[32,2688]{1,0:T(8,128)(2,1)S(1)} %pad_maximum_fusion.7), channel_id=1, source_target_pairs={{0,4},{1,5},{2,6},{3,7},{4,0},{5,1},{6,2},{7,3},{8,12},{9,13},{10,... | collective-permute-start | bytes 516104 | tf_op jit(solution)/shard_map/ppermute | solution.py:17
  37.7 10.8 %collective-permute-start.14 = (bf16[64,2688]{1,0:T(8,128)(2,1)S(1)}, bf16[64,2688]{1,0:T(8,128)(2,1)S(1)}, u32[]{:S(2)}, u32[]{:S(2)}) collective-permute-start(bf16[64,2688]{1,0:T(8,128)(2,1)S(1)} %pad_maximum_fusion.4), channel_id=1, source_target_pairs={{0,2},{1,3},{2,0},{3,1},{4,6},{5,7},{6,4},{7,5},{8,10},{9,11},{10,... | collective-permute-start | bytes 1032200 | tf_op jit(solution)/shard_map/ppermute | solution.py:17
  38.2 2.2 %collective-permute-start.3 = (bf16[128,2688]{1,0:T(8,128)(2,1)S(1)}, bf16[128,2688]{1,0:T(8,128)(2,1)S(1)}, u32[]{:S(2)}, u32[]{:S(2)}) collective-permute-start(bf16[128,2688]{1,0:T(8,128)(2,1)S(1)} %constant_dynamic-update-slice_fusion.5.refs_1_), channel_id=1, source_target_pairs={{0,1},{1,0},{2,3},{3,2},{4,5},{5,4},{6,7},{7,6},{8,9},{9,8},{10,11... | collective-permute-start | bytes 2064392 | tf_op jit(solution)/shard_map/ppermute | solution.py:17
  39.5 12.8 %collective-permute-start.11 = (bf16[64,2688]{1,0:T(8,128)(2,1)S(1)}, bf16[64,2688]{1,0:T(8,128)(2,1)S(1)}, u32[]{:S(2)}, u32[]{:S(2)}) collective-permute-start(bf16[64,2688]{1,0:T(8,128)(2,1)S(1)} %pad_maximum_fusion.3), channel_id=1, source_target_pairs={{0,2},{1,3},{2,0},{3,1},{4,6},{5,7},{6,4},{7,5},{8,10},{9,11},{10,... | collective-permute-start | bytes 1032200 | tf_op jit(solution)/shard_map/ppermute | solution.py:17
  47.9 8.4 %collective-permute-start.8 = (bf16[128,2560]{1,0:T(8,128)(2,1)S(1)}, bf16[128,2560]{1,0:T(8,128)(2,1)S(1)}, u32[]{:S(2)}, u32[]{:S(2)}) collective-permute-start(bf16[128,2560]{1,0:T(8,128)(2,1)S(1)} %get-tuple-element.36), channel_id=1, source_target_pairs={{0,1},{1,0},{2,3},{3,2},{4,5},{5,4},{6,7},{7,6},{8,9},{9,8},{10,11... | collective-permute-start | bytes 1966088 | tf_op jit(solution)/shard_map/ppermute | solution.py:17
  48.1 4.3 %collective-permute-start.7 = (bf16[128,2688]{1,0:T(8,128)(2,1)S(1)}, bf16[128,2688]{1,0:T(8,128)(2,1)S(1)}, u32[]{:S(2)}, u32[]{:S(2)}) collective-permute-start(bf16[128,2688]{1,0:T(8,128)(2,1)S(1)} %pad_maximum_fusion.refs_1_), channel_id=1, source_target_pairs={{0,1},{1,0},{2,3},{3,2},{4,5},{5,4},{6,7},{7,6},{8,9},{9,8},{10,11... | collective-permute-start | bytes 2064392 | tf_op jit(solution)/shard_map/ppermute | solution.py:17
  55.7 7.0 %collective-permute-start.21 = (bf16[128,2560]{1,0:T(8,128)(2,1)S(1)}, bf16[128,2560]{1,0:T(8,128)(2,1)S(1)}, u32[]{:S(2)}, u32[]{:S(2)}) collective-permute-start(bf16[128,2560]{1,0:T(8,128)(2,1)S(1)} %get-tuple-element.48), channel_id=1, source_target_pairs={{0,1},{1,0},{2,3},{3,2},{4,5},{5,4},{6,7},{7,6},{8,9},{9,8},{10,11... | collective-permute-start | bytes 1966088 | tf_op jit(solution)/shard_map/ppermute | solution.py:17
  55.8 3.1 %collective-permute-start.15 = (bf16[128,2688]{1,0:T(8,128)(2,1)S(1)}, bf16[128,2688]{1,0:T(8,128)(2,1)S(1)}, u32[]{:S(2)}, u32[]{:S(2)}) collective-permute-start(bf16[128,2688]{1,0:T(8,128)(2,1)S(1)} %pad_maximum_fusion.2.refs_1_), channel_id=1, source_target_pairs={{0,1},{1,0},{2,3},{3,2},{4,5},{5,4},{6,7},{7,6},{8,9},{9,8},{10,11... | collective-permute-start | bytes 2064392 | tf_op jit(solution)/shard_map/ppermute | solution.py:17
  56.5 14.5 %collective-permute-start.18 = (bf16[64,2560]{1,0:T(8,128)(2,1)S(1)}, bf16[64,2560]{1,0:T(8,128)(2,1)S(1)}, u32[]{:S(2)}, u32[]{:S(2)}) collective-permute-start(bf16[64,2560]{1,0:T(8,128)(2,1)S(1)} %get-tuple-element.54), channel_id=1, source_target_pairs={{0,2},{1,3},{2,0},{3,1},{4,6},{5,7},{6,4},{7,5},{8,10},{9,11},{10,... | collective-permute-start | bytes 983048 | tf_op jit(solution)/shard_map/ppermute | solution.py:17
  62.2 6.6 %collective-permute-start.25 = (bf16[128,2560]{1,0:T(8,128)(2,1)S(1)}, bf16[128,2560]{1,0:T(8,128)(2,1)S(1)}, u32[]{:S(2)}, u32[]{:S(2)}) collective-permute-start(bf16[128,2560]{1,0:T(8,128)(2,1)S(1)} %get-tuple-element.51), channel_id=1, source_target_pairs={{0,1},{1,0},{2,3},{3,2},{4,5},{5,4},{6,7},{7,6},{8,9},{9,8},{10,11... | collective-permute-start | bytes 1966088 | tf_op jit(solution)/shard_map/ppermute | solution.py:17
  62.4 2.9 %collective-permute-start.16 = (bf16[128,2688]{1,0:T(8,128)(2,1)S(1)}, bf16[128,2688]{1,0:T(8,128)(2,1)S(1)}, u32[]{:S(2)}, u32[]{:S(2)}) collective-permute-start(bf16[128,2688]{1,0:T(8,128)(2,1)S(1)} %pad_maximum_fusion.1.refs_1_), channel_id=1, source_target_pairs={{0,1},{1,0},{2,3},{3,2},{4,5},{5,4},{6,7},{7,6},{8,9},{9,8},{10,11... | collective-permute-start | bytes 2064392 | tf_op jit(solution)/shard_map/ppermute | solution.py:17
  62.9 10.8 %collective-permute-start.22 = (bf16[64,2560]{1,0:T(8,128)(2,1)S(1)}, bf16[64,2560]{1,0:T(8,128)(2,1)S(1)}, u32[]{:S(2)}, u32[]{:S(2)}) collective-permute-start(bf16[64,2560]{1,0:T(8,128)(2,1)S(1)} %get-tuple-element.56), channel_id=1, source_target_pairs={{0,2},{1,3},{2,0},{3,1},{4,6},{5,7},{6,4},{7,5},{8,10},{9,11},{10,... | collective-permute-start | bytes 983048 | tf_op jit(solution)/shard_map/ppermute | solution.py:17
  68.6 2.2 %collective-permute-start.17 = (bf16[128,2560]{1,0:T(8,128)(2,1)S(1)}, bf16[128,2560]{1,0:T(8,128)(2,1)S(1)}, u32[]{:S(2)}, u32[]{:S(2)}) collective-permute-start(bf16[128,2560]{1,0:T(8,128)(2,1)S(1)} %get-tuple-element.45), channel_id=1, source_target_pairs={{0,1},{1,0},{2,3},{3,2},{4,5},{5,4},{6,7},{7,6},{8,9},{9,8},{10,11... | collective-permute-start | bytes 1966088 | tf_op jit(solution)/shard_map/ppermute | solution.py:17
  69.0 11.3 %collective-permute-start.26 = (bf16[64,2560]{1,0:T(8,128)(2,1)S(1)}, bf16[64,2560]{1,0:T(8,128)(2,1)S(1)}, u32[]{:S(2)}, u32[]{:S(2)}) collective-permute-start(bf16[64,2560]{1,0:T(8,128)(2,1)S(1)} %get-tuple-element.58), channel_id=1, source_target_pairs={{0,2},{1,3},{2,0},{3,1},{4,6},{5,7},{6,4},{7,5},{8,10},{9,11},{10,... | collective-permute-start | bytes 983048 | tf_op jit(solution)/shard_map/ppermute | solution.py:17
  71.0 10.9 %collective-permute-start.19 = (bf16[32,2560]{1,0:T(8,128)(2,1)S(1)}, bf16[32,2560]{1,0:T(8,128)(2,1)S(1)}, u32[]{:S(2)}, u32[]{:S(2)}) collective-permute-start(bf16[32,2560]{1,0:T(8,128)(2,1)S(1)} %get-tuple-element.62), channel_id=1, source_target_pairs={{0,4},{1,5},{2,6},{3,7},{4,0},{5,1},{6,2},{7,3},{8,12},{9,13},{10,... | collective-permute-start | bytes 491528 | tf_op jit(solution)/shard_map/ppermute | solution.py:17
  73.8 10.8 %collective-permute-start.23 = (bf16[32,2560]{1,0:T(8,128)(2,1)S(1)}, bf16[32,2560]{1,0:T(8,128)(2,1)S(1)}, u32[]{:S(2)}, u32[]{:S(2)}) collective-permute-start(bf16[32,2560]{1,0:T(8,128)(2,1)S(1)} %get-tuple-element.64), channel_id=1, source_target_pairs={{0,4},{1,5},{2,6},{3,7},{4,0},{5,1},{6,2},{7,3},{8,12},{9,13},{10,... | collective-permute-start | bytes 491528 | tf_op jit(solution)/shard_map/ppermute | solution.py:17
  80.4 7.2 %collective-permute-start.27 = (bf16[32,2560]{1,0:T(8,128)(2,1)S(1)}, bf16[32,2560]{1,0:T(8,128)(2,1)S(1)}, u32[]{:S(2)}, u32[]{:S(2)}) collective-permute-start(bf16[32,2560]{1,0:T(8,128)(2,1)S(1)} %get-tuple-element.66), channel_id=1, source_target_pairs={{0,4},{1,5},{2,6},{3,7},{4,0},{5,1},{6,2},{7,3},{8,12},{9,13},{10,... | collective-permute-start | bytes 491528 | tf_op jit(solution)/shard_map/ppermute | solution.py:17
  80.7 12.3 %collective-permute-start.29 = (bf16[64,2560]{1,0:T(8,128)(2,1)S(1)}, bf16[64,2560]{1,0:T(8,128)(2,1)S(1)}, u32[]{:S(2)}, u32[]{:S(2)}) collective-permute-start(bf16[64,2560]{1,0:T(8,128)(2,1)S(1)} %get-tuple-element.60), channel_id=1, source_target_pairs={{0,2},{1,3},{2,0},{3,1},{4,6},{5,7},{6,4},{7,5},{8,10},{9,11},{10,... | collective-permute-start | bytes 983048 | tf_op jit(solution)/shard_map/ppermute | solution.py:17
  81.9 11.0 %collective-permute-start.20 = (bf16[16,2560]{1,0:T(8,128)(2,1)S(1)}, bf16[16,2560]{1,0:T(8,128)(2,1)S(1)}, u32[]{:S(2)}, u32[]{:S(2)}) collective-permute-start(bf16[16,2560]{1,0:T(8,128)(2,1)S(1)} %add_convert_fusion.26), channel_id=1, source_target_pairs={{0,8},{1,9},{2,10},{3,11},{4,12},{5,13},{6,14},{7,15},{8,0},{9,1},... | collective-permute-start | bytes 245768 | tf_op jit(solution)/shard_map/ppermute | solution.py:17
  84.6 10.1 %collective-permute-start.24 = (bf16[16,2560]{1,0:T(8,128)(2,1)S(1)}, bf16[16,2560]{1,0:T(8,128)(2,1)S(1)}, u32[]{:S(2)}, u32[]{:S(2)}) collective-permute-start(bf16[16,2560]{1,0:T(8,128)(2,1)S(1)} %add_convert_fusion.23), channel_id=1, source_target_pairs={{0,8},{1,9},{2,10},{3,11},{4,12},{5,13},{6,14},{7,15},{8,0},{9,1},... | collective-permute-start | bytes 245768 | tf_op jit(solution)/shard_map/ppermute | solution.py:17
  87.6 12.0 %collective-permute-start.28 = (bf16[16,2560]{1,0:T(8,128)(2,1)S(1)}, bf16[16,2560]{1,0:T(8,128)(2,1)S(1)}, u32[]{:S(2)}, u32[]{:S(2)}) collective-permute-start(bf16[16,2560]{1,0:T(8,128)(2,1)S(1)} %add_convert_fusion.20), channel_id=1, source_target_pairs={{0,8},{1,9},{2,10},{3,11},{4,12},{5,13},{6,14},{7,15},{8,0},{9,1},... | collective-permute-start | bytes 245768 | tf_op jit(solution)/shard_map/ppermute | solution.py:17
  93.1 5.4 %collective-permute-start.30 = (bf16[32,2560]{1,0:T(8,128)(2,1)S(1)}, bf16[32,2560]{1,0:T(8,128)(2,1)S(1)}, u32[]{:S(2)}, u32[]{:S(2)}) collective-permute-start(bf16[32,2560]{1,0:T(8,128)(2,1)S(1)} %get-tuple-element.68), channel_id=1, source_target_pairs={{0,4},{1,5},{2,6},{3,7},{4,0},{5,1},{6,2},{7,3},{8,12},{9,13},{10,... | collective-permute-start | bytes 491528 | tf_op jit(solution)/shard_map/ppermute | solution.py:17
  98.5 5.9 %collective-permute-start.31 = (bf16[16,2560]{1,0:T(8,128)(2,1)S(1)}, bf16[16,2560]{1,0:T(8,128)(2,1)S(1)}, u32[]{:S(2)}, u32[]{:S(2)}) collective-permute-start(bf16[16,2560]{1,0:T(8,128)(2,1)S(1)} %add_convert_fusion.17), channel_id=1, source_target_pairs={{0,8},{1,9},{2,10},{3,11},{4,12},{5,13},{6,14},{7,15},{8,0},{9,1},... | collective-permute-start | bytes 245768 | tf_op jit(solution)/shard_map/ppermute | solution.py:17
  (8 other events, 28.6 us)

commit v4 on v3

--- a/solution.py
+++ b/solution.py
@@ -149,7 +149,8 @@
     bits = [1 << i for i in reversed(range(axis_size.bit_length() - 1))]
     beside, last = bits[-2:]
     outward = bits
-    gathers = [outward] * PIECES
+    early = [beside] + bits[:-2] + [last]
+    gathers = [outward] * (PIECES - 1) + [early]
     scatters = [outward[::-1]] * PIECES
 
     rows = hidden_states.reshape(step_count * row_count, feature_width)
@@ -166,17 +167,30 @@
         got[piece, stage] = held[piece]
 
     final = len(bits) - 1
+    sums, crossed = [None] * PIECES, {}
+
+    def cross(piece, *ties):
+        near = after(held[piece], *ties) if ties else held[piece]
+        crossed[piece] = near, swap(near, axis_size, last)
+
+    def work(piece, *late):
+        near, far = crossed[piece]
+        near = after(near, *late) if late else near
+        sums[piece] = expert_rows(near, far, experts, places_of(gathers[piece], scatters[piece]), *matrices)
+
+    for piece in (0, 1):
+        for stage in range(final):
+            grow(piece, stage, *((got[0, 0],) if (piece, stage) == (1, 0) else ()))
+    grow(PIECES - 1, 0)
+
+    grow(2, 0, got[0, final - 2])
+    for stage in range(1, final):
+        grow(2, stage)
+    for stage in range(1, final):
+        grow(3, stage, *((got[1, final - 2],) if stage == 1 else ()))
     for piece in range(PIECES):
-        ties = () if piece == 0 else (got[0, 0],) if piece == 1 else (got[piece - 2, final - 2],)
-        grow(piece, 0, *ties)
-        for stage in range(1, final):
-            grow(piece, stage)
-    sums = []
-    for piece in range(PIECES):
-        near = after(held[piece], sums[-1][0]) if sums else held[piece]
-        far = swap(near, axis_size, last)
-        places = places_of(gathers[piece], scatters[piece])
-        sums.append(expert_rows(near, far, experts, places, *matrices))
+        cross(piece, *((sums[piece - 2][0],) if piece >= 2 else ()))
+        work(piece)
 
     def shrink(piece, stage, *late):
         keep, send = sums[piece]

time: 105 us -> 97.1 us (0.925)
  waiting for transfers between devices: 54 us -> 34.6 us
  starting transfers between devices: 28.5 us -> 39.4 us
    ppermute x32, waiting for transfers between devices: 54 us -> 34.6 us  [swap(): lax.ppermute(array, 'expert', [(i, i ^ bit) for i in range(axis_size)])]
    ppermute x32, starting transfers between devices: 28.5 us -> 39.4 us  [swap(): lax.ppermute(array, 'expert', [(i, i ^ bit) for i in range(axis_size)])]
    unnamed x21 -> x22, local copies, waits for them, and re-layouts: 6.7 us -> 6.75 us
  transfers between devices with their start and end apart: 32 -> 32, of which waited for: 20 -> 16; matrix products, arithmetic and copies ran while one was open for 1% -> 2% of each run, Pallas kernels for 12% -> 14%
where the time goes in v4:
time: 97.1 us; the launch traced here: 96.8 us
  starting transfers between devices  39.4 us (41%)
  waiting for transfers between devices  34.6 us (36%)
  Pallas kernels  13.6 us (14%)
  local copies, waits for them, and re-layouts  6.81 us (7%)
  other arithmetic  2.12 us (2%)
    ppermute x32, starting transfers between devices, swap(): lax.ppermute(array, 'expert', [(i, i ^ bit) for i in range(axis_size)])  39.4 us
    ppermute x32, waiting for transfers between devices, swap(): lax.ppermute(array, 'expert', [(i, i ^ bit) for i in range(axis_size)])  34.6 us
    pallas_call x4, Pallas kernels, expert_rows(): pl.pallas_call(lambda *refs: expert_kernel(experts, places, *refs), out_s...  13.2 us
    unnamed x22, local copies, waits for them, and re-layouts  6.75 us
  transfers between devices with their start and end apart: 32, of which 16 were waited for; matrix products, arithmetic and copies ran while one was open for 2% of the time, Pallas kernels for 14%

profile of v4, /device:TPU:0, one launch (start us, length us, event | category | flops | bytes accessed | tf_op | source)
XLA Modules:
  0.0 96.8 jit_solution(12696119143436641374)
XLA Ops:
  2.8 4.1 %collective-permute-start = (bf16[16,2688]{1,0:T(8,128)(2,1)S(1)}, bf16[16,2688]{1,0:T(8,128)(2,1)S(1)}, u32[]{:S(2)}, u32[]{:S(2)}) collective-permute-start(bf16[16,2688]{1,0:T(8,128)(2,1)S(1)} %get-tuple-element.28), channel_id=1, source_target_pairs={{0,8},{1,9},{2,10},{3,11},{4,12},{5,13},{6,14},{7,15},{8,0},{9,1},... | collective-permute-start | bytes 258056 | tf_op jit(solution)/shard_map/ppermute | solution.py:17
  6.9 1.5 %collective-permute-start.9 = (bf16[16,2688]{1,0:T(8,128)(2,1)S(1)}, bf16[16,2688]{1,0:T(8,128)(2,1)S(1)}, u32[]{:S(2)}, u32[]{:S(2)}) collective-permute-start(bf16[16,2688]{1,0:T(8,128)(2,1)S(1)} %get-tuple-element.35), channel_id=1, source_target_pairs={{0,2},{1,3},{2,0},{3,1},{4,6},{5,7},{6,4},{7,5},{8,10},{9,11},{10,... | collective-permute-start | bytes 258056 | tf_op jit(solution)/shard_map/ppermute | solution.py:17
  8.5 2.8 %collective-permute-done = bf16[16,2688]{1,0:T(8,128)(2,1)S(1)} collective-permute-done((bf16[16,2688]{1,0:T(8,128)(2,1)S(1)}, bf16[16,2688]{1,0:T(8,128)(2,1)S(1)}, u32[]{:S(2)}, u32[]{:S(2)}) %collective-permute-start) | collective-permute-done | bytes 86048 | tf_op jit(solution)/shard_map/ppermute | solution.py:17
  12.1 3.4 %collective-permute-start.4 = (bf16[16,2688]{1,0:T(8,128)(2,1)S(1)}, bf16[16,2688]{1,0:T(8,128)(2,1)S(1)}, u32[]{:S(2)}, u32[]{:S(2)}) collective-permute-start(bf16[16,2688]{1,0:T(8,128)(2,1)S(1)} %get-tuple-element.31), channel_id=1, source_target_pairs={{0,8},{1,9},{2,10},{3,11},{4,12},{5,13},{6,14},{7,15},{8,0},{9,1},... | collective-permute-start | bytes 258056 | tf_op jit(solution)/shard_map/ppermute | solution.py:17
  15.5 2.5 %collective-permute-done.4 = bf16[16,2688]{1,0:T(8,128)(2,1)S(1)} collective-permute-done((bf16[16,2688]{1,0:T(8,128)(2,1)S(1)}, bf16[16,2688]{1,0:T(8,128)(2,1)S(1)}, u32[]{:S(2)}, u32[]{:S(2)}) %collective-permute-start.4) | collective-permute-done | bytes 86048 | tf_op jit(solution)/shard_map/ppermute | solution.py:17
  18.0 3.8 %collective-permute-start.5 = (bf16[32,2688]{1,0:T(8,128)(2,1)S(1)}, bf16[32,2688]{1,0:T(8,128)(2,1)S(1)}, u32[]{:S(2)}, u32[]{:S(2)}) collective-permute-start(bf16[32,2688]{1,0:T(8,128)(2,1)S(1)} %pad_maximum_fusion.5), channel_id=1, source_target_pairs={{0,4},{1,5},{2,6},{3,7},{4,0},{5,1},{6,2},{7,3},{8,12},{9,13},{10,... | collective-permute-start | bytes 516104 | tf_op jit(solution)/shard_map/ppermute | solution.py:17
  22.0 1.6 %collective-permute-start.2 = (bf16[64,2688]{1,0:T(8,128)(2,1)S(1)}, bf16[64,2688]{1,0:T(8,128)(2,1)S(1)}, u32[]{:S(2)}, u32[]{:S(2)}) collective-permute-start(bf16[64,2688]{1,0:T(8,128)(2,1)S(1)} %get-tuple-element.68), channel_id=1, source_target_pairs={{0,2},{1,3},{2,0},{3,1},{4,6},{5,7},{6,4},{7,5},{8,10},{9,11},{10,... | collective-permute-start | bytes 1032200 | tf_op jit(solution)/shard_map/ppermute | solution.py:17
  24.7 1.3 %collective-permute-done.5 = bf16[32,2688]{1,0:T(8,128)(2,1)S(1)} collective-permute-done((bf16[32,2688]{1,0:T(8,128)(2,1)S(1)}, bf16[32,2688]{1,0:T(8,128)(2,1)S(1)}, u32[]{:S(2)}, u32[]{:S(2)}) %collective-permute-start.5) | collective-permute-done | bytes 172064 | tf_op jit(solution)/shard_map/ppermute | solution.py:17
  26.0 2.3 %collective-permute-start.6 = (bf16[64,2688]{1,0:T(8,128)(2,1)S(1)}, bf16[64,2688]{1,0:T(8,128)(2,1)S(1)}, u32[]{:S(2)}, u32[]{:S(2)}) collective-permute-start(bf16[64,2688]{1,0:T(8,128)(2,1)S(1)} %get-tuple-element.70), channel_id=1, source_target_pairs={{0,2},{1,3},{2,0},{3,1},{4,6},{5,7},{6,4},{7,5},{8,10},{9,11},{10,... | collective-permute-start | bytes 1032200 | tf_op jit(solution)/shard_map/ppermute | solution.py:17
  29.5 1.5 %collective-permute-start.18 = (bf16[32,2688]{1,0:T(8,128)(2,1)S(1)}, bf16[32,2688]{1,0:T(8,128)(2,1)S(1)}, u32[]{:S(2)}, u32[]{:S(2)}) collective-permute-start(bf16[32,2688]{1,0:T(8,128)(2,1)S(1)} %pad_maximum_fusion.7), channel_id=1, source_target_pairs={{0,4},{1,5},{2,6},{3,7},{4,0},{5,1},{6,2},{7,3},{8,12},{9,13},{10,... | collective-permute-start | bytes 516104 | tf_op jit(solution)/shard_map/ppermute | solution.py:17
  31.0 6.0 %collective-permute-done.10 = bf16[32,2688]{1,0:T(8,128)(2,1)S(1)} collective-permute-done((bf16[32,2688]{1,0:T(8,128)(2,1)S(1)}, bf16[32,2688]{1,0:T(8,128)(2,1)S(1)}, u32[]{:S(2)}, u32[]{:S(2)}) %collective-permute-start.10) | collective-permute-done | bytes 172064 | tf_op jit(solution)/shard_map/ppermute | solution.py:17
  37.2 1.6 %collective-permute-done.18 = bf16[32,2688]{1,0:T(8,128)(2,1)S(1)} collective-permute-done((bf16[32,2688]{1,0:T(8,128)(2,1)S(1)}, bf16[32,2688]{1,0:T(8,128)(2,1)S(1)}, u32[]{:S(2)}, u32[]{:S(2)}) %collective-permute-start.18) | collective-permute-done | bytes 172064 | tf_op jit(solution)/shard_map/ppermute | solution.py:17
  39.3 2.1 %copy-done.1 = bf16[1,2560,768]{2,1,0:T(8,128)(2,1)S(1)} copy-done((bf16[1,2560,768]{2,1,0:T(8,128)(2,1)S(1)}, bf16[1,2560,768]{2,1,0:T(8,128)(2,1)}, u32[]{:S(2)}) %copy-start.1) | copy-done | bytes 3932184
  41.4 2.1 %copy-done.3 = bf16[1,768,2560]{2,1,0:T(8,128)(2,1)S(1)} copy-done((bf16[1,768,2560]{2,1,0:T(8,128)(2,1)S(1)}, bf16[1,768,2560]{2,1,0:T(8,128)(2,1)}, u32[]{:S(2)}) %copy-start.3) | copy-done | bytes 3932184
  43.5 3.3 %shard_map.65 = (bf16[128,2560]{1,0:T(8,128)(2,1)S(1)}, bf16[128,2560]{1,0:T(8,128)(2,1)S(1)}) custom-call(s32[1]{0:T(128)} %bitcast.refs_0_, bf16[128,2688]{1,0:T(8,128)(2,1)S(1)} %constant_dynamic-update-slice_fusion.5.refs_1_, bf16[128,2688]{1,0:T(8,128)(2,1)S(1)} %collective-permute-done.3.refs_2_, bf16[2560,768]{1,0:T(8,128)(2,1)S(1)} %bitcast.8, ...), custom_call_target="tpu_custom_call" | custom-call | flops 1000 | bytes 1000 | tf_op jit(solution)/shard_map/pallas_call | solution.py:126
  47.9 3.3 %shard_map.66 = (bf16[128,2560]{1,0:T(8,128)(2,1)S(1)}, bf16[128,2560]{1,0:T(8,128)(2,1)S(1)}) custom-call(s32[1]{0:T(128)} %bitcast.refs_0_, bf16[128,2688]{1,0:T(8,128)(2,1)S(1)} %constant_dynamic-update-slice_fusion.12.refs_1_, bf16[128,2688]{1,0:T(8,128)(2,1)S(1)} %collective-permute-done.7.refs_2_, bf16[2560,768]{1,0:T(8,128)(2,1)S(1)} %bitcast.9, ...), custom_call_target="tpu_custom_call" | custom-call | flops 1000 | bytes 1000 | tf_op jit(solution)/shard_map/pallas_call | solution.py:126
  52.0 1.5 %collective-permute-start.14 = (bf16[64,2560]{1,0:T(8,128)(2,1)S(1)}, bf16[64,2560]{1,0:T(8,128)(2,1)S(1)}, u32[]{:S(2)}, u32[]{:S(2)}) collective-permute-start(bf16[64,2560]{1,0:T(8,128)(2,1)S(1)} %get-tuple-element.52), channel_id=1, source_target_pairs={{0,2},{1,3},{2,0},{3,1},{4,6},{5,7},{6,4},{7,5},{8,10},{9,11},{10,... | collective-permute-start | bytes 983048 | tf_op jit(solution)/shard_map/ppermute | solution.py:17
  53.5 3.3 %shard_map.68 = (bf16[128,2560]{1,0:T(8,128)(2,1)S(1)}, bf16[128,2560]{1,0:T(8,128)(2,1)S(1)}) custom-call(s32[1]{0:T(128)} %bitcast.refs_0_, bf16[128,2688]{1,0:T(8,128)(2,1)S(1)} %pad_maximum_fusion.1.refs_1_, bf16[128,2688]{1,0:T(8,128)(2,1)S(1)} %collective-permute-done.20.refs_2_, bf16[2560,768]{1,0:T(8,128)(2,1)S(1)} %bitcast.10, ...), custom_call_target="tpu_custom_call" | custom-call | flops 1000 | bytes 1000 | tf_op jit(solution)/shard_map/pallas_call | solution.py:126
  57.8 3.3 %shard_map.67 = (bf16[128,2560]{1,0:T(8,128)(2,1)S(1)}, bf16[128,2560]{1,0:T(8,128)(2,1)S(1)}) custom-call(s32[1]{0:T(128)} %bitcast.refs_0_, bf16[128,2688]{1,0:T(8,128)(2,1)S(1)} %pad_maximum_fusion.refs_1_, bf16[128,2688]{1,0:T(8,128)(2,1)S(1)} %collective-permute-done.12.refs_2_, bf16[2560,768]{1,0:T(8,128)(2,1)S(1)} %bitcast.11, ...), custom_call_target="tpu_custom_call" | custom-call | flops 1000 | bytes 1000 | tf_op jit(solution)/shard_map/pallas_call | solution.py:126
  61.4 1.5 %collective-permute-start.26 = (bf16[64,2560]{1,0:T(8,128)(2,1)S(1)}, bf16[64,2560]{1,0:T(8,128)(2,1)S(1)}, u32[]{:S(2)}, u32[]{:S(2)}) collective-permute-start(bf16[64,2560]{1,0:T(8,128)(2,1)S(1)} %get-tuple-element.56), channel_id=1, source_target_pairs={{0,2},{1,3},{2,0},{3,1},{4,6},{5,7},{6,4},{7,5},{8,10},{9,11},{10,... | collective-permute-start | bytes 983048 | tf_op jit(solution)/shard_map/ppermute | solution.py:17
  63.5 2.1 %collective-permute-start.15 = (bf16[32,2560]{1,0:T(8,128)(2,1)S(1)}, bf16[32,2560]{1,0:T(8,128)(2,1)S(1)}, u32[]{:S(2)}, u32[]{:S(2)}) collective-permute-start(bf16[32,2560]{1,0:T(8,128)(2,1)S(1)} %get-tuple-element.60), channel_id=1, source_target_pairs={{0,4},{1,5},{2,6},{3,7},{4,0},{5,1},{6,2},{7,3},{8,12},{9,13},{10,... | collective-permute-start | bytes 491528 | tf_op jit(solution)/shard_map/ppermute | solution.py:17
  65.6 4.0 %collective-permute-done.22 = bf16[64,2560]{1,0:T(8,128)(2,1)S(1)} collective-permute-done((bf16[64,2560]{1,0:T(8,128)(2,1)S(1)}, bf16[64,2560]{1,0:T(8,128)(2,1)S(1)}, u32[]{:S(2)}, u32[]{:S(2)}) %collective-permute-start.22) | collective-permute-done | bytes 327712 | tf_op jit(solution)/shard_map/ppermute | solution.py:17
  69.7 2.1 %collective-permute-start.23 = (bf16[32,2560]{1,0:T(8,128)(2,1)S(1)}, bf16[32,2560]{1,0:T(8,128)(2,1)S(1)}, u32[]{:S(2)}, u32[]{:S(2)}) collective-permute-start(bf16[32,2560]{1,0:T(8,128)(2,1)S(1)} %get-tuple-element.62), channel_id=1, source_target_pairs={{0,4},{1,5},{2,6},{3,7},{4,0},{5,1},{6,2},{7,3},{8,12},{9,13},{10,... | collective-permute-start | bytes 491528 | tf_op jit(solution)/shard_map/ppermute | solution.py:17
  72.6 1.2 %collective-permute-start.16 = (bf16[16,2560]{1,0:T(8,128)(2,1)S(1)}, bf16[16,2560]{1,0:T(8,128)(2,1)S(1)}, u32[]{:S(2)}, u32[]{:S(2)}) collective-permute-start(bf16[16,2560]{1,0:T(8,128)(2,1)S(1)} %add_convert_fusion.26), channel_id=1, source_target_pairs={{0,8},{1,9},{2,10},{3,11},{4,12},{5,13},{6,14},{7,15},{8,0},{9,1},... | collective-permute-start | bytes 245768 | tf_op jit(solution)/shard_map/ppermute | solution.py:17
  73.8 2.3 %collective-permute-done.23 = bf16[32,2560]{1,0:T(8,128)(2,1)S(1)} collective-permute-done((bf16[32,2560]{1,0:T(8,128)(2,1)S(1)}, bf16[32,2560]{1,0:T(8,128)(2,1)S(1)}, u32[]{:S(2)}, u32[]{:S(2)}) %collective-permute-start.23) | collective-permute-done | bytes 163872 | tf_op jit(solution)/shard_map/ppermute | solution.py:17
  76.1 2.2 %collective-permute-start.24 = (bf16[16,2560]{1,0:T(8,128)(2,1)S(1)}, bf16[16,2560]{1,0:T(8,128)(2,1)S(1)}, u32[]{:S(2)}, u32[]{:S(2)}) collective-permute-start(bf16[16,2560]{1,0:T(8,128)(2,1)S(1)} %add_convert_fusion.23), channel_id=1, source_target_pairs={{0,8},{1,9},{2,10},{3,11},{4,12},{5,13},{6,14},{7,15},{8,0},{9,1},... | collective-permute-start | bytes 245768 | tf_op jit(solution)/shard_map/ppermute | solution.py:17
  78.8 1.7 %collective-permute-done.16 = bf16[16,2560]{1,0:T(8,128)(2,1)S(1)} collective-permute-done((bf16[16,2560]{1,0:T(8,128)(2,1)S(1)}, bf16[16,2560]{1,0:T(8,128)(2,1)S(1)}, u32[]{:S(2)}, u32[]{:S(2)}) %collective-permute-start.16) | collective-permute-done | bytes 81952 | tf_op jit(solution)/shard_map/ppermute | solution.py:17
  81.6 1.6 %collective-permute-done.29 = bf16[64,2560]{1,0:T(8,128)(2,1)S(1)} collective-permute-done((bf16[64,2560]{1,0:T(8,128)(2,1)S(1)}, bf16[64,2560]{1,0:T(8,128)(2,1)S(1)}, u32[]{:S(2)}, u32[]{:S(2)}) %collective-permute-start.29) | collective-permute-done | bytes 327712 | tf_op jit(solution)/shard_map/ppermute | solution.py:17
  83.3 2.1 %collective-permute-start.30 = (bf16[32,2560]{1,0:T(8,128)(2,1)S(1)}, bf16[32,2560]{1,0:T(8,128)(2,1)S(1)}, u32[]{:S(2)}, u32[]{:S(2)}) collective-permute-start(bf16[32,2560]{1,0:T(8,128)(2,1)S(1)} %get-tuple-element.66), channel_id=1, source_target_pairs={{0,4},{1,5},{2,6},{3,7},{4,0},{5,1},{6,2},{7,3},{8,12},{9,13},{10,... | collective-permute-start | bytes 491528 | tf_op jit(solution)/shard_map/ppermute | solution.py:17
  85.8 4.8 %collective-permute-done.30 = bf16[32,2560]{1,0:T(8,128)(2,1)S(1)} collective-permute-done((bf16[32,2560]{1,0:T(8,128)(2,1)S(1)}, bf16[32,2560]{1,0:T(8,128)(2,1)S(1)}, u32[]{:S(2)}, u32[]{:S(2)}) %collective-permute-start.30) | collective-permute-done | bytes 163872 | tf_op jit(solution)/shard_map/ppermute | solution.py:17
  90.6 1.8 %collective-permute-start.31 = (bf16[16,2560]{1,0:T(8,128)(2,1)S(1)}, bf16[16,2560]{1,0:T(8,128)(2,1)S(1)}, u32[]{:S(2)}, u32[]{:S(2)}) collective-permute-start(bf16[16,2560]{1,0:T(8,128)(2,1)S(1)} %add_convert_fusion.17), channel_id=1, source_target_pairs={{0,8},{1,9},{2,10},{3,11},{4,12},{5,13},{6,14},{7,15},{8,0},{9,1},... | collective-permute-start | bytes 245768 | tf_op jit(solution)/shard_map/ppermute | solution.py:17
  92.4 3.6 %collective-permute-done.31 = bf16[16,2560]{1,0:T(8,128)(2,1)S(1)} collective-permute-done((bf16[16,2560]{1,0:T(8,128)(2,1)S(1)}, bf16[16,2560]{1,0:T(8,128)(2,1)S(1)}, u32[]{:S(2)}, u32[]{:S(2)}) %collective-permute-start.31) | collective-permute-done | bytes 81952 | tf_op jit(solution)/shard_map/ppermute | solution.py:17
  (85 shorter events, 14.4 us)
Async XLA Ops:
  2.8 8.5 %collective-permute-start = (bf16[16,2688]{1,0:T(8,128)(2,1)S(1)}, bf16[16,2688]{1,0:T(8,128)(2,1)S(1)}, u32[]{:S(2)}, u32[]{:S(2)}) collective-permute-start(bf16[16,2688]{1,0:T(8,128)(2,1)S(1)} %get-tuple-element.28), channel_id=1, source_target_pairs={{0,8},{1,9},{2,10},{3,11},{4,12},{5,13},{6,14},{7,15},{8,0},{9,1},... | collective-permute-start | bytes 258056 | tf_op jit(solution)/shard_map/ppermute | solution.py:17
  6.9 8.6 %collective-permute-start.9 = (bf16[16,2688]{1,0:T(8,128)(2,1)S(1)}, bf16[16,2688]{1,0:T(8,128)(2,1)S(1)}, u32[]{:S(2)}, u32[]{:S(2)}) collective-permute-start(bf16[16,2688]{1,0:T(8,128)(2,1)S(1)} %get-tuple-element.35), channel_id=1, source_target_pairs={{0,2},{1,3},{2,0},{3,1},{4,6},{5,7},{6,4},{7,5},{8,10},{9,11},{10,... | collective-permute-start | bytes 258056 | tf_op jit(solution)/shard_map/ppermute | solution.py:17
  11.3 10.6 %collective-permute-start.1 = (bf16[32,2688]{1,0:T(8,128)(2,1)S(1)}, bf16[32,2688]{1,0:T(8,128)(2,1)S(1)}, u32[]{:S(2)}, u32[]{:S(2)}) collective-permute-start(bf16[32,2688]{1,0:T(8,128)(2,1)S(1)} %get-tuple-element.73), channel_id=1, source_target_pairs={{0,4},{1,5},{2,6},{3,7},{4,0},{5,1},{6,2},{7,3},{8,12},{9,13},{10,... | collective-permute-start | bytes 516104 | tf_op jit(solution)/shard_map/ppermute | solution.py:17
  12.1 5.9 %collective-permute-start.4 = (bf16[16,2688]{1,0:T(8,128)(2,1)S(1)}, bf16[16,2688]{1,0:T(8,128)(2,1)S(1)}, u32[]{:S(2)}, u32[]{:S(2)}) collective-permute-start(bf16[16,2688]{1,0:T(8,128)(2,1)S(1)} %get-tuple-element.31), channel_id=1, source_target_pairs={{0,8},{1,9},{2,10},{3,11},{4,12},{5,13},{6,14},{7,15},{8,0},{9,1},... | collective-permute-start | bytes 258056 | tf_op jit(solution)/shard_map/ppermute | solution.py:17
  18.0 7.9 %collective-permute-start.5 = (bf16[32,2688]{1,0:T(8,128)(2,1)S(1)}, bf16[32,2688]{1,0:T(8,128)(2,1)S(1)}, u32[]{:S(2)}, u32[]{:S(2)}) collective-permute-start(bf16[32,2688]{1,0:T(8,128)(2,1)S(1)} %pad_maximum_fusion.5), channel_id=1, source_target_pairs={{0,4},{1,5},{2,6},{3,7},{4,0},{5,1},{6,2},{7,3},{8,12},{9,13},{10,... | collective-permute-start | bytes 516104 | tf_op jit(solution)/shard_map/ppermute | solution.py:17
  22.0 15.1 %collective-permute-start.2 = (bf16[64,2688]{1,0:T(8,128)(2,1)S(1)}, bf16[64,2688]{1,0:T(8,128)(2,1)S(1)}, u32[]{:S(2)}, u32[]{:S(2)}) collective-permute-start(bf16[64,2688]{1,0:T(8,128)(2,1)S(1)} %get-tuple-element.68), channel_id=1, source_target_pairs={{0,2},{1,3},{2,0},{3,1},{4,6},{5,7},{6,4},{7,5},{8,10},{9,11},{10,... | collective-permute-start | bytes 1032200 | tf_op jit(solution)/shard_map/ppermute | solution.py:17
  23.5 5.9 %collective-permute-start.17 = (bf16[16,2688]{1,0:T(8,128)(2,1)S(1)}, bf16[16,2688]{1,0:T(8,128)(2,1)S(1)}, u32[]{:S(2)}, u32[]{:S(2)}) collective-permute-start(bf16[16,2688]{1,0:T(8,128)(2,1)S(1)} %get-tuple-element.42), channel_id=1, source_target_pairs={{0,8},{1,9},{2,10},{3,11},{4,12},{5,13},{6,14},{7,15},{8,0},{9,1},... | collective-permute-start | bytes 258056 | tf_op jit(solution)/shard_map/ppermute | solution.py:17
  26.0 12.9 %collective-permute-start.6 = (bf16[64,2688]{1,0:T(8,128)(2,1)S(1)}, bf16[64,2688]{1,0:T(8,128)(2,1)S(1)}, u32[]{:S(2)}, u32[]{:S(2)}) collective-permute-start(bf16[64,2688]{1,0:T(8,128)(2,1)S(1)} %get-tuple-element.70), channel_id=1, source_target_pairs={{0,2},{1,3},{2,0},{3,1},{4,6},{5,7},{6,4},{7,5},{8,10},{9,11},{10,... | collective-permute-start | bytes 1032200 | tf_op jit(solution)/shard_map/ppermute | solution.py:17
  28.3 8.6 %collective-permute-start.10 = (bf16[32,2688]{1,0:T(8,128)(2,1)S(1)}, bf16[32,2688]{1,0:T(8,128)(2,1)S(1)}, u32[]{:S(2)}, u32[]{:S(2)}) collective-permute-start(bf16[32,2688]{1,0:T(8,128)(2,1)S(1)} %pad_maximum_fusion.6), channel_id=1, source_target_pairs={{0,8},{1,9},{2,10},{3,11},{4,12},{5,13},{6,14},{7,15},{8,0},{9,1},... | collective-permute-start | bytes 516104 | tf_op jit(solution)/shard_map/ppermute | solution.py:17
  29.5 9.3 %collective-permute-start.18 = (bf16[32,2688]{1,0:T(8,128)(2,1)S(1)}, bf16[32,2688]{1,0:T(8,128)(2,1)S(1)}, u32[]{:S(2)}, u32[]{:S(2)}) collective-permute-start(bf16[32,2688]{1,0:T(8,128)(2,1)S(1)} %pad_maximum_fusion.7), channel_id=1, source_target_pairs={{0,4},{1,5},{2,6},{3,7},{4,0},{5,1},{6,2},{7,3},{8,12},{9,13},{10,... | collective-permute-start | bytes 516104 | tf_op jit(solution)/shard_map/ppermute | solution.py:17
  37.0 10.2 %collective-permute-start.11 = (bf16[64,2688]{1,0:T(8,128)(2,1)S(1)}, bf16[64,2688]{1,0:T(8,128)(2,1)S(1)}, u32[]{:S(2)}, u32[]{:S(2)}) collective-permute-start(bf16[64,2688]{1,0:T(8,128)(2,1)S(1)} %pad_maximum_fusion.2), channel_id=1, source_target_pairs={{0,4},{1,5},{2,6},{3,7},{4,0},{5,1},{6,2},{7,3},{8,12},{9,13},{10,... | collective-permute-start | bytes 1032200 | tf_op jit(solution)/shard_map/ppermute | solution.py:17
  37.1 2.2 %collective-permute-start.3 = (bf16[128,2688]{1,0:T(8,128)(2,1)S(1)}, bf16[128,2688]{1,0:T(8,128)(2,1)S(1)}, u32[]{:S(2)}, u32[]{:S(2)}) collective-permute-start(bf16[128,2688]{1,0:T(8,128)(2,1)S(1)} %constant_dynamic-update-slice_fusion.5.refs_1_), channel_id=1, source_target_pairs={{0,1},{1,0},{2,3},{3,2},{4,5},{5,4},{6,7},{7,6},{8,9},{9,8},{10,11... | collective-permute-start | bytes 2064392 | tf_op jit(solution)/shard_map/ppermute | solution.py:17
  38.8 8.9 %collective-permute-start.19 = (bf16[64,2688]{1,0:T(8,128)(2,1)S(1)}, bf16[64,2688]{1,0:T(8,128)(2,1)S(1)}, u32[]{:S(2)}, u32[]{:S(2)}) collective-permute-start(bf16[64,2688]{1,0:T(8,128)(2,1)S(1)} %pad_maximum_fusion.3), channel_id=1, source_target_pairs={{0,2},{1,3},{2,0},{3,1},{4,6},{5,7},{6,4},{7,5},{8,10},{9,11},{10,... | collective-permute-start | bytes 1032200 | tf_op jit(solution)/shard_map/ppermute | solution.py:17
  39.0 8.9 %collective-permute-start.7 = (bf16[128,2688]{1,0:T(8,128)(2,1)S(1)}, bf16[128,2688]{1,0:T(8,128)(2,1)S(1)}, u32[]{:S(2)}, u32[]{:S(2)}) collective-permute-start(bf16[128,2688]{1,0:T(8,128)(2,1)S(1)} %constant_dynamic-update-slice_fusion.12.refs_1_), channel_id=1, source_target_pairs={{0,1},{1,0},{2,3},{3,2},{4,5},{5,4},{6,7},{7,6},{8,9},{9,8},{10,11... | collective-permute-start | bytes 2064392 | tf_op jit(solution)/shard_map/ppermute | solution.py:17
  46.9 5.0 %collective-permute-start.8 = (bf16[128,2560]{1,0:T(8,128)(2,1)S(1)}, bf16[128,2560]{1,0:T(8,128)(2,1)S(1)}, u32[]{:S(2)}, u32[]{:S(2)}) collective-permute-start(bf16[128,2560]{1,0:T(8,128)(2,1)S(1)} %get-tuple-element.34), channel_id=1, source_target_pairs={{0,1},{1,0},{2,3},{3,2},{4,5},{5,4},{6,7},{7,6},{8,9},{9,8},{10,11... | collective-permute-start | bytes 1966088 | tf_op jit(solution)/shard_map/ppermute | solution.py:17
  47.8 5.7 %collective-permute-start.20 = (bf16[128,2688]{1,0:T(8,128)(2,1)S(1)}, bf16[128,2688]{1,0:T(8,128)(2,1)S(1)}, u32[]{:S(2)}, u32[]{:S(2)}) collective-permute-start(bf16[128,2688]{1,0:T(8,128)(2,1)S(1)} %pad_maximum_fusion.1.refs_1_), channel_id=1, source_target_pairs={{0,1},{1,0},{2,3},{3,2},{4,5},{5,4},{6,7},{7,6},{8,9},{9,8},{10,11... | collective-permute-start | bytes 2064392 | tf_op jit(solution)/shard_map/ppermute | solution.py:17
  51.2 6.6 %collective-permute-start.12 = (bf16[128,2688]{1,0:T(8,128)(2,1)S(1)}, bf16[128,2688]{1,0:T(8,128)(2,1)S(1)}, u32[]{:S(2)}, u32[]{:S(2)}) collective-permute-start(bf16[128,2688]{1,0:T(8,128)(2,1)S(1)} %pad_maximum_fusion.refs_1_), channel_id=1, source_target_pairs={{0,1},{1,0},{2,3},{3,2},{4,5},{5,4},{6,7},{7,6},{8,9},{9,8},{10,11... | collective-permute-start | bytes 2064392 | tf_op jit(solution)/shard_map/ppermute | solution.py:17
  51.8 5.3 %collective-permute-start.21 = (bf16[128,2560]{1,0:T(8,128)(2,1)S(1)}, bf16[128,2560]{1,0:T(8,128)(2,1)S(1)}, u32[]{:S(2)}, u32[]{:S(2)}) collective-permute-start(bf16[128,2560]{1,0:T(8,128)(2,1)S(1)} %get-tuple-element.46), channel_id=1, source_target_pairs={{0,1},{1,0},{2,3},{3,2},{4,5},{5,4},{6,7},{7,6},{8,9},{9,8},{10,11... | collective-permute-start | bytes 1966088 | tf_op jit(solution)/shard_map/ppermute | solution.py:17
  52.0 11.5 %collective-permute-start.14 = (bf16[64,2560]{1,0:T(8,128)(2,1)S(1)}, bf16[64,2560]{1,0:T(8,128)(2,1)S(1)}, u32[]{:S(2)}, u32[]{:S(2)}) collective-permute-start(bf16[64,2560]{1,0:T(8,128)(2,1)S(1)} %get-tuple-element.52), channel_id=1, source_target_pairs={{0,2},{1,3},{2,0},{3,1},{4,6},{5,7},{6,4},{7,5},{8,10},{9,11},{10,... | collective-permute-start | bytes 983048 | tf_op jit(solution)/shard_map/ppermute | solution.py:17
  56.8 4.5 %collective-permute-start.25 = (bf16[128,2560]{1,0:T(8,128)(2,1)S(1)}, bf16[128,2560]{1,0:T(8,128)(2,1)S(1)}, u32[]{:S(2)}, u32[]{:S(2)}) collective-permute-start(bf16[128,2560]{1,0:T(8,128)(2,1)S(1)} %get-tuple-element.49), channel_id=1, source_target_pairs={{0,1},{1,0},{2,3},{3,2},{4,5},{5,4},{6,7},{7,6},{8,9},{9,8},{10,11... | collective-permute-start | bytes 1966088 | tf_op jit(solution)/shard_map/ppermute | solution.py:17
  57.2 12.4 %collective-permute-start.22 = (bf16[64,2560]{1,0:T(8,128)(2,1)S(1)}, bf16[64,2560]{1,0:T(8,128)(2,1)S(1)}, u32[]{:S(2)}, u32[]{:S(2)}) collective-permute-start(bf16[64,2560]{1,0:T(8,128)(2,1)S(1)} %get-tuple-element.54), channel_id=1, source_target_pairs={{0,2},{1,3},{2,0},{3,1},{4,6},{5,7},{6,4},{7,5},{8,10},{9,11},{10,... | collective-permute-start | bytes 983048 | tf_op jit(solution)/shard_map/ppermute | solution.py:17
  61.1 2.2 %collective-permute-start.13 = (bf16[128,2560]{1,0:T(8,128)(2,1)S(1)}, bf16[128,2560]{1,0:T(8,128)(2,1)S(1)}, u32[]{:S(2)}, u32[]{:S(2)}) collective-permute-start(bf16[128,2560]{1,0:T(8,128)(2,1)S(1)} %get-tuple-element.39), channel_id=1, source_target_pairs={{0,1},{1,0},{2,3},{3,2},{4,5},{5,4},{6,7},{7,6},{8,9},{9,8},{10,11... | collective-permute-start | bytes 1966088 | tf_op jit(solution)/shard_map/ppermute | solution.py:17
  61.4 16.9 %collective-permute-start.26 = (bf16[64,2560]{1,0:T(8,128)(2,1)S(1)}, bf16[64,2560]{1,0:T(8,128)(2,1)S(1)}, u32[]{:S(2)}, u32[]{:S(2)}) collective-permute-start(bf16[64,2560]{1,0:T(8,128)(2,1)S(1)} %get-tuple-element.56), channel_id=1, source_target_pairs={{0,2},{1,3},{2,0},{3,1},{4,6},{5,7},{6,4},{7,5},{8,10},{9,11},{10,... | collective-permute-start | bytes 983048 | tf_op jit(solution)/shard_map/ppermute | solution.py:17
  63.5 9.0 %collective-permute-start.15 = (bf16[32,2560]{1,0:T(8,128)(2,1)S(1)}, bf16[32,2560]{1,0:T(8,128)(2,1)S(1)}, u32[]{:S(2)}, u32[]{:S(2)}) collective-permute-start(bf16[32,2560]{1,0:T(8,128)(2,1)S(1)} %get-tuple-element.60), channel_id=1, source_target_pairs={{0,4},{1,5},{2,6},{3,7},{4,0},{5,1},{6,2},{7,3},{8,12},{9,13},{10,... | collective-permute-start | bytes 491528 | tf_op jit(solution)/shard_map/ppermute | solution.py:17
  69.7 6.4 %collective-permute-start.23 = (bf16[32,2560]{1,0:T(8,128)(2,1)S(1)}, bf16[32,2560]{1,0:T(8,128)(2,1)S(1)}, u32[]{:S(2)}, u32[]{:S(2)}) collective-permute-start(bf16[32,2560]{1,0:T(8,128)(2,1)S(1)} %get-tuple-element.62), channel_id=1, source_target_pairs={{0,4},{1,5},{2,6},{3,7},{4,0},{5,1},{6,2},{7,3},{8,12},{9,13},{10,... | collective-permute-start | bytes 491528 | tf_op jit(solution)/shard_map/ppermute | solution.py:17
  71.8 11.4 %collective-permute-start.29 = (bf16[64,2560]{1,0:T(8,128)(2,1)S(1)}, bf16[64,2560]{1,0:T(8,128)(2,1)S(1)}, u32[]{:S(2)}, u32[]{:S(2)}) collective-permute-start(bf16[64,2560]{1,0:T(8,128)(2,1)S(1)} %get-tuple-element.58), channel_id=1, source_target_pairs={{0,2},{1,3},{2,0},{3,1},{4,6},{5,7},{6,4},{7,5},{8,10},{9,11},{10,... | collective-permute-start | bytes 983048 | tf_op jit(solution)/shard_map/ppermute | solution.py:17
  72.6 7.9 %collective-permute-start.16 = (bf16[16,2560]{1,0:T(8,128)(2,1)S(1)}, bf16[16,2560]{1,0:T(8,128)(2,1)S(1)}, u32[]{:S(2)}, u32[]{:S(2)}) collective-permute-start(bf16[16,2560]{1,0:T(8,128)(2,1)S(1)} %add_convert_fusion.26), channel_id=1, source_target_pairs={{0,8},{1,9},{2,10},{3,11},{4,12},{5,13},{6,14},{7,15},{8,0},{9,1},... | collective-permute-start | bytes 245768 | tf_op jit(solution)/shard_map/ppermute | solution.py:17
  76.1 5.5 %collective-permute-start.24 = (bf16[16,2560]{1,0:T(8,128)(2,1)S(1)}, bf16[16,2560]{1,0:T(8,128)(2,1)S(1)}, u32[]{:S(2)}, u32[]{:S(2)}) collective-permute-start(bf16[16,2560]{1,0:T(8,128)(2,1)S(1)} %add_convert_fusion.23), channel_id=1, source_target_pairs={{0,8},{1,9},{2,10},{3,11},{4,12},{5,13},{6,14},{7,15},{8,0},{9,1},... | collective-permute-start | bytes 245768 | tf_op jit(solution)/shard_map/ppermute | solution.py:17
  78.4 6.9 %collective-permute-start.27 = (bf16[32,2560]{1,0:T(8,128)(2,1)S(1)}, bf16[32,2560]{1,0:T(8,128)(2,1)S(1)}, u32[]{:S(2)}, u32[]{:S(2)}) collective-permute-start(bf16[32,2560]{1,0:T(8,128)(2,1)S(1)} %get-tuple-element.64), channel_id=1, source_target_pairs={{0,4},{1,5},{2,6},{3,7},{4,0},{5,1},{6,2},{7,3},{8,12},{9,13},{10,... | collective-permute-start | bytes 491528 | tf_op jit(solution)/shard_map/ppermute | solution.py:17
  83.3 7.3 %collective-permute-start.30 = (bf16[32,2560]{1,0:T(8,128)(2,1)S(1)}, bf16[32,2560]{1,0:T(8,128)(2,1)S(1)}, u32[]{:S(2)}, u32[]{:S(2)}) collective-permute-start(bf16[32,2560]{1,0:T(8,128)(2,1)S(1)} %get-tuple-element.66), channel_id=1, source_target_pairs={{0,4},{1,5},{2,6},{3,7},{4,0},{5,1},{6,2},{7,3},{8,12},{9,13},{10,... | collective-permute-start | bytes 491528 | tf_op jit(solution)/shard_map/ppermute | solution.py:17
  85.4 7.0 %collective-permute-start.28 = (bf16[16,2560]{1,0:T(8,128)(2,1)S(1)}, bf16[16,2560]{1,0:T(8,128)(2,1)S(1)}, u32[]{:S(2)}, u32[]{:S(2)}) collective-permute-start(bf16[16,2560]{1,0:T(8,128)(2,1)S(1)} %add_convert_fusion.20), channel_id=1, source_target_pairs={{0,8},{1,9},{2,10},{3,11},{4,12},{5,13},{6,14},{7,15},{8,0},{9,1},... | collective-permute-start | bytes 245768 | tf_op jit(solution)/shard_map/ppermute | solution.py:17
  90.6 5.4 %collective-permute-start.31 = (bf16[16,2560]{1,0:T(8,128)(2,1)S(1)}, bf16[16,2560]{1,0:T(8,128)(2,1)S(1)}, u32[]{:S(2)}, u32[]{:S(2)}) collective-permute-start(bf16[16,2560]{1,0:T(8,128)(2,1)S(1)} %add_convert_fusion.17), channel_id=1, source_target_pairs={{0,8},{1,9},{2,10},{3,11},{4,12},{5,13},{6,14},{7,15},{8,0},{9,1},... | collective-permute-start | bytes 245768 | tf_op jit(solution)/shard_map/ppermute | solution.py:17
  (8 other events, 33.9 us)

commit v5 on v4

--- a/solution.py
+++ b/solution.py
@@ -87,7 +87,7 @@
     )(rows, ids, weights)
 
 
-def expert_kernel(experts, places, own_ref, near_ref, far_ref, gate_ref, up_ref, down_ref, keep_ref, send_ref):
+def expert_kernel(experts, places, own_ref, near_ref, far_ref, gate_ref, up_ref, down_ref, keep_ref, send_ref, rows_ref, hidden_ref):
     width = gate_ref.shape[0]
     half = near_ref.shape[0]
     share = half // len(places)
@@ -95,21 +95,25 @@
     block = min(BLOCK // 2, half)
     for start in range(0, half, block):
         part = slice(start, start + block)
-        rows = jnp.concatenate([near_ref[part, :], far_ref[part, :]], axis=0)
-        tokens = rows[:, :width]
-        spread = rows[:, width:].astype(jnp.float32)
+        rows_ref[:block, :] = near_ref[part, :]
+        rows_ref[block:, :] = far_ref[part, :]
+        spread = rows_ref[:, width:].astype(jnp.float32)
         lane = lax.broadcasted_iota(jnp.int32, spread.shape, 1)
         mine = (lane == own) | (lane == own + experts)
         weight = jnp.sum(jnp.where(mine, spread, 0.0), axis=1, keepdims=True)
-        gate = jnp.dot(tokens, gate_ref[...], preferred_element_type=jnp.float32)
-        up = jnp.dot(tokens, up_ref[...], preferred_element_type=jnp.float32)
-        hidden = (gate / (1.0 + jnp.exp(-gate)) * up).astype(jnp.bfloat16)
-        result = jnp.dot(hidden, down_ref[...], preferred_element_type=jnp.float32)
-        scaled = (result * weight).astype(jnp.bfloat16)
-        for row in range(0, block, share):
-            place = places[(start + row) // share] * share
-            keep_ref[place : place + share, :] = scaled[row : row + share]
-            send_ref[place : place + share, :] = scaled[block + row : block + row + share]
+        for begin in range(0, hidden_ref.shape[1], BLOCK):
+            cut = slice(begin, begin + BLOCK)
+            gate = jnp.dot(rows_ref[:, :width], gate_ref[:, cut], preferred_element_type=jnp.float32)
+            up = jnp.dot(rows_ref[:, :width], up_ref[:, cut], preferred_element_type=jnp.float32)
+            hidden_ref[:, cut] = (gate / (1.0 + jnp.exp(-gate)) * up).astype(jnp.bfloat16)
+        for begin in range(0, width, width):
+            cut = slice(begin, begin + width)
+            result = jnp.dot(hidden_ref[...], down_ref[:, cut], preferred_element_type=jnp.float32)
+            scaled = (result * weight).astype(jnp.bfloat16)
+            for row in range(0, block, share):
+                place = places[(start + row) // share] * share
+                keep_ref[place : place + share, cut] = scaled[row : row + share]
+                send_ref[place : place + share, cut] = scaled[block + row : block + row + share]
 
 
 def places_of(gather, scatter):
@@ -128,6 +132,10 @@
         out_shape=(shape, shape),
         in_specs=[pl.BlockSpec(memory_space=pltpu.SMEM)] + [VMEM] * 5,
         out_specs=(VMEM, VMEM),
+        scratch_shapes=[
+            pltpu.VMEM((2 * min(BLOCK // 2, half), near.shape[1]), jnp.bfloat16),
+            pltpu.VMEM((2 * min(BLOCK // 2, half), gate_proj.shape[1]), jnp.bfloat16),
+        ],
         compiler_params=pltpu.CompilerParams(vmem_limit_bytes=32 * MIB),
         cost_estimate=WORK_COST,
     )(lax.axis_index("expert").reshape(1), near, far, gate_proj, up_proj, down_proj)
@@ -204,7 +212,7 @@
 
     firsts = [keep for keep, _ in sums]
     for piece in range(PIECES):
-        shrink(piece, 0, *firsts[piece + 1 : piece + 2])
+        shrink(piece, 0, *firsts[piece + 1 : piece + 2] if piece else ())
     closed = sums[-1][0]
 
     for stage in range(1, final + 1):

time: 97.1 us -> 97.1 us (level)
  no operation moved by 1% of the time
where the time goes in v5:
time: 97.1 us; the launch traced here: 96.8 us
  starting transfers between devices  39.4 us (41%)
  waiting for transfers between devices  34.6 us (36%)
  Pallas kernels  13.6 us (14%)
  local copies, waits for them, and re-layouts  6.81 us (7%)
  other arithmetic  2.12 us (2%)
    ppermute x32, starting transfers between devices, swap(): lax.ppermute(array, 'expert', [(i, i ^ bit) for i in range(axis_size)])  39.4 us
    ppermute x32, waiting for transfers between devices, swap(): lax.ppermute(array, 'expert', [(i, i ^ bit) for i in range(axis_size)])  34.6 us
    pallas_call x4, Pallas kernels, expert_rows(): pl.pallas_call(lambda *refs: expert_kernel(experts, places, *refs), out_s...  13.2 us
    unnamed x22, local copies, waits for them, and re-layouts  6.75 us
  transfers between devices with their start and end apart: 32, of which 16 were waited for; matrix products, arithmetic and copies ran while one was open for 2% of the time, Pallas kernels for 14%

profile of v5, /device:TPU:0, one launch (start us, length us, event | category | flops | bytes accessed | tf_op | source)
XLA Modules:
  0.0 96.8 jit_solution(12148471369985293534)
XLA Ops:
  2.8 4.1 %collective-permute-start = (bf16[16,2688]{1,0:T(8,128)(2,1)S(1)}, bf16[16,2688]{1,0:T(8,128)(2,1)S(1)}, u32[]{:S(2)}, u32[]{:S(2)}) collective-permute-start(bf16[16,2688]{1,0:T(8,128)(2,1)S(1)} %get-tuple-element.27), channel_id=1, source_target_pairs={{0,8},{1,9},{2,10},{3,11},{4,12},{5,13},{6,14},{7,15},{8,0},{9,1},... | collective-permute-start | bytes 258056 | tf_op jit(solution)/shard_map/ppermute | solution.py:17
  6.9 1.5 %collective-permute-start.5 = (bf16[16,2688]{1,0:T(8,128)(2,1)S(1)}, bf16[16,2688]{1,0:T(8,128)(2,1)S(1)}, u32[]{:S(2)}, u32[]{:S(2)}) collective-permute-start(bf16[16,2688]{1,0:T(8,128)(2,1)S(1)} %get-tuple-element.30), channel_id=1, source_target_pairs={{0,2},{1,3},{2,0},{3,1},{4,6},{5,7},{6,4},{7,5},{8,10},{9,11},{10,... | collective-permute-start | bytes 258056 | tf_op jit(solution)/shard_map/ppermute | solution.py:17
  8.5 2.8 %collective-permute-done = bf16[16,2688]{1,0:T(8,128)(2,1)S(1)} collective-permute-done((bf16[16,2688]{1,0:T(8,128)(2,1)S(1)}, bf16[16,2688]{1,0:T(8,128)(2,1)S(1)}, u32[]{:S(2)}, u32[]{:S(2)}) %collective-permute-start) | collective-permute-done | bytes 86048 | tf_op jit(solution)/shard_map/ppermute | solution.py:17
  12.1 3.4 %collective-permute-start.6 = (bf16[16,2688]{1,0:T(8,128)(2,1)S(1)}, bf16[16,2688]{1,0:T(8,128)(2,1)S(1)}, u32[]{:S(2)}, u32[]{:S(2)}) collective-permute-start(bf16[16,2688]{1,0:T(8,128)(2,1)S(1)} %get-tuple-element.32), channel_id=1, source_target_pairs={{0,8},{1,9},{2,10},{3,11},{4,12},{5,13},{6,14},{7,15},{8,0},{9,1},... | collective-permute-start | bytes 258056 | tf_op jit(solution)/shard_map/ppermute | solution.py:17
  15.5 2.5 %collective-permute-done.6 = bf16[16,2688]{1,0:T(8,128)(2,1)S(1)} collective-permute-done((bf16[16,2688]{1,0:T(8,128)(2,1)S(1)}, bf16[16,2688]{1,0:T(8,128)(2,1)S(1)}, u32[]{:S(2)}, u32[]{:S(2)}) %collective-permute-start.6) | collective-permute-done | bytes 86048 | tf_op jit(solution)/shard_map/ppermute | solution.py:17
  18.0 3.8 %collective-permute-start.7 = (bf16[32,2688]{1,0:T(8,128)(2,1)S(1)}, bf16[32,2688]{1,0:T(8,128)(2,1)S(1)}, u32[]{:S(2)}, u32[]{:S(2)}) collective-permute-start(bf16[32,2688]{1,0:T(8,128)(2,1)S(1)} %pad_maximum_fusion.6), channel_id=1, source_target_pairs={{0,4},{1,5},{2,6},{3,7},{4,0},{5,1},{6,2},{7,3},{8,12},{9,13},{10,... | collective-permute-start | bytes 516104 | tf_op jit(solution)/shard_map/ppermute | solution.py:17
  22.0 1.6 %collective-permute-start.2 = (bf16[64,2688]{1,0:T(8,128)(2,1)S(1)}, bf16[64,2688]{1,0:T(8,128)(2,1)S(1)}, u32[]{:S(2)}, u32[]{:S(2)}) collective-permute-start(bf16[64,2688]{1,0:T(8,128)(2,1)S(1)} %get-tuple-element.66), channel_id=1, source_target_pairs={{0,2},{1,3},{2,0},{3,1},{4,6},{5,7},{6,4},{7,5},{8,10},{9,11},{10,... | collective-permute-start | bytes 1032200 | tf_op jit(solution)/shard_map/ppermute | solution.py:17
  24.7 1.3 %collective-permute-done.7 = bf16[32,2688]{1,0:T(8,128)(2,1)S(1)} collective-permute-done((bf16[32,2688]{1,0:T(8,128)(2,1)S(1)}, bf16[32,2688]{1,0:T(8,128)(2,1)S(1)}, u32[]{:S(2)}, u32[]{:S(2)}) %collective-permute-start.7) | collective-permute-done | bytes 172064 | tf_op jit(solution)/shard_map/ppermute | solution.py:17
  26.0 2.3 %collective-permute-start.10 = (bf16[64,2688]{1,0:T(8,128)(2,1)S(1)}, bf16[64,2688]{1,0:T(8,128)(2,1)S(1)}, u32[]{:S(2)}, u32[]{:S(2)}) collective-permute-start(bf16[64,2688]{1,0:T(8,128)(2,1)S(1)} %get-tuple-element.68), channel_id=1, source_target_pairs={{0,2},{1,3},{2,0},{3,1},{4,6},{5,7},{6,4},{7,5},{8,10},{9,11},{10,... | collective-permute-start | bytes 1032200 | tf_op jit(solution)/shard_map/ppermute | solution.py:17
  29.5 1.5 %collective-permute-start.18 = (bf16[32,2688]{1,0:T(8,128)(2,1)S(1)}, bf16[32,2688]{1,0:T(8,128)(2,1)S(1)}, u32[]{:S(2)}, u32[]{:S(2)}) collective-permute-start(bf16[32,2688]{1,0:T(8,128)(2,1)S(1)} %pad_maximum_fusion.7), channel_id=1, source_target_pairs={{0,4},{1,5},{2,6},{3,7},{4,0},{5,1},{6,2},{7,3},{8,12},{9,13},{10,... | collective-permute-start | bytes 516104 | tf_op jit(solution)/shard_map/ppermute | solution.py:17
  31.0 6.0 %collective-permute-done.8 = bf16[32,2688]{1,0:T(8,128)(2,1)S(1)} collective-permute-done((bf16[32,2688]{1,0:T(8,128)(2,1)S(1)}, bf16[32,2688]{1,0:T(8,128)(2,1)S(1)}, u32[]{:S(2)}, u32[]{:S(2)}) %collective-permute-start.8) | collective-permute-done | bytes 172064 | tf_op jit(solution)/shard_map/ppermute | solution.py:17
  37.2 1.6 %collective-permute-done.18 = bf16[32,2688]{1,0:T(8,128)(2,1)S(1)} collective-permute-done((bf16[32,2688]{1,0:T(8,128)(2,1)S(1)}, bf16[32,2688]{1,0:T(8,128)(2,1)S(1)}, u32[]{:S(2)}, u32[]{:S(2)}) %collective-permute-start.18) | collective-permute-done | bytes 172064 | tf_op jit(solution)/shard_map/ppermute | solution.py:17
  39.3 2.1 %copy-done.1 = bf16[1,2560,768]{2,1,0:T(8,128)(2,1)S(1)} copy-done((bf16[1,2560,768]{2,1,0:T(8,128)(2,1)S(1)}, bf16[1,2560,768]{2,1,0:T(8,128)(2,1)}, u32[]{:S(2)}) %copy-start.1) | copy-done | bytes 3932184
  41.4 2.1 %copy-done.3 = bf16[1,768,2560]{2,1,0:T(8,128)(2,1)S(1)} copy-done((bf16[1,768,2560]{2,1,0:T(8,128)(2,1)S(1)}, bf16[1,768,2560]{2,1,0:T(8,128)(2,1)}, u32[]{:S(2)}) %copy-start.3) | copy-done | bytes 3932184
  43.5 3.3 %shard_map.65 = (bf16[128,2560]{1,0:T(8,128)(2,1)S(1)}, bf16[128,2560]{1,0:T(8,128)(2,1)S(1)}) custom-call(s32[1]{0:T(128)} %bitcast.refs_0_, bf16[128,2688]{1,0:T(8,128)(2,1)S(1)} %constant_dynamic-update-slice_fusion.5.refs_1_, bf16[128,2688]{1,0:T(8,128)(2,1)S(1)} %collective-permute-done.3.refs_2_, bf16[2560,768]{1,0:T(8,128)(2,1)S(1)} %bitcast.8, ...), custom_call_target="tpu_custom_call" | custom-call | flops 1000 | bytes 1000 | tf_op jit(solution)/shard_map/pallas_call | solution.py:130
  47.9 3.3 %shard_map.66 = (bf16[128,2560]{1,0:T(8,128)(2,1)S(1)}, bf16[128,2560]{1,0:T(8,128)(2,1)S(1)}) custom-call(s32[1]{0:T(128)} %bitcast.refs_0_, bf16[128,2688]{1,0:T(8,128)(2,1)S(1)} %constant_dynamic-update-slice_fusion.12.refs_1_, bf16[128,2688]{1,0:T(8,128)(2,1)S(1)} %collective-permute-done.11.refs_2_, bf16[2560,768]{1,0:T(8,128)(2,1)S(1)} %bitcast.9, ...), custom_call_target="tpu_custom_call" | custom-call | flops 1000 | bytes 1000 | tf_op jit(solution)/shard_map/pallas_call | solution.py:130
  52.0 1.5 %collective-permute-start.14 = (bf16[64,2560]{1,0:T(8,128)(2,1)S(1)}, bf16[64,2560]{1,0:T(8,128)(2,1)S(1)}, u32[]{:S(2)}, u32[]{:S(2)}) collective-permute-start(bf16[64,2560]{1,0:T(8,128)(2,1)S(1)} %get-tuple-element.50), channel_id=1, source_target_pairs={{0,2},{1,3},{2,0},{3,1},{4,6},{5,7},{6,4},{7,5},{8,10},{9,11},{10,... | collective-permute-start | bytes 983048 | tf_op jit(solution)/shard_map/ppermute | solution.py:17
  53.5 3.3 %shard_map.68 = (bf16[128,2560]{1,0:T(8,128)(2,1)S(1)}, bf16[128,2560]{1,0:T(8,128)(2,1)S(1)}) custom-call(s32[1]{0:T(128)} %bitcast.refs_0_, bf16[128,2688]{1,0:T(8,128)(2,1)S(1)} %pad_maximum_fusion.1.refs_1_, bf16[128,2688]{1,0:T(8,128)(2,1)S(1)} %collective-permute-done.20.refs_2_, bf16[2560,768]{1,0:T(8,128)(2,1)S(1)} %bitcast.10, ...), custom_call_target="tpu_custom_call" | custom-call | flops 1000 | bytes 1000 | tf_op jit(solution)/shard_map/pallas_call | solution.py:130
  57.9 3.3 %shard_map.67 = (bf16[128,2560]{1,0:T(8,128)(2,1)S(1)}, bf16[128,2560]{1,0:T(8,128)(2,1)S(1)}) custom-call(s32[1]{0:T(128)} %bitcast.refs_0_, bf16[128,2688]{1,0:T(8,128)(2,1)S(1)} %pad_maximum_fusion.refs_1_, bf16[128,2688]{1,0:T(8,128)(2,1)S(1)} %collective-permute-done.12.refs_2_, bf16[2560,768]{1,0:T(8,128)(2,1)S(1)} %bitcast.11, ...), custom_call_target="tpu_custom_call" | custom-call | flops 1000 | bytes 1000 | tf_op jit(solution)/shard_map/pallas_call | solution.py:130
  61.4 1.5 %collective-permute-start.26 = (bf16[64,2560]{1,0:T(8,128)(2,1)S(1)}, bf16[64,2560]{1,0:T(8,128)(2,1)S(1)}, u32[]{:S(2)}, u32[]{:S(2)}) collective-permute-start(bf16[64,2560]{1,0:T(8,128)(2,1)S(1)} %get-tuple-element.54), channel_id=1, source_target_pairs={{0,2},{1,3},{2,0},{3,1},{4,6},{5,7},{6,4},{7,5},{8,10},{9,11},{10,... | collective-permute-start | bytes 983048 | tf_op jit(solution)/shard_map/ppermute | solution.py:17
  63.6 2.1 %collective-permute-start.15 = (bf16[32,2560]{1,0:T(8,128)(2,1)S(1)}, bf16[32,2560]{1,0:T(8,128)(2,1)S(1)}, u32[]{:S(2)}, u32[]{:S(2)}) collective-permute-start(bf16[32,2560]{1,0:T(8,128)(2,1)S(1)} %get-tuple-element.58), channel_id=1, source_target_pairs={{0,4},{1,5},{2,6},{3,7},{4,0},{5,1},{6,2},{7,3},{8,12},{9,13},{10,... | collective-permute-start | bytes 491528 | tf_op jit(solution)/shard_map/ppermute | solution.py:17
  65.6 4.0 %collective-permute-done.22 = bf16[64,2560]{1,0:T(8,128)(2,1)S(1)} collective-permute-done((bf16[64,2560]{1,0:T(8,128)(2,1)S(1)}, bf16[64,2560]{1,0:T(8,128)(2,1)S(1)}, u32[]{:S(2)}, u32[]{:S(2)}) %collective-permute-start.22) | collective-permute-done | bytes 327712 | tf_op jit(solution)/shard_map/ppermute | solution.py:17
  69.7 2.1 %collective-permute-start.23 = (bf16[32,2560]{1,0:T(8,128)(2,1)S(1)}, bf16[32,2560]{1,0:T(8,128)(2,1)S(1)}, u32[]{:S(2)}, u32[]{:S(2)}) collective-permute-start(bf16[32,2560]{1,0:T(8,128)(2,1)S(1)} %get-tuple-element.60), channel_id=1, source_target_pairs={{0,4},{1,5},{2,6},{3,7},{4,0},{5,1},{6,2},{7,3},{8,12},{9,13},{10,... | collective-permute-start | bytes 491528 | tf_op jit(solution)/shard_map/ppermute | solution.py:17
  72.6 1.2 %collective-permute-start.16 = (bf16[16,2560]{1,0:T(8,128)(2,1)S(1)}, bf16[16,2560]{1,0:T(8,128)(2,1)S(1)}, u32[]{:S(2)}, u32[]{:S(2)}) collective-permute-start(bf16[16,2560]{1,0:T(8,128)(2,1)S(1)} %add_convert_fusion.26), channel_id=1, source_target_pairs={{0,8},{1,9},{2,10},{3,11},{4,12},{5,13},{6,14},{7,15},{8,0},{9,1},... | collective-permute-start | bytes 245768 | tf_op jit(solution)/shard_map/ppermute | solution.py:17
  73.8 2.2 %collective-permute-done.23 = bf16[32,2560]{1,0:T(8,128)(2,1)S(1)} collective-permute-done((bf16[32,2560]{1,0:T(8,128)(2,1)S(1)}, bf16[32,2560]{1,0:T(8,128)(2,1)S(1)}, u32[]{:S(2)}, u32[]{:S(2)}) %collective-permute-start.23) | collective-permute-done | bytes 163872 | tf_op jit(solution)/shard_map/ppermute | solution.py:17
  76.1 2.3 %collective-permute-start.24 = (bf16[16,2560]{1,0:T(8,128)(2,1)S(1)}, bf16[16,2560]{1,0:T(8,128)(2,1)S(1)}, u32[]{:S(2)}, u32[]{:S(2)}) collective-permute-start(bf16[16,2560]{1,0:T(8,128)(2,1)S(1)} %add_convert_fusion.23), channel_id=1, source_target_pairs={{0,8},{1,9},{2,10},{3,11},{4,12},{5,13},{6,14},{7,15},{8,0},{9,1},... | collective-permute-start | bytes 245768 | tf_op jit(solution)/shard_map/ppermute | solution.py:17
  78.8 1.7 %collective-permute-done.16 = bf16[16,2560]{1,0:T(8,128)(2,1)S(1)} collective-permute-done((bf16[16,2560]{1,0:T(8,128)(2,1)S(1)}, bf16[16,2560]{1,0:T(8,128)(2,1)S(1)}, u32[]{:S(2)}, u32[]{:S(2)}) %collective-permute-start.16) | collective-permute-done | bytes 81952 | tf_op jit(solution)/shard_map/ppermute | solution.py:17
  81.6 1.6 %collective-permute-done.29 = bf16[64,2560]{1,0:T(8,128)(2,1)S(1)} collective-permute-done((bf16[64,2560]{1,0:T(8,128)(2,1)S(1)}, bf16[64,2560]{1,0:T(8,128)(2,1)S(1)}, u32[]{:S(2)}, u32[]{:S(2)}) %collective-permute-start.29) | collective-permute-done | bytes 327712 | tf_op jit(solution)/shard_map/ppermute | solution.py:17
  83.3 2.1 %collective-permute-start.30 = (bf16[32,2560]{1,0:T(8,128)(2,1)S(1)}, bf16[32,2560]{1,0:T(8,128)(2,1)S(1)}, u32[]{:S(2)}, u32[]{:S(2)}) collective-permute-start(bf16[32,2560]{1,0:T(8,128)(2,1)S(1)} %get-tuple-element.64), channel_id=1, source_target_pairs={{0,4},{1,5},{2,6},{3,7},{4,0},{5,1},{6,2},{7,3},{8,12},{9,13},{10,... | collective-permute-start | bytes 491528 | tf_op jit(solution)/shard_map/ppermute | solution.py:17
  85.7 4.8 %collective-permute-done.30 = bf16[32,2560]{1,0:T(8,128)(2,1)S(1)} collective-permute-done((bf16[32,2560]{1,0:T(8,128)(2,1)S(1)}, bf16[32,2560]{1,0:T(8,128)(2,1)S(1)}, u32[]{:S(2)}, u32[]{:S(2)}) %collective-permute-start.30) | collective-permute-done | bytes 163872 | tf_op jit(solution)/shard_map/ppermute | solution.py:17
  90.6 1.8 %collective-permute-start.31 = (bf16[16,2560]{1,0:T(8,128)(2,1)S(1)}, bf16[16,2560]{1,0:T(8,128)(2,1)S(1)}, u32[]{:S(2)}, u32[]{:S(2)}) collective-permute-start(bf16[16,2560]{1,0:T(8,128)(2,1)S(1)} %add_convert_fusion.17), channel_id=1, source_target_pairs={{0,8},{1,9},{2,10},{3,11},{4,12},{5,13},{6,14},{7,15},{8,0},{9,1},... | collective-permute-start | bytes 245768 | tf_op jit(solution)/shard_map/ppermute | solution.py:17
  92.4 3.6 %collective-permute-done.31 = bf16[16,2560]{1,0:T(8,128)(2,1)S(1)} collective-permute-done((bf16[16,2560]{1,0:T(8,128)(2,1)S(1)}, bf16[16,2560]{1,0:T(8,128)(2,1)S(1)}, u32[]{:S(2)}, u32[]{:S(2)}) %collective-permute-start.31) | collective-permute-done | bytes 81952 | tf_op jit(solution)/shard_map/ppermute | solution.py:17
  (85 shorter events, 14.4 us)
Async XLA Ops:
  2.8 8.5 %collective-permute-start = (bf16[16,2688]{1,0:T(8,128)(2,1)S(1)}, bf16[16,2688]{1,0:T(8,128)(2,1)S(1)}, u32[]{:S(2)}, u32[]{:S(2)}) collective-permute-start(bf16[16,2688]{1,0:T(8,128)(2,1)S(1)} %get-tuple-element.27), channel_id=1, source_target_pairs={{0,8},{1,9},{2,10},{3,11},{4,12},{5,13},{6,14},{7,15},{8,0},{9,1},... | collective-permute-start | bytes 258056 | tf_op jit(solution)/shard_map/ppermute | solution.py:17
  6.9 8.6 %collective-permute-start.5 = (bf16[16,2688]{1,0:T(8,128)(2,1)S(1)}, bf16[16,2688]{1,0:T(8,128)(2,1)S(1)}, u32[]{:S(2)}, u32[]{:S(2)}) collective-permute-start(bf16[16,2688]{1,0:T(8,128)(2,1)S(1)} %get-tuple-element.30), channel_id=1, source_target_pairs={{0,2},{1,3},{2,0},{3,1},{4,6},{5,7},{6,4},{7,5},{8,10},{9,11},{10,... | collective-permute-start | bytes 258056 | tf_op jit(solution)/shard_map/ppermute | solution.py:17
  11.3 10.6 %collective-permute-start.1 = (bf16[32,2688]{1,0:T(8,128)(2,1)S(1)}, bf16[32,2688]{1,0:T(8,128)(2,1)S(1)}, u32[]{:S(2)}, u32[]{:S(2)}) collective-permute-start(bf16[32,2688]{1,0:T(8,128)(2,1)S(1)} %get-tuple-element.71), channel_id=1, source_target_pairs={{0,4},{1,5},{2,6},{3,7},{4,0},{5,1},{6,2},{7,3},{8,12},{9,13},{10,... | collective-permute-start | bytes 516104 | tf_op jit(solution)/shard_map/ppermute | solution.py:17
  12.1 5.9 %collective-permute-start.6 = (bf16[16,2688]{1,0:T(8,128)(2,1)S(1)}, bf16[16,2688]{1,0:T(8,128)(2,1)S(1)}, u32[]{:S(2)}, u32[]{:S(2)}) collective-permute-start(bf16[16,2688]{1,0:T(8,128)(2,1)S(1)} %get-tuple-element.32), channel_id=1, source_target_pairs={{0,8},{1,9},{2,10},{3,11},{4,12},{5,13},{6,14},{7,15},{8,0},{9,1},... | collective-permute-start | bytes 258056 | tf_op jit(solution)/shard_map/ppermute | solution.py:17
  18.0 7.9 %collective-permute-start.7 = (bf16[32,2688]{1,0:T(8,128)(2,1)S(1)}, bf16[32,2688]{1,0:T(8,128)(2,1)S(1)}, u32[]{:S(2)}, u32[]{:S(2)}) collective-permute-start(bf16[32,2688]{1,0:T(8,128)(2,1)S(1)} %pad_maximum_fusion.6), channel_id=1, source_target_pairs={{0,4},{1,5},{2,6},{3,7},{4,0},{5,1},{6,2},{7,3},{8,12},{9,13},{10,... | collective-permute-start | bytes 516104 | tf_op jit(solution)/shard_map/ppermute | solution.py:17
  22.0 15.1 %collective-permute-start.2 = (bf16[64,2688]{1,0:T(8,128)(2,1)S(1)}, bf16[64,2688]{1,0:T(8,128)(2,1)S(1)}, u32[]{:S(2)}, u32[]{:S(2)}) collective-permute-start(bf16[64,2688]{1,0:T(8,128)(2,1)S(1)} %get-tuple-element.66), channel_id=1, source_target_pairs={{0,2},{1,3},{2,0},{3,1},{4,6},{5,7},{6,4},{7,5},{8,10},{9,11},{10,... | collective-permute-start | bytes 1032200 | tf_op jit(solution)/shard_map/ppermute | solution.py:17
  23.5 5.9 %collective-permute-start.17 = (bf16[16,2688]{1,0:T(8,128)(2,1)S(1)}, bf16[16,2688]{1,0:T(8,128)(2,1)S(1)}, u32[]{:S(2)}, u32[]{:S(2)}) collective-permute-start(bf16[16,2688]{1,0:T(8,128)(2,1)S(1)} %get-tuple-element.40), channel_id=1, source_target_pairs={{0,8},{1,9},{2,10},{3,11},{4,12},{5,13},{6,14},{7,15},{8,0},{9,1},... | collective-permute-start | bytes 258056 | tf_op jit(solution)/shard_map/ppermute | solution.py:17
  26.0 12.9 %collective-permute-start.10 = (bf16[64,2688]{1,0:T(8,128)(2,1)S(1)}, bf16[64,2688]{1,0:T(8,128)(2,1)S(1)}, u32[]{:S(2)}, u32[]{:S(2)}) collective-permute-start(bf16[64,2688]{1,0:T(8,128)(2,1)S(1)} %get-tuple-element.68), channel_id=1, source_target_pairs={{0,2},{1,3},{2,0},{3,1},{4,6},{5,7},{6,4},{7,5},{8,10},{9,11},{10,... | collective-permute-start | bytes 1032200 | tf_op jit(solution)/shard_map/ppermute | solution.py:17
  28.3 8.6 %collective-permute-start.8 = (bf16[32,2688]{1,0:T(8,128)(2,1)S(1)}, bf16[32,2688]{1,0:T(8,128)(2,1)S(1)}, u32[]{:S(2)}, u32[]{:S(2)}) collective-permute-start(bf16[32,2688]{1,0:T(8,128)(2,1)S(1)} %pad_maximum_fusion.5), channel_id=1, source_target_pairs={{0,8},{1,9},{2,10},{3,11},{4,12},{5,13},{6,14},{7,15},{8,0},{9,1},... | collective-permute-start | bytes 516104 | tf_op jit(solution)/shard_map/ppermute | solution.py:17
  29.5 9.3 %collective-permute-start.18 = (bf16[32,2688]{1,0:T(8,128)(2,1)S(1)}, bf16[32,2688]{1,0:T(8,128)(2,1)S(1)}, u32[]{:S(2)}, u32[]{:S(2)}) collective-permute-start(bf16[32,2688]{1,0:T(8,128)(2,1)S(1)} %pad_maximum_fusion.7), channel_id=1, source_target_pairs={{0,4},{1,5},{2,6},{3,7},{4,0},{5,1},{6,2},{7,3},{8,12},{9,13},{10,... | collective-permute-start | bytes 516104 | tf_op jit(solution)/shard_map/ppermute | solution.py:17
  37.0 10.2 %collective-permute-start.9 = (bf16[64,2688]{1,0:T(8,128)(2,1)S(1)}, bf16[64,2688]{1,0:T(8,128)(2,1)S(1)}, u32[]{:S(2)}, u32[]{:S(2)}) collective-permute-start(bf16[64,2688]{1,0:T(8,128)(2,1)S(1)} %pad_maximum_fusion.2), channel_id=1, source_target_pairs={{0,4},{1,5},{2,6},{3,7},{4,0},{5,1},{6,2},{7,3},{8,12},{9,13},{10,... | collective-permute-start | bytes 1032200 | tf_op jit(solution)/shard_map/ppermute | solution.py:17
  37.1 2.2 %collective-permute-start.3 = (bf16[128,2688]{1,0:T(8,128)(2,1)S(1)}, bf16[128,2688]{1,0:T(8,128)(2,1)S(1)}, u32[]{:S(2)}, u32[]{:S(2)}) collective-permute-start(bf16[128,2688]{1,0:T(8,128)(2,1)S(1)} %constant_dynamic-update-slice_fusion.5.refs_1_), channel_id=1, source_target_pairs={{0,1},{1,0},{2,3},{3,2},{4,5},{5,4},{6,7},{7,6},{8,9},{9,8},{10,11... | collective-permute-start | bytes 2064392 | tf_op jit(solution)/shard_map/ppermute | solution.py:17
  38.8 8.9 %collective-permute-start.19 = (bf16[64,2688]{1,0:T(8,128)(2,1)S(1)}, bf16[64,2688]{1,0:T(8,128)(2,1)S(1)}, u32[]{:S(2)}, u32[]{:S(2)}) collective-permute-start(bf16[64,2688]{1,0:T(8,128)(2,1)S(1)} %pad_maximum_fusion.3), channel_id=1, source_target_pairs={{0,2},{1,3},{2,0},{3,1},{4,6},{5,7},{6,4},{7,5},{8,10},{9,11},{10,... | collective-permute-start | bytes 1032200 | tf_op jit(solution)/shard_map/ppermute | solution.py:17
  39.0 8.9 %collective-permute-start.11 = (bf16[128,2688]{1,0:T(8,128)(2,1)S(1)}, bf16[128,2688]{1,0:T(8,128)(2,1)S(1)}, u32[]{:S(2)}, u32[]{:S(2)}) collective-permute-start(bf16[128,2688]{1,0:T(8,128)(2,1)S(1)} %constant_dynamic-update-slice_fusion.12.refs_1_), channel_id=1, source_target_pairs={{0,1},{1,0},{2,3},{3,2},{4,5},{5,4},{6,7},{7,6},{8,9},{9,8},{10,11... | collective-permute-start | bytes 2064392 | tf_op jit(solution)/shard_map/ppermute | solution.py:17
  46.8 5.0 %collective-permute-start.4 = (bf16[128,2560]{1,0:T(8,128)(2,1)S(1)}, bf16[128,2560]{1,0:T(8,128)(2,1)S(1)}, u32[]{:S(2)}, u32[]{:S(2)}) collective-permute-start(bf16[128,2560]{1,0:T(8,128)(2,1)S(1)} %get-tuple-element.29), channel_id=1, source_target_pairs={{0,1},{1,0},{2,3},{3,2},{4,5},{5,4},{6,7},{7,6},{8,9},{9,8},{10,11... | collective-permute-start | bytes 1966088 | tf_op jit(solution)/shard_map/ppermute | solution.py:17
  47.8 5.7 %collective-permute-start.20 = (bf16[128,2688]{1,0:T(8,128)(2,1)S(1)}, bf16[128,2688]{1,0:T(8,128)(2,1)S(1)}, u32[]{:S(2)}, u32[]{:S(2)}) collective-permute-start(bf16[128,2688]{1,0:T(8,128)(2,1)S(1)} %pad_maximum_fusion.1.refs_1_), channel_id=1, source_target_pairs={{0,1},{1,0},{2,3},{3,2},{4,5},{5,4},{6,7},{7,6},{8,9},{9,8},{10,11... | collective-permute-start | bytes 2064392 | tf_op jit(solution)/shard_map/ppermute | solution.py:17
  51.2 6.6 %collective-permute-start.12 = (bf16[128,2688]{1,0:T(8,128)(2,1)S(1)}, bf16[128,2688]{1,0:T(8,128)(2,1)S(1)}, u32[]{:S(2)}, u32[]{:S(2)}) collective-permute-start(bf16[128,2688]{1,0:T(8,128)(2,1)S(1)} %pad_maximum_fusion.refs_1_), channel_id=1, source_target_pairs={{0,1},{1,0},{2,3},{3,2},{4,5},{5,4},{6,7},{7,6},{8,9},{9,8},{10,11... | collective-permute-start | bytes 2064392 | tf_op jit(solution)/shard_map/ppermute | solution.py:17
  51.8 5.3 %collective-permute-start.21 = (bf16[128,2560]{1,0:T(8,128)(2,1)S(1)}, bf16[128,2560]{1,0:T(8,128)(2,1)S(1)}, u32[]{:S(2)}, u32[]{:S(2)}) collective-permute-start(bf16[128,2560]{1,0:T(8,128)(2,1)S(1)} %get-tuple-element.44), channel_id=1, source_target_pairs={{0,1},{1,0},{2,3},{3,2},{4,5},{5,4},{6,7},{7,6},{8,9},{9,8},{10,11... | collective-permute-start | bytes 1966088 | tf_op jit(solution)/shard_map/ppermute | solution.py:17
  52.0 11.5 %collective-permute-start.14 = (bf16[64,2560]{1,0:T(8,128)(2,1)S(1)}, bf16[64,2560]{1,0:T(8,128)(2,1)S(1)}, u32[]{:S(2)}, u32[]{:S(2)}) collective-permute-start(bf16[64,2560]{1,0:T(8,128)(2,1)S(1)} %get-tuple-element.50), channel_id=1, source_target_pairs={{0,2},{1,3},{2,0},{3,1},{4,6},{5,7},{6,4},{7,5},{8,10},{9,11},{10,... | collective-permute-start | bytes 983048 | tf_op jit(solution)/shard_map/ppermute | solution.py:17
  56.8 4.5 %collective-permute-start.25 = (bf16[128,2560]{1,0:T(8,128)(2,1)S(1)}, bf16[128,2560]{1,0:T(8,128)(2,1)S(1)}, u32[]{:S(2)}, u32[]{:S(2)}) collective-permute-start(bf16[128,2560]{1,0:T(8,128)(2,1)S(1)} %get-tuple-element.47), channel_id=1, source_target_pairs={{0,1},{1,0},{2,3},{3,2},{4,5},{5,4},{6,7},{7,6},{8,9},{9,8},{10,11... | collective-permute-start | bytes 1966088 | tf_op jit(solution)/shard_map/ppermute | solution.py:17
  57.2 12.4 %collective-permute-start.22 = (bf16[64,2560]{1,0:T(8,128)(2,1)S(1)}, bf16[64,2560]{1,0:T(8,128)(2,1)S(1)}, u32[]{:S(2)}, u32[]{:S(2)}) collective-permute-start(bf16[64,2560]{1,0:T(8,128)(2,1)S(1)} %get-tuple-element.52), channel_id=1, source_target_pairs={{0,2},{1,3},{2,0},{3,1},{4,6},{5,7},{6,4},{7,5},{8,10},{9,11},{10,... | collective-permute-start | bytes 983048 | tf_op jit(solution)/shard_map/ppermute | solution.py:17
  61.2 2.2 %collective-permute-start.13 = (bf16[128,2560]{1,0:T(8,128)(2,1)S(1)}, bf16[128,2560]{1,0:T(8,128)(2,1)S(1)}, u32[]{:S(2)}, u32[]{:S(2)}) collective-permute-start(bf16[128,2560]{1,0:T(8,128)(2,1)S(1)} %get-tuple-element.37), channel_id=1, source_target_pairs={{0,1},{1,0},{2,3},{3,2},{4,5},{5,4},{6,7},{7,6},{8,9},{9,8},{10,11... | collective-permute-start | bytes 1966088 | tf_op jit(solution)/shard_map/ppermute | solution.py:17
  61.4 16.9 %collective-permute-start.26 = (bf16[64,2560]{1,0:T(8,128)(2,1)S(1)}, bf16[64,2560]{1,0:T(8,128)(2,1)S(1)}, u32[]{:S(2)}, u32[]{:S(2)}) collective-permute-start(bf16[64,2560]{1,0:T(8,128)(2,1)S(1)} %get-tuple-element.54), channel_id=1, source_target_pairs={{0,2},{1,3},{2,0},{3,1},{4,6},{5,7},{6,4},{7,5},{8,10},{9,11},{10,... | collective-permute-start | bytes 983048 | tf_op jit(solution)/shard_map/ppermute | solution.py:17
  63.6 9.0 %collective-permute-start.15 = (bf16[32,2560]{1,0:T(8,128)(2,1)S(1)}, bf16[32,2560]{1,0:T(8,128)(2,1)S(1)}, u32[]{:S(2)}, u32[]{:S(2)}) collective-permute-start(bf16[32,2560]{1,0:T(8,128)(2,1)S(1)} %get-tuple-element.58), channel_id=1, source_target_pairs={{0,4},{1,5},{2,6},{3,7},{4,0},{5,1},{6,2},{7,3},{8,12},{9,13},{10,... | collective-permute-start | bytes 491528 | tf_op jit(solution)/shard_map/ppermute | solution.py:17
  69.7 6.4 %collective-permute-start.23 = (bf16[32,2560]{1,0:T(8,128)(2,1)S(1)}, bf16[32,2560]{1,0:T(8,128)(2,1)S(1)}, u32[]{:S(2)}, u32[]{:S(2)}) collective-permute-start(bf16[32,2560]{1,0:T(8,128)(2,1)S(1)} %get-tuple-element.60), channel_id=1, source_target_pairs={{0,4},{1,5},{2,6},{3,7},{4,0},{5,1},{6,2},{7,3},{8,12},{9,13},{10,... | collective-permute-start | bytes 491528 | tf_op jit(solution)/shard_map/ppermute | solution.py:17
  71.7 11.4 %collective-permute-start.29 = (bf16[64,2560]{1,0:T(8,128)(2,1)S(1)}, bf16[64,2560]{1,0:T(8,128)(2,1)S(1)}, u32[]{:S(2)}, u32[]{:S(2)}) collective-permute-start(bf16[64,2560]{1,0:T(8,128)(2,1)S(1)} %get-tuple-element.56), channel_id=1, source_target_pairs={{0,2},{1,3},{2,0},{3,1},{4,6},{5,7},{6,4},{7,5},{8,10},{9,11},{10,... | collective-permute-start | bytes 983048 | tf_op jit(solution)/shard_map/ppermute | solution.py:17
  72.6 7.9 %collective-permute-start.16 = (bf16[16,2560]{1,0:T(8,128)(2,1)S(1)}, bf16[16,2560]{1,0:T(8,128)(2,1)S(1)}, u32[]{:S(2)}, u32[]{:S(2)}) collective-permute-start(bf16[16,2560]{1,0:T(8,128)(2,1)S(1)} %add_convert_fusion.26), channel_id=1, source_target_pairs={{0,8},{1,9},{2,10},{3,11},{4,12},{5,13},{6,14},{7,15},{8,0},{9,1},... | collective-permute-start | bytes 245768 | tf_op jit(solution)/shard_map/ppermute | solution.py:17
  76.1 5.5 %collective-permute-start.24 = (bf16[16,2560]{1,0:T(8,128)(2,1)S(1)}, bf16[16,2560]{1,0:T(8,128)(2,1)S(1)}, u32[]{:S(2)}, u32[]{:S(2)}) collective-permute-start(bf16[16,2560]{1,0:T(8,128)(2,1)S(1)} %add_convert_fusion.23), channel_id=1, source_target_pairs={{0,8},{1,9},{2,10},{3,11},{4,12},{5,13},{6,14},{7,15},{8,0},{9,1},... | collective-permute-start | bytes 245768 | tf_op jit(solution)/shard_map/ppermute | solution.py:17
  78.4 6.9 %collective-permute-start.27 = (bf16[32,2560]{1,0:T(8,128)(2,1)S(1)}, bf16[32,2560]{1,0:T(8,128)(2,1)S(1)}, u32[]{:S(2)}, u32[]{:S(2)}) collective-permute-start(bf16[32,2560]{1,0:T(8,128)(2,1)S(1)} %get-tuple-element.62), channel_id=1, source_target_pairs={{0,4},{1,5},{2,6},{3,7},{4,0},{5,1},{6,2},{7,3},{8,12},{9,13},{10,... | collective-permute-start | bytes 491528 | tf_op jit(solution)/shard_map/ppermute | solution.py:17
  83.3 7.3 %collective-permute-start.30 = (bf16[32,2560]{1,0:T(8,128)(2,1)S(1)}, bf16[32,2560]{1,0:T(8,128)(2,1)S(1)}, u32[]{:S(2)}, u32[]{:S(2)}) collective-permute-start(bf16[32,2560]{1,0:T(8,128)(2,1)S(1)} %get-tuple-element.64), channel_id=1, source_target_pairs={{0,4},{1,5},{2,6},{3,7},{4,0},{5,1},{6,2},{7,3},{8,12},{9,13},{10,... | collective-permute-start | bytes 491528 | tf_op jit(solution)/shard_map/ppermute | solution.py:17
  85.4 7.0 %collective-permute-start.28 = (bf16[16,2560]{1,0:T(8,128)(2,1)S(1)}, bf16[16,2560]{1,0:T(8,128)(2,1)S(1)}, u32[]{:S(2)}, u32[]{:S(2)}) collective-permute-start(bf16[16,2560]{1,0:T(8,128)(2,1)S(1)} %add_convert_fusion.20), channel_id=1, source_target_pairs={{0,8},{1,9},{2,10},{3,11},{4,12},{5,13},{6,14},{7,15},{8,0},{9,1},... | collective-permute-start | bytes 245768 | tf_op jit(solution)/shard_map/ppermute | solution.py:17
  90.6 5.4 %collective-permute-start.31 = (bf16[16,2560]{1,0:T(8,128)(2,1)S(1)}, bf16[16,2560]{1,0:T(8,128)(2,1)S(1)}, u32[]{:S(2)}, u32[]{:S(2)}) collective-permute-start(bf16[16,2560]{1,0:T(8,128)(2,1)S(1)} %add_convert_fusion.17), channel_id=1, source_target_pairs={{0,8},{1,9},{2,10},{3,11},{4,12},{5,13},{6,14},{7,15},{8,0},{9,1},... | collective-permute-start | bytes 245768 | tf_op jit(solution)/shard_map/ppermute | solution.py:17
  (8 other events, 34.0 us)
